TPU v7x, 32 devices: a whole 2x2x4 slice. The times are simulated.
32 devices in a mesh: row: 8 (over y, x, core), col: 4 (over z).
Axes of the slice: x: 2, y: 2, z: 4, core: 2. Of those that a mesh axis runs over, the one named last changes fastest.
Arguments:
- amplitudes: bfloat16 [8192, 8192], P('row', 'col'), may hold values from -6 to 6
- integrals: bfloat16 [8192, 1024], P('col', 'row'), may hold values from -0.0625 to 0.0625
- tile_mask: int32 [64, 64], P('row', 'col'), may hold values 0 or 1
Outputs:
- residual: bfloat16 [8192, 1024], P('row', 'col')
All inputs are finite; a program needn't handle non-finite values. No bound on the sum of `tile_mask` on one device may be relied on, other than what follows from the above.
Results may differ from a plain program's by a relative error of at most 0.001.
Values may be sent and summed in bfloat16 or wider, within the bound.
No kernel may reach another device: no remote copies, remote signals or barrier semaphores. Data moves between devices by JAX's collectives and lax.ppermute only.
A program may use at most 64 MiB of HBM per device.

v0:
```python
import functools

import jax
import jax.numpy as jnp
from jax import lax
from jax.experimental import pallas as pl
from jax.experimental.pallas import tpu as pltpu
from jax.sharding import PartitionSpec as P

TILE = 128
CODE_ROWS = 16
LEVELS = 32767.0
STEPS_PER_OCTAVE = 64.0
BLOCK_ROWS = 512
ADD_ROWS = 512


def apply_mask(amplitudes, tile_mask):
    tiles_m, tiles_k = tile_mask.shape
    tile_rows = amplitudes.shape[0] // tiles_m
    tile_cols = amplitudes.shape[1] // tiles_k
    blocks = amplitudes.reshape(tiles_m, tile_rows, tiles_k, tile_cols)
    weights = tile_mask.astype(amplitudes.dtype)[:, None, :, None]
    return (blocks * weights).reshape(amplitudes.shape)


def general(amplitudes, integrals, tile_mask):
    masked = apply_mask(amplitudes, tile_mask)
    partial_sums = jnp.dot(
        masked,
        lax.all_gather(integrals, "row", axis=1, tiled=True),
        preferred_element_type=jnp.float32,
    )
    summed = lax.psum_scatter(partial_sums, "col", scatter_dimension=1, tiled=True)
    return summed.astype(jnp.bfloat16)


def decode(ref, step, rows, block_rows, weight):
    groups = block_rows // TILE
    start = pl.multiple_of(step * block_rows, block_rows)
    levels = ref[pl.ds(start, block_rows), :].astype(jnp.int32).astype(jnp.float32)
    codes = ref[pl.ds(rows, CODE_ROWS), :].astype(jnp.int32).astype(jnp.float32)
    pieces = []
    which = lax.broadcasted_iota(jnp.int32, codes.shape, 0)
    for g in range(groups):
        code = jnp.sum(jnp.where(which == step * groups + g, codes, 0.0), axis=0, keepdims=True)
        unit = jnp.exp2(code / STEPS_PER_OCTAVE) * (weight / LEVELS)
        pieces.append(levels[g * TILE : (g + 1) * TILE] * unit)
    return jnp.concatenate(pieces, axis=0)


def encode(acc, step, out_ref, code_ref, rows):
    block_rows = acc.shape[0]
    groups = block_rows // TILE
    pieces = []
    for g in range(groups):
        part = acc[g * TILE : (g + 1) * TILE]
        largest = jnp.max(jnp.abs(part), axis=0, keepdims=True)
        code = jnp.ceil(jnp.log(jnp.maximum(largest, 1e-30)) * (STEPS_PER_OCTAVE / 0.6931471805599453))
        scaled = jnp.round(part * (jnp.exp2(-code / STEPS_PER_OCTAVE) * LEVELS))
        pieces.append(jnp.clip(scaled, -LEVELS, LEVELS).astype(jnp.int32))
        code_ref[pl.ds(step * groups + g, 1), :] = code
    start = pl.multiple_of(step * block_rows, block_rows)
    out_ref[pl.ds(start, block_rows), :] = jnp.concatenate(pieces, axis=0).astype(jnp.int16)

    @pl.when(step == pl.num_programs(0) - 1)
    def _():
        out_ref[pl.ds(rows, CODE_ROWS), :] = code_ref[...].astype(jnp.int32).astype(jnp.int16)


def fetch(chosen, core, mine, other, b, first, sem):
    width = mine[0][0].shape[1]
    here = pl.ds(pl.multiple_of(first + core * width, width), width)
    there = pl.ds(pl.multiple_of(first + (1 - core) * width, width), width)
    for j in range(len(mine)):

        @pl.when(chosen == j)
        def _():
            for parts, lanes in ((mine[j], here), (other[j], there)):
                start = 0
                for part in parts:
                    pltpu.make_async_copy(part, b.at[pl.ds(start, part.shape[0]), lanes], sem).start()
                    start += part.shape[0]


def multiply_kernel(slots, kinds, rows, width, sources, facts, a_ref, *refs):
    held, refs = list(refs[: sum(sources)]), refs[sum(sources) :]
    held = [[held.pop(0) for _ in range(parts)] for parts in sources]
    mine, other = held[: len(held) // 2], held[len(held) // 2 :]
    count = sum(len(kind) for kind in kinds)
    outs, refs = list(refs[:count]), refs[count:]
    b, sems, codes = refs[0], refs[1], list(refs[2:])
    step = pl.program_id(0)

    @pl.when(step == 0)
    def _():
        for j, slot in enumerate(slots):
            fetch(facts[slot] ^ facts[CHIP], facts[CORE], mine, other, b, j * width, sems.at[j])
        for j in range(len(slots)):
            span = b.at[:, pl.ds(j * width, width)]
            pltpu.make_async_copy(span, span, sems.at[j]).wait()

    acc = jnp.dot(a_ref[...], b[...], preferred_element_type=jnp.float32)
    for j, kind in enumerate(kinds):
        part = acc[:, j * width : (j + 1) * width]
        for form in kind:
            out_ref = outs.pop(0)
            if form != "plain":
                lanes = {"coded": slice(None), "left": slice(width // 2), "right": slice(width // 2, None)}[form]
                encode(part[:, lanes], step, out_ref, codes.pop(0), rows)
            else:
                out_ref[...] = part


def multiply(facts, masked, columns, slots, kinds):
    rows, depth = masked.shape
    columns = [x if isinstance(x, tuple) else (x,) for x in columns]
    sources = tuple(len(parts) for parts in columns)
    columns = [part for parts in columns for part in parts]
    width = columns[0].shape[1] * 2
    packed = (rows + CODE_ROWS, width)
    forms = [form for kind in kinds for form in kind]
    part = (packed[0], width // 2)
    specs = {
        "coded": (pl.BlockSpec(packed, lambda i, c: (0, 0)), jax.ShapeDtypeStruct(packed, jnp.int16)),
        "plain": (pl.BlockSpec((BLOCK_ROWS, width), lambda i, c: (i, 0)), jax.ShapeDtypeStruct((rows, width), jnp.float32)),
    }
    specs["left"] = specs["right"] = (pl.BlockSpec(part, lambda i, c: (0, 0)), jax.ShapeDtypeStruct(part, jnp.int16))
    outs = [specs[form] for form in forms]
    return pl.pallas_call(
        functools.partial(multiply_kernel, slots, kinds, rows, width, sources),
        out_shape=[shape for _, shape in outs],
        grid_spec=pltpu.PrefetchScalarGridSpec(
            num_scalar_prefetch=1,
            grid=(rows // BLOCK_ROWS,),
            in_specs=[pl.BlockSpec((BLOCK_ROWS, depth), lambda i, c: (i, 0))]
            + [pl.BlockSpec(memory_space=pl.ANY)] * len(columns),
            out_specs=[spec for spec, _ in outs],
            scratch_shapes=[pltpu.VMEM((depth, width * len(slots)), masked.dtype), pltpu.SemaphoreType.DMA((len(slots),))]
            + [pltpu.VMEM((CODE_ROWS, specs[form][1].shape[1]), jnp.float32) for form in forms if form != "plain"],
        ),
        compiler_params=pltpu.CompilerParams(vmem_limit_bytes=24 * 1024 * 1024),
        cost_estimate=pl.CostEstimate(flops=3000000000, bytes_accessed=9000000, transcendentals=0),
    )(facts, masked, *columns)


def add_kernel(terms, rows, facts, *refs):
    step = pl.program_id(0)
    count = sum(parts for _, parts in terms)
    blocks, refs = list(refs[:count]), refs[count:]
    acc = None
    for weight, parts in terms:
        share = facts[weight].astype(jnp.float32)
        block, *more = [blocks.pop(0) for _ in range(parts)]
        if block.dtype == jnp.int16:
            value = jnp.concatenate([decode(x, step, rows, ADD_ROWS, share) for x in (block, *more)], axis=1)
        else:
            value = block[...] if weight == ALWAYS else block[...] * share
        acc = value if acc is None else acc + value
    if refs[0].dtype == jnp.int16:
        encode(acc, step, refs[0], refs[1], rows)
    else:
        refs[0][...] = acc.astype(refs[0].dtype)


def add(facts, terms, dtype=jnp.int16):
    rows, width = terms[0][0].shape
    terms = [(x if isinstance(x, tuple) else (x,), weight) for x, weight in terms]
    blocks = [part for x, _ in terms for part in x]
    packed = (rows + CODE_ROWS, width)
    plain = pl.BlockSpec((ADD_ROWS, width), lambda i, c: (i, 0))
    coded = pl.BlockSpec(packed, lambda i, c: (0, 0))
    if dtype == jnp.int16:
        out_spec, out_shape = coded, jax.ShapeDtypeStruct(packed, dtype)
        scratch = [pltpu.VMEM((CODE_ROWS, width), jnp.float32)]
    else:
        out_spec, out_shape = plain, jax.ShapeDtypeStruct((rows, width), dtype)
        scratch = []
    return pl.pallas_call(
        functools.partial(add_kernel, tuple((weight, len(x)) for x, weight in terms), rows),
        out_shape=out_shape,
        grid_spec=pltpu.PrefetchScalarGridSpec(
            num_scalar_prefetch=1,
            grid=(rows // ADD_ROWS,),
            in_specs=[pl.BlockSpec(x.shape, lambda i, c: (0, 0)) if x.dtype == jnp.int16 else plain for x in blocks],
            out_specs=out_spec,
            scratch_shapes=scratch,
        ),
        compiler_params=pltpu.CompilerParams(vmem_limit_bytes=16 * 1024 * 1024),
        cost_estimate=pl.CostEstimate(flops=3000000000, bytes_accessed=9000000, transcendentals=0),
    )(facts, *blocks)


def plan_of(chip, at):
    end = at in (0, 3)
    far, near = (3, 2) if at < 2 else (0, 1)
    late = chip == (0 if at < 2 else 3)
    passed = (near, far) if late else (far, near)
    home = 0 if at < 2 else 3
    if end:
        first, second, third, relayed = passed[0], passed[1], 3 - near, (chip, chip)
    else:
        straight = chip ^ home != 3
        first, second = (home, chip) if straight else (chip, home)
        third, relayed = chip, passed
    early = chip != (3 if at < 2 else 0)
    return (first, second, third, *relayed, at, 1, int(end and early), int(end and not early), int(not end))


FIRST, SECOND, THIRD, RELAY_ONE, RELAY_TWO, HERE, ALWAYS, EARLY, LATE, INNER, CORE, CHIP = range(12)


def line_pairs(choose):
    return [(row * 4 + a, row * 4 + b) for row in range(8) for a, b in choose(row // 2)]


def line_of_four(amplitudes, integrals, tile_mask):
    row = lax.axis_index("row")
    at = lax.axis_index("col")
    core, chip = row % 2, row // 2

    def after(value, *others):
        return lax.optimization_barrier((value, *others))[0]

    def across(block, bit):
        return lax.ppermute(block, "row", [(i, i ^ bit) for i in range(8)])

    def along(block, choose):
        return lax.ppermute(block, ("row", "col"), line_pairs(choose))

    def pairs(p):
        return [(0, 1), (1, 0), (2, 3), (3, 2)]

    inward = [(0, 1), (3, 2)]

    def second_pairs(p):
        return inward + [(1, 0)] * (p == 3) + [(2, 3)] * (p == 0)

    def relay_one(p):
        return [(1, 2 if p == 0 else 3), (2, 1 if p == 3 else 0)]

    def relay_two(p):
        return [(1, 3 if p == 0 else 2), (2, 0 if p == 3 else 1)]

    by_x, by_y, twin = across(integrals, 2), across(integrals, 4), across(integrals, 1)
    plans = jnp.asarray([plan_of(p, z) for p in range(4) for z in range(4)], jnp.int32)
    planned = lax.dynamic_slice_in_dim(plans, chip * 4 + at, 1)[0]
    facts = jnp.concatenate([planned, jnp.stack([core, chip]).astype(jnp.int32)])
    masked = apply_mask(amplitudes, tile_mask)
    by_x, by_y = after(by_x, masked, facts), after(by_y, masked, facts)
    half = integrals.shape[0] // 2
    by_both = across(by_y[:half], 2), across(by_x[half:], 4)
    straight = (integrals, by_x, by_y, twin, across(by_x, 1), across(by_y, 1))
    coded, plain = ("coded",), ("plain",)
    out_left, out_right = multiply(facts, masked, straight, (FIRST,), (("left", "right"),))
    one = along(out_left, pairs), along(out_right, pairs)
    (share_one,) = multiply(after(facts, out_right), masked, straight, (RELAY_ONE,), (plain,))
    columns = (*straight[:3], by_both, *straight[3:], tuple(across(after(x, share_one), 1) for x in by_both))
    (out_two,) = multiply(after(facts, share_one, one[0]), masked, columns, (SECOND,), (coded,))
    two = along(out_two, second_pairs)
    out_relay_one = add(after(facts, out_two), [(share_one, ALWAYS), (one, ALWAYS)])
    relayed_one = along(out_relay_one, relay_one)
    out_three, share_two = multiply(
        after(facts, out_relay_one), masked, columns, (THIRD, RELAY_TWO), (coded, plain)
    )
    three = along(out_three, lambda p: inward)
    out_relay_two = add(after(facts, out_three), [(share_two, ALWAYS), (two, ALWAYS)])
    relayed_two = along(out_relay_two, relay_two)
    (own,) = multiply(after(facts, out_relay_two), masked, columns, (HERE,), (plain,))
    most = add(
        facts,
        [(own, ALWAYS), (one, EARLY), (two, LATE), (relayed_one, ALWAYS)],
        jnp.float32,
    )
    return add(facts, [(most, ALWAYS), (three, INNER), (relayed_two, ALWAYS)], jnp.bfloat16)


def solution(mesh):
    body = line_of_four if mesh.shape["col"] == 4 and mesh.shape["row"] == 8 else general
    placed = (P("row", "col"), P("col", "row"), P("row", "col"))
    return jax.shard_map(
        body, mesh=mesh, in_specs=placed, out_specs=P("row", "col"), check_vma=False
    )
```

profile of v0, /device:TPU:10, one launch (start us, length us, event | category | flops | bytes accessed | tf_op | source)
XLA Modules:
  0.0 64.5 jit_solution(7124585165867572947)
XLA Ops:
  0.0 0.0 collective-permute-start.2
  0.0 1.5 %collective-permute-start.1 = (bf16[2048,128]{1,0:T(8,128)(2,1)}, bf16[2048,128]{1,0:T(8,128)(2,1)S(1)}, u32[]{:S(2)}, u32[]{:S(2)}) collective-permute-start(bf16[2048,128]{1,0:T(8,128)(2,1)} %refs_0_.9), channel_id=1, source_target_pairs={{0,16},{4,20},{8,24},{12,28},{16,0},{20,4},{24,8},{28,12},{1,17},{... | collective-permute-start | bytes 1572872 | tf_op jit(solution)/shard_map/ppermute | solution.py:226
  1.5 0.5 collective-permute-start
  2.1 0.7 %convert_element_type.3 = bf16[8,16]{1,0:T(8,128)(2,1)S(1)} convert(s32[8,16]{1,0:T(8,128)} %param.6) | non-fusion elementwise | flops 128 | bytes 768 | tf_op jit(solution)/shard_map/convert_element_type | solution.py:23
  2.7 0.0 copy-start.1
  2.8 0.8 %dynamic-slice_bitcast_fusion = s32[10]{0:T(128)S(1)} fusion(s32[16,10]{1,0:T(8,128)} %constant.40.clone, s32[]{:T(128)S(6)} %select_n.15), kind=kLoop, calls=%fused_computation.2 | loop fusion | bytes 84 | tf_op jit(solution)/shard_map/squeeze | solution.py:247
  3.6 0.1 pad_add_fusion.facts
  3.7 0.6 mul.15
  4.3 0.7 %copy-done.1 = bf16[1024,2048]{1,0:T(8,128)(2,1)S(1)} copy-done((bf16[1024,2048]{1,0:T(8,128)(2,1)S(1)}, bf16[1024,2048]{1,0:T(8,128)(2,1)}, u32[]{:S(2)}) %copy-start.1) | copy-done | bytes 4194328
  5.0 0.0 copy-start
  5.0 0.9 %bitcast_multiply_fusion.a_ref = bf16[1024,2048]{1,0:T(8,128)(2,1)S(1)} fusion(bf16[1024,2048]{1,0:T(8,128)(2,1)S(1)} %copy-done.1, bf16[128,8,16,128]{3,2,1,0:T(8,128)(2,1)S(1)} %bitcast.8), kind=kLoop, calls=%fused_computation | loop fusion | flops 2097152 | bytes 12582912 | tf_op jit(solution)/shard_map/mul | solution.py:24
  5.9 8.7 %collective-permute-done.1.refs_2_ = bf16[2048,128]{1,0:T(8,128)(2,1)S(1)} collective-permute-done((bf16[2048,128]{1,0:T(8,128)(2,1)}, bf16[2048,128]{1,0:T(8,128)(2,1)S(1)}, u32[]{:S(2)}, u32[]{:S(2)}) %collective-permute-start.1) | collective-permute-done | bytes 524320 | tf_op jit(solution)/shard_map/ppermute | solution.py:226
  14.6 1.2 %collective-permute-done.refs_1_ = bf16[2048,128]{1,0:T(8,128)(2,1)S(1)} collective-permute-done((bf16[2048,128]{1,0:T(8,128)(2,1)}, bf16[2048,128]{1,0:T(8,128)(2,1)S(1)}, u32[]{:S(2)}, u32[]{:S(2)}) %collective-permute-start) | collective-permute-done | bytes 524320 | tf_op jit(solution)/shard_map/ppermute | solution.py:226
  15.8 0.0 collective-permute-start.3
  15.8 0.5 collective-permute-start.4
  16.4 0.6 collective-permute-start.6
  17.0 0.5 collective-permute-start.7
  17.5 0.0 collective-permute-done.2.refs_3_.refs_5_
  17.5 0.2 collective-permute-done.3.refs_4_.refs_6_
  17.7 0.7 %collective-permute-done.4.refs_5_.refs_7_ = bf16[2048,128]{1,0:T(8,128)(2,1)S(1)} collective-permute-done((bf16[2048,128]{1,0:T(8,128)(2,1)S(1)}, bf16[2048,128]{1,0:T(8,128)(2,1)S(1)}, u32[]{:S(2)}, u32[]{:S(2)}) %collective-permute-start.4) | collective-permute-done | bytes 524320 | tf_op jit(solution)/shard_map/ppermute | solution.py:226
  18.5 0.0 copy-done
  18.5 2.5 %shard_map.46 = (s16[1040,128]{1,0:T(8,128)(2,1)S(1)}, s16[1040,128]{1,0:T(8,128)(2,1)S(1)}) custom-call(s32[12]{0:T(128)S(1)} %pad_add_fusion.facts, bf16[1024,2048]{1,0:T(8,128)(2,1)S(1)} %bitcast_multiply_fusion.a_ref, bf16[2048,128]{1,0:T(8,128)(2,1)S(1)} %copy-done, bf16[2048,128]{1,0:T(8,128)(2,1)S(1)} %collective-permute-done.refs_1_, ...), custom_call_target="tpu_custom_call" | custom-call | flops 3000000000 | bytes 9000000 | tf_op jit(solution)/shard_map/pallas_call | solution.py:130
  20.9 0.5 collective-permute-start.5
  21.5 2.2 %shard_map.47.refs_0_ = f32[1024,256]{1,0:T(8,128)S(1)} custom-call(s32[12]{0:T(128)S(1)} %pad_add_fusion.facts, bf16[1024,2048]{1,0:T(8,128)(2,1)S(1)} %bitcast_multiply_fusion.a_ref, bf16[2048,128]{1,0:T(8,128)(2,1)S(1)} %copy-done, bf16[2048,128]{1,0:T(8,128)(2,1)S(1)} %collective-permute-done.refs_1_, ...), custom_call_target="tpu_custom_call" | custom-call | flops 3000000000 | bytes 9000000 | tf_op jit(solution)/shard_map/pallas_call | solution.py:130
  23.7 1.2 %collective-permute-done.7.refs_4_ = bf16[1024,128]{1,0:T(8,128)(2,1)S(1)} collective-permute-done((bf16[1024,128]{1,0:T(8,128)(2,1)S(1)}, bf16[1024,128]{1,0:T(8,128)(2,1)S(1)}, u32[]{:S(2)}, u32[]{:S(2)}) %collective-permute-start.7) | collective-permute-done | bytes 262176 | tf_op jit(solution)/shard_map/ppermute | solution.py:226
  24.9 0.0 collective-permute-done.6.refs_3_
  24.9 0.0 collective-permute-start.8
  24.9 0.5 collective-permute-start.9
  25.4 0.5 collective-permute-start.10
  25.9 4.4 %collective-permute-done.5.refs_1_ = s16[1040,128]{1,0:T(8,128)(2,1)S(1)} collective-permute-done((s16[1040,128]{1,0:T(8,128)(2,1)S(1)}, s16[1040,128]{1,0:T(8,128)(2,1)S(1)}, u32[]{:S(2)}, u32[]{:S(2)}) %collective-permute-start.5) | collective-permute-done | bytes 266272 | tf_op jit(solution)/shard_map/ppermute | solution.py:229
  30.2 0.0 collective-permute-done.8.refs_8_
  30.2 0.0 collective-permute-done.9.refs_9_
  30.2 2.4 %shard_map.48 = s16[1040,256]{1,0:T(8,128)(2,1)S(1)} custom-call(s32[12]{0:T(128)S(1)} %pad_add_fusion.facts, bf16[1024,2048]{1,0:T(8,128)(2,1)S(1)} %bitcast_multiply_fusion.a_ref, bf16[2048,128]{1,0:T(8,128)(2,1)S(1)} %copy-done, bf16[2048,128]{1,0:T(8,128)(2,1)S(1)} %collective-permute-done.refs_1_, bf16[2048,128]{1,0:T(8,128)(2,1)S(1)} %collective-permute-done.1.refs_2_, ...), custom_call_target="tpu_custom_call" | custom-call | flops 3000000000 | bytes 9000000 | tf_op jit(solution)/shard_map/pallas_call | solution.py:130
  32.6 1.3 %collective-permute-start.11 = (s16[1040,256]{1,0:T(8,128)(2,1)S(1)}, s16[1040,256]{1,0:T(8,128)(2,1)S(1)}, u32[]{:S(2)}, u32[]{:S(2)}) collective-permute-start(s16[1040,256]{1,0:T(8,128)(2,1)S(1)} %shard_map.48), channel_id=1, source_target_pairs={{0,1},{3,2},{2,3},{4,5},{7,6},{6,7},{8,9},{11,10},{12,13},{15,14},... | collective-permute-start | bytes 1597448 | tf_op jit(solution)/shard_map/ppermute | solution.py:229
  33.9 1.2 %collective-permute-done.10.refs_2_ = s16[1040,128]{1,0:T(8,128)(2,1)S(1)} collective-permute-done((s16[1040,128]{1,0:T(8,128)(2,1)S(1)}, s16[1040,128]{1,0:T(8,128)(2,1)S(1)}, u32[]{:S(2)}, u32[]{:S(2)}) %collective-permute-start.10) | collective-permute-done | bytes 266272 | tf_op jit(solution)/shard_map/ppermute | solution.py:229
  35.1 1.0 %shard_map.49 = s16[1040,256]{1,0:T(8,128)(2,1)S(1)} custom-call(s32[12]{0:T(128)S(1)} %pad_add_fusion.facts, f32[1024,256]{1,0:T(8,128)S(1)} %shard_map.47.refs_0_, s16[1040,128]{1,0:T(8,128)(2,1)S(1)} %collective-permute-done.5.refs_1_, s16[1040,128]{1,0:T(8,128)(2,1)S(1)} %collective-permute-done.10.refs_2_), custom_call_target="tpu_custom_call" | custom-call | flops 3000000000 | bytes 9000000 | tf_op jit(solution)/shard_map/pallas_call | solution.py:179
  36.1 4.5 %collective-permute-start.12 = (s16[1040,256]{1,0:T(8,128)(2,1)S(1)}, s16[1040,256]{1,0:T(8,128)(2,1)S(1)}, u32[]{:S(2)}, u32[]{:S(2)}) collective-permute-start(s16[1040,256]{1,0:T(8,128)(2,1)S(1)} %shard_map.49), channel_id=1, source_target_pairs={{1,2},{2,0},{5,6},{6,4},{9,11},{10,8},{13,15},{14,12},{17,19},{18,... | collective-permute-start | bytes 1597448 | tf_op jit(solution)/shard_map/ppermute | solution.py:229
  40.7 3.7 %shard_map.50 = (s16[1040,256]{1,0:T(8,128)(2,1)S(1)}, f32[1024,256]{1,0:T(8,128)S(1)}) custom-call(s32[12]{0:T(128)S(1)} %pad_add_fusion.facts, bf16[1024,2048]{1,0:T(8,128)(2,1)S(1)} %bitcast_multiply_fusion.a_ref, bf16[2048,128]{1,0:T(8,128)(2,1)S(1)} %copy-done, bf16[2048,128]{1,0:T(8,128)(2,1)S(1)} %collective-permute-done.refs_1_, ...), custom_call_target="tpu_custom_call" | custom-call | flops 3000000000 | bytes 9000000 | tf_op jit(solution)/shard_map/pallas_call | solution.py:130
  44.4 1.3 %collective-permute-start.13 = (s16[1040,256]{1,0:T(8,128)(2,1)S(1)}, s16[1040,256]{1,0:T(8,128)(2,1)S(1)}, u32[]{:S(2)}, u32[]{:S(2)}) collective-permute-start(s16[1040,256]{1,0:T(8,128)(2,1)S(1)} %get-tuple-element.29), channel_id=1, source_target_pairs={{0,1},{3,2},{4,5},{7,6},{8,9},{11,10},{12,13},{15,14},{16,17},{19,... | collective-permute-start | bytes 1597448 | tf_op jit(solution)/shard_map/ppermute | solution.py:229
  45.7 1.3 %collective-permute-done.11.refs_1_.refs_3_ = s16[1040,256]{1,0:T(8,128)(2,1)S(1)} collective-permute-done((s16[1040,256]{1,0:T(8,128)(2,1)S(1)}, s16[1040,256]{1,0:T(8,128)(2,1)S(1)}, u32[]{:S(2)}, u32[]{:S(2)}) %collective-permute-start.11) | collective-permute-done | bytes 532512 | tf_op jit(solution)/shard_map/ppermute | solution.py:229
  47.0 1.0 %shard_map.51 = s16[1040,256]{1,0:T(8,128)(2,1)S(1)} custom-call(s32[12]{0:T(128)S(1)} %pad_add_fusion.facts, f32[1024,256]{1,0:T(8,128)S(1)} %get-tuple-element.31.refs_0_, s16[1040,256]{1,0:T(8,128)(2,1)S(1)} %collective-permute-done.11.refs_1_.refs_3_), custom_call_target="tpu_custom_call" | custom-call | flops 3000000000 | bytes 9000000 | tf_op jit(solution)/shard_map/pallas_call | solution.py:179
  48.0 4.8 %collective-permute-start.14 = (s16[1040,256]{1,0:T(8,128)(2,1)S(1)}, s16[1040,256]{1,0:T(8,128)(2,1)S(1)}, u32[]{:S(2)}, u32[]{:S(2)}) collective-permute-start(s16[1040,256]{1,0:T(8,128)(2,1)S(1)} %shard_map.51), channel_id=1, source_target_pairs={{1,3},{2,1},{5,7},{6,5},{9,10},{10,9},{13,14},{14,13},{17,18},{18,... | collective-permute-start | bytes 1597448 | tf_op jit(solution)/shard_map/ppermute | solution.py:229
  52.8 2.2 %shard_map.52.refs_0_ = f32[1024,256]{1,0:T(8,128)S(1)} custom-call(s32[12]{0:T(128)S(1)} %pad_add_fusion.facts, bf16[1024,2048]{1,0:T(8,128)(2,1)S(1)} %bitcast_multiply_fusion.a_ref, bf16[2048,128]{1,0:T(8,128)(2,1)S(1)} %copy-done, bf16[2048,128]{1,0:T(8,128)(2,1)S(1)} %collective-permute-done.refs_1_, ...), custom_call_target="tpu_custom_call" | custom-call | flops 3000000000 | bytes 9000000 | tf_op jit(solution)/shard_map/pallas_call | solution.py:130
  55.1 0.0 collective-permute-done.12.refs_4_
  55.1 1.1 %shard_map.53.refs_0_ = f32[1024,256]{1,0:T(8,128)S(1)} custom-call(s32[12]{0:T(128)S(1)} %pad_add_fusion.facts, f32[1024,256]{1,0:T(8,128)S(1)} %shard_map.52.refs_0_, s16[1040,128]{1,0:T(8,128)(2,1)S(1)} %collective-permute-done.5.refs_1_, s16[1040,128]{1,0:T(8,128)(2,1)S(1)} %collective-permute-done.10.refs_2_, ...), custom_call_target="tpu_custom_call" | custom-call | flops 3000000000 | bytes 9000000 | tf_op jit(solution)/shard_map/pallas_call | solution.py:179
  56.2 3.2 %collective-permute-done.13.refs_1_ = s16[1040,256]{1,0:T(8,128)(2,1)S(1)} collective-permute-done((s16[1040,256]{1,0:T(8,128)(2,1)S(1)}, s16[1040,256]{1,0:T(8,128)(2,1)S(1)}, u32[]{:S(2)}, u32[]{:S(2)}) %collective-permute-start.13) | collective-permute-done | bytes 532512 | tf_op jit(solution)/shard_map/ppermute | solution.py:229
  59.3 3.5 %collective-permute-done.14.refs_2_ = s16[1040,256]{1,0:T(8,128)(2,1)S(1)} collective-permute-done((s16[1040,256]{1,0:T(8,128)(2,1)S(1)}, s16[1040,256]{1,0:T(8,128)(2,1)S(1)}, u32[]{:S(2)}, u32[]{:S(2)}) %collective-permute-start.14) | collective-permute-done | bytes 532512 | tf_op jit(solution)/shard_map/ppermute | solution.py:229
  62.8 1.6 %shard_map.54 = bf16[1024,256]{1,0:T(8,128)(2,1)} custom-call(s32[12]{0:T(128)S(1)} %pad_add_fusion.facts, f32[1024,256]{1,0:T(8,128)S(1)} %shard_map.53.refs_0_, s16[1040,256]{1,0:T(8,128)(2,1)S(1)} %collective-permute-done.13.refs_1_, s16[1040,256]{1,0:T(8,128)(2,1)S(1)} %collective-permute-done.14.refs_2_), custom_call_target="tpu_custom_call" | custom-call | flops 3000000000 | bytes 9000000 | tf_op jit(solution)/shard_map/pallas_call | solution.py:179
  (2 shorter events, 0.0 us)
Async XLA Ops:
  0.0 17.5 %collective-permute-start.2 = (bf16[2048,128]{1,0:T(8,128)(2,1)}, bf16[2048,128]{1,0:T(8,128)(2,1)S(1)}, u32[]{:S(2)}, u32[]{:S(2)}) collective-permute-start(bf16[2048,128]{1,0:T(8,128)(2,1)} %refs_0_.9), channel_id=1, source_target_pairs={{0,4},{4,0},{8,12},{12,8},{16,20},{20,16},{24,28},{28,24},{1,5},{5... | collective-permute-start | bytes 1572872 | tf_op jit(solution)/shard_map/ppermute | solution.py:226
  0.0 14.5 %collective-permute-start.1 = (bf16[2048,128]{1,0:T(8,128)(2,1)}, bf16[2048,128]{1,0:T(8,128)(2,1)S(1)}, u32[]{:S(2)}, u32[]{:S(2)}) collective-permute-start(bf16[2048,128]{1,0:T(8,128)(2,1)} %refs_0_.9), channel_id=1, source_target_pairs={{0,16},{4,20},{8,24},{12,28},{16,0},{20,4},{24,8},{28,12},{1,17},{... | collective-permute-start | bytes 1572872 | tf_op jit(solution)/shard_map/ppermute | solution.py:226
  1.5 14.3 %collective-permute-start = (bf16[2048,128]{1,0:T(8,128)(2,1)}, bf16[2048,128]{1,0:T(8,128)(2,1)S(1)}, u32[]{:S(2)}, u32[]{:S(2)}) collective-permute-start(bf16[2048,128]{1,0:T(8,128)(2,1)} %refs_0_.9), channel_id=1, source_target_pairs={{0,8},{4,12},{8,0},{12,4},{16,24},{20,28},{24,16},{28,20},{1,9},{5... | collective-permute-start | bytes 1572872 | tf_op jit(solution)/shard_map/ppermute | solution.py:226
  2.7 2.2 %copy-start.1 = (bf16[1024,2048]{1,0:T(8,128)(2,1)S(1)}, bf16[1024,2048]{1,0:T(8,128)(2,1)}, u32[]{:S(2)}) copy-start(bf16[1024,2048]{1,0:T(8,128)(2,1)} %param.4) | copy-start | bytes 12582916
  5.0 13.5 %copy-start = (bf16[2048,128]{1,0:T(8,128)(2,1)S(1)}, bf16[2048,128]{1,0:T(8,128)(2,1)}, u32[]{:S(2)}) copy-start(bf16[2048,128]{1,0:T(8,128)(2,1)} %refs_0_.9) | copy-start | bytes 1572868
  15.8 1.9 %collective-permute-start.3 = (bf16[2048,128]{1,0:T(8,128)(2,1)S(1)}, bf16[2048,128]{1,0:T(8,128)(2,1)S(1)}, u32[]{:S(2)}, u32[]{:S(2)}) collective-permute-start(bf16[2048,128]{1,0:T(8,128)(2,1)S(1)} %collective-permute-done.refs_1_), channel_id=1, source_target_pairs={{0,4},{4,0},{8,12},{12,8},{16,20},{20,16},{24,28},{28,24},{1,5},{5... | collective-permute-start | bytes 1572872 | tf_op jit(solution)/shard_map/ppermute | solution.py:226
  15.8 2.7 %collective-permute-start.4 = (bf16[2048,128]{1,0:T(8,128)(2,1)S(1)}, bf16[2048,128]{1,0:T(8,128)(2,1)S(1)}, u32[]{:S(2)}, u32[]{:S(2)}) collective-permute-start(bf16[2048,128]{1,0:T(8,128)(2,1)S(1)} %collective-permute-done.1.refs_2_), channel_id=1, source_target_pairs={{0,4},{4,0},{8,12},{12,8},{16,20},{20,16},{24,28},{28,24},{1,5},{5... | collective-permute-start | bytes 1572872 | tf_op jit(solution)/shard_map/ppermute | solution.py:226
  16.4 8.5 %collective-permute-start.6 = (bf16[1024,128]{1,0:T(8,128)(2,1)S(1)}, bf16[1024,128]{1,0:T(8,128)(2,1)S(1)}, u32[]{:S(2)}, u32[]{:S(2)}) collective-permute-start(bf16[1024,128]{1,0:T(8,128)(2,1)S(1)} %slice.6), channel_id=1, source_target_pairs={{0,8},{4,12},{8,0},{12,4},{16,24},{20,28},{24,16},{28,20},{1,9},{5... | collective-permute-start | bytes 786440 | tf_op jit(solution)/shard_map/ppermute | solution.py:226
  17.0 7.9 %collective-permute-start.7 = (bf16[1024,128]{1,0:T(8,128)(2,1)S(1)}, bf16[1024,128]{1,0:T(8,128)(2,1)S(1)}, u32[]{:S(2)}, u32[]{:S(2)}) collective-permute-start(bf16[1024,128]{1,0:T(8,128)(2,1)S(1)} %slice.7), channel_id=1, source_target_pairs={{0,16},{4,20},{8,24},{12,28},{16,0},{20,4},{24,8},{28,12},{1,17},{... | collective-permute-start | bytes 786440 | tf_op jit(solution)/shard_map/ppermute | solution.py:226
  20.9 9.3 %collective-permute-start.5 = (s16[1040,128]{1,0:T(8,128)(2,1)S(1)}, s16[1040,128]{1,0:T(8,128)(2,1)S(1)}, u32[]{:S(2)}, u32[]{:S(2)}) collective-permute-start(s16[1040,128]{1,0:T(8,128)(2,1)S(1)} %get-tuple-element.23), channel_id=1, source_target_pairs={{0,1},{1,0},{2,3},{3,2},{4,5},{5,4},{6,7},{7,6},{8,9},{9,8},{10,11... | collective-permute-start | bytes 798728 | tf_op jit(solution)/shard_map/ppermute | solution.py:229
  24.9 5.4 %collective-permute-start.8 = (bf16[1024,128]{1,0:T(8,128)(2,1)S(1)}, bf16[1024,128]{1,0:T(8,128)(2,1)S(1)}, u32[]{:S(2)}, u32[]{:S(2)}) collective-permute-start(bf16[1024,128]{1,0:T(8,128)(2,1)S(1)} %collective-permute-done.6.refs_3_), channel_id=1, source_target_pairs={{0,4},{4,0},{8,12},{12,8},{16,20},{20,16},{24,28},{28,24},{1,5},{5... | collective-permute-start | bytes 786440 | tf_op jit(solution)/shard_map/ppermute | solution.py:226
  24.9 5.4 %collective-permute-start.9 = (bf16[1024,128]{1,0:T(8,128)(2,1)S(1)}, bf16[1024,128]{1,0:T(8,128)(2,1)S(1)}, u32[]{:S(2)}, u32[]{:S(2)}) collective-permute-start(bf16[1024,128]{1,0:T(8,128)(2,1)S(1)} %collective-permute-done.7.refs_4_), channel_id=1, source_target_pairs={{0,4},{4,0},{8,12},{12,8},{16,20},{20,16},{24,28},{28,24},{1,5},{5... | collective-permute-start | bytes 786440 | tf_op jit(solution)/shard_map/ppermute | solution.py:226
  25.4 9.7 %collective-permute-start.10 = (s16[1040,128]{1,0:T(8,128)(2,1)S(1)}, s16[1040,128]{1,0:T(8,128)(2,1)S(1)}, u32[]{:S(2)}, u32[]{:S(2)}) collective-permute-start(s16[1040,128]{1,0:T(8,128)(2,1)S(1)} %get-tuple-element.21), channel_id=1, source_target_pairs={{0,1},{1,0},{2,3},{3,2},{4,5},{5,4},{6,7},{7,6},{8,9},{9,8},{10,11... | collective-permute-start | bytes 798728 | tf_op jit(solution)/shard_map/ppermute | solution.py:229
  32.6 14.4 %collective-permute-start.11 = (s16[1040,256]{1,0:T(8,128)(2,1)S(1)}, s16[1040,256]{1,0:T(8,128)(2,1)S(1)}, u32[]{:S(2)}, u32[]{:S(2)}) collective-permute-start(s16[1040,256]{1,0:T(8,128)(2,1)S(1)} %shard_map.48), channel_id=1, source_target_pairs={{0,1},{3,2},{2,3},{4,5},{7,6},{6,7},{8,9},{11,10},{12,13},{15,14},... | collective-permute-start | bytes 1597448 | tf_op jit(solution)/shard_map/ppermute | solution.py:229
  36.1 18.9 %collective-permute-start.12 = (s16[1040,256]{1,0:T(8,128)(2,1)S(1)}, s16[1040,256]{1,0:T(8,128)(2,1)S(1)}, u32[]{:S(2)}, u32[]{:S(2)}) collective-permute-start(s16[1040,256]{1,0:T(8,128)(2,1)S(1)} %shard_map.49), channel_id=1, source_target_pairs={{1,2},{2,0},{5,6},{6,4},{9,11},{10,8},{13,15},{14,12},{17,19},{18,... | collective-permute-start | bytes 1597448 | tf_op jit(solution)/shard_map/ppermute | solution.py:229
  44.4 14.9 %collective-permute-start.13 = (s16[1040,256]{1,0:T(8,128)(2,1)S(1)}, s16[1040,256]{1,0:T(8,128)(2,1)S(1)}, u32[]{:S(2)}, u32[]{:S(2)}) collective-permute-start(s16[1040,256]{1,0:T(8,128)(2,1)S(1)} %get-tuple-element.29), channel_id=1, source_target_pairs={{0,1},{3,2},{4,5},{7,6},{8,9},{11,10},{12,13},{15,14},{16,17},{19,... | collective-permute-start | bytes 1597448 | tf_op jit(solution)/shard_map/ppermute | solution.py:229
  48.0 14.8 %collective-permute-start.14 = (s16[1040,256]{1,0:T(8,128)(2,1)S(1)}, s16[1040,256]{1,0:T(8,128)(2,1)S(1)}, u32[]{:S(2)}, u32[]{:S(2)}) collective-permute-start(s16[1040,256]{1,0:T(8,128)(2,1)S(1)} %shard_map.51), channel_id=1, source_target_pairs={{1,3},{2,1},{5,7},{6,5},{9,10},{10,9},{13,14},{14,13},{17,18},{18,... | collective-permute-start | bytes 1597448 | tf_op jit(solution)/shard_map/ppermute | solution.py:229
where the time goes:
time: 65.6 us; the launch traced here: 64.5 us
  waiting for transfers between devices  25.7 us (39%)
  Pallas kernels  17.7 us (27%)
  starting transfers between devices  17.1 us (26%)
  local copies, waits for them, and re-layouts  2.16 us (3%)
  other arithmetic  1.67 us (3%)
    ppermute x6, waiting for transfers between devices, along(): return lax.ppermute(block, ('row', 'col'), line_pairs(choose))  13.6 us
    pallas_call x5, Pallas kernels, multiply(): pl.pallas_call(functools.partial(multiply_kernel, slots, kinds, rows, wid...  13.1 us
    ppermute x6, starting transfers between devices, along(): return lax.ppermute(block, ('row', 'col'), line_pairs(choose))  12.9 us
    ppermute x9, waiting for transfers between devices, across(): return lax.ppermute(block, 'row', [(i, i ^ bit) for i in range(8)])  12.1 us
    pallas_call x4, Pallas kernels, add(): pl.pallas_call(functools.partial(add_kernel, tuple(((weight, len(x)) for...  4.68 us
    ppermute x9, starting transfers between devices, across(): return lax.ppermute(block, 'row', [(i, i ^ bit) for i in range(8)])  4.18 us
  transfers between devices with their start and end apart: 15, of which 10 were waited for; matrix products, arithmetic and copies ran while one was open for 5% of the time, Pallas kernels for 25%

commit v1 on v0

--- a/solution.py
+++ b/solution.py
@@ -163,12 +163,14 @@
         refs[0][...] = acc.astype(refs[0].dtype)
 
 
-def add(facts, terms, dtype=jnp.int16):
+def add(facts, terms, dtype=jnp.int16, side=None):
     rows, width = terms[0][0].shape
+    if side is not None:
+        width //= 2
     terms = [(x if isinstance(x, tuple) else (x,), weight) for x, weight in terms]
     blocks = [part for x, _ in terms for part in x]
     packed = (rows + CODE_ROWS, width)
-    plain = pl.BlockSpec((ADD_ROWS, width), lambda i, c: (i, 0))
+    plain = pl.BlockSpec((ADD_ROWS, width), lambda i, c: (i, side or 0))
     coded = pl.BlockSpec(packed, lambda i, c: (0, 0))
     if dtype == jnp.int16:
         out_spec, out_shape = coded, jax.ShapeDtypeStruct(packed, dtype)
@@ -256,19 +258,21 @@
     one = along(out_left, pairs), along(out_right, pairs)
     (share_one,) = multiply(after(facts, out_right), masked, straight, (RELAY_ONE,), (plain,))
     columns = (*straight[:3], by_both, *straight[3:], tuple(across(after(x, share_one), 1) for x in by_both))
-    (out_two,) = multiply(after(facts, share_one, one[0]), masked, columns, (SECOND,), (coded,))
-    two = along(out_two, second_pairs)
-    out_relay_one = add(after(facts, out_two), [(share_one, ALWAYS), (one, ALWAYS)])
+    *out_two, own = multiply(
+        after(facts, share_one, one[0]), masked, columns, (SECOND, HERE), (("left", "right"), plain)
+    )
+    two = along(out_two[0], second_pairs), along(out_two[1], second_pairs)
+    out_relay_one = add(after(facts, *out_two), [(share_one, ALWAYS), (one, ALWAYS)])
     relayed_one = along(out_relay_one, relay_one)
     out_three, share_two = multiply(
         after(facts, out_relay_one), masked, columns, (THIRD, RELAY_TWO), (coded, plain)
     )
-    three = along(out_three, lambda p: inward)
-    out_relay_two = add(after(facts, out_three), [(share_two, ALWAYS), (two, ALWAYS)])
-    relayed_two = along(out_relay_two, relay_two)
-    (own,) = multiply(after(facts, out_relay_two), masked, columns, (HERE,), (plain,))
+    relay_left = add(after(facts, out_three), [(share_two, ALWAYS), (two[0], ALWAYS)], side=0)
+    three = along(after(out_three, relay_left), lambda p: inward)
+    relay_right = add(after(facts, relay_left), [(share_two, ALWAYS), (two[1], ALWAYS)], side=1)
+    relayed_two = along(relay_left, relay_two), along(relay_right, relay_two)
     most = add(
-        facts,
+        after(facts, relay_right),
         [(own, ALWAYS), (one, EARLY), (two, LATE), (relayed_one, ALWAYS)],
         jnp.float32,
     )

time: 65.6 us -> 68.1 us (1.038)
  starting transfers between devices: 17.1 us -> 20.5 us
  waiting for transfers between devices: 25.7 us -> 24.7 us
    ppermute x6 -> x8, starting transfers between devices: 12.9 us -> 16.3 us  [along(): return lax.ppermute(block, ('row', 'col'), line_pairs(choose))]
    ppermute x6 -> x8, waiting for transfers between devices: 13.6 us -> 12.6 us  [along(): return lax.ppermute(block, ('row', 'col'), line_pairs(choose))]
    pallas_call x5 -> x4, Pallas kernels: 13.1 us -> 12.3 us  [multiply(): pl.pallas_call(functools.partial(multiply_kernel, slots, kinds, rows, wid...]
    pallas_call x4 -> x5, Pallas kernels: 4.68 us -> 5.43 us  [add(): pl.pallas_call(functools.partial(add_kernel, tuple(((weight, len(x)) for...]
  transfers between devices with their start and end apart: 15 -> 17, of which waited for: 10 -> 8; matrix products, arithmetic and copies ran while one was open for 5% -> 5% of each run, Pallas kernels for 25% -> 24%
where the time goes in v1:
time: 68.1 us; the launch traced here: 67 us
  waiting for transfers between devices  24.7 us (36%)
  starting transfers between devices  20.5 us (30%)
  Pallas kernels  17.7 us (26%)
  local copies, waits for them, and re-layouts  2.16 us (3%)
  other arithmetic  1.67 us (2%)
    ppermute x8, starting transfers between devices, along(): return lax.ppermute(block, ('row', 'col'), line_pairs(choose))  16.3 us
    ppermute x8, waiting for transfers between devices, along(): return lax.ppermute(block, ('row', 'col'), line_pairs(choose))  12.6 us
    pallas_call x4, Pallas kernels, multiply(): pl.pallas_call(functools.partial(multiply_kernel, slots, kinds, rows, wid...  12.3 us
    ppermute x9, waiting for transfers between devices, across(): return lax.ppermute(block, 'row', [(i, i ^ bit) for i in range(8)])  12.1 us
    pallas_call x5, Pallas kernels, add(): pl.pallas_call(functools.partial(add_kernel, tuple(((weight, len(x)) for...  5.43 us
    ppermute x9, starting transfers between devices, across(): return lax.ppermute(block, 'row', [(i, i ^ bit) for i in range(8)])  4.18 us
  transfers between devices with their start and end apart: 17, of which 8 were waited for; matrix products, arithmetic and copies ran while one was open for 5% of the time, Pallas kernels for 24%

profile of v1, /device:TPU:10, one launch (start us, length us, event | category | flops | bytes accessed | tf_op | source)
XLA Modules:
  0.0 67.0 jit_solution(2297985302593165933)
XLA Ops:
  0.0 0.0 collective-permute-start.2
  0.0 1.5 %collective-permute-start.1 = (bf16[2048,128]{1,0:T(8,128)(2,1)}, bf16[2048,128]{1,0:T(8,128)(2,1)S(1)}, u32[]{:S(2)}, u32[]{:S(2)}) collective-permute-start(bf16[2048,128]{1,0:T(8,128)(2,1)} %refs_0_.7), channel_id=1, source_target_pairs={{0,16},{4,20},{8,24},{12,28},{16,0},{20,4},{24,8},{28,12},{1,17},{... | collective-permute-start | bytes 1572872 | tf_op jit(solution)/shard_map/ppermute | solution.py:228
  1.5 0.5 collective-permute-start
  2.1 0.7 %convert_element_type.3 = bf16[8,16]{1,0:T(8,128)(2,1)S(1)} convert(s32[8,16]{1,0:T(8,128)} %param.6) | non-fusion elementwise | flops 128 | bytes 768 | tf_op jit(solution)/shard_map/convert_element_type | solution.py:23
  2.8 0.8 %dynamic-slice_bitcast_fusion = s32[10]{0:T(128)S(1)} fusion(s32[16,10]{1,0:T(8,128)} %constant.40.clone, s32[]{:T(128)S(6)} %select_n.15), kind=kLoop, calls=%fused_computation.2 | loop fusion | bytes 84 | tf_op jit(solution)/shard_map/squeeze | solution.py:249
  3.6 0.1 pad_add_fusion.facts
  3.7 0.6 mul.15
  4.3 0.7 copy-done.1
  5.0 0.9 %bitcast_multiply_fusion.a_ref = bf16[1024,2048]{1,0:T(8,128)(2,1)S(1)} fusion(bf16[1024,2048]{1,0:T(8,128)(2,1)S(1)} %copy-done.1, bf16[128,8,16,128]{3,2,1,0:T(8,128)(2,1)S(1)} %bitcast.8), kind=kLoop, calls=%fused_computation | loop fusion | flops 2097152 | bytes 12582912 | tf_op jit(solution)/shard_map/mul | solution.py:24
  5.9 8.7 %collective-permute-done.1.refs_2_ = bf16[2048,128]{1,0:T(8,128)(2,1)S(1)} collective-permute-done((bf16[2048,128]{1,0:T(8,128)(2,1)}, bf16[2048,128]{1,0:T(8,128)(2,1)S(1)}, u32[]{:S(2)}, u32[]{:S(2)}) %collective-permute-start.1) | collective-permute-done | bytes 524320 | tf_op jit(solution)/shard_map/ppermute | solution.py:228
  14.6 1.2 %collective-permute-done.refs_1_ = bf16[2048,128]{1,0:T(8,128)(2,1)S(1)} collective-permute-done((bf16[2048,128]{1,0:T(8,128)(2,1)}, bf16[2048,128]{1,0:T(8,128)(2,1)S(1)}, u32[]{:S(2)}, u32[]{:S(2)}) %collective-permute-start) | collective-permute-done | bytes 524320 | tf_op jit(solution)/shard_map/ppermute | solution.py:228
  15.8 0.0 collective-permute-start.3
  15.8 0.5 collective-permute-start.4
  16.4 0.6 collective-permute-start.6
  17.0 0.5 collective-permute-start.7
  17.5 0.0 collective-permute-done.2.refs_3_.refs_5_
  17.5 0.2 collective-permute-done.3.refs_4_.refs_6_
  17.7 0.7 %collective-permute-done.4.refs_5_.refs_7_ = bf16[2048,128]{1,0:T(8,128)(2,1)S(1)} collective-permute-done((bf16[2048,128]{1,0:T(8,128)(2,1)S(1)}, bf16[2048,128]{1,0:T(8,128)(2,1)S(1)}, u32[]{:S(2)}, u32[]{:S(2)}) %collective-permute-start.4) | collective-permute-done | bytes 524320 | tf_op jit(solution)/shard_map/ppermute | solution.py:228
  18.5 2.5 %shard_map.46 = (s16[1040,128]{1,0:T(8,128)(2,1)S(1)}, s16[1040,128]{1,0:T(8,128)(2,1)S(1)}) custom-call(s32[12]{0:T(128)S(1)} %pad_add_fusion.facts, bf16[1024,2048]{1,0:T(8,128)(2,1)S(1)} %bitcast_multiply_fusion.a_ref, bf16[2048,128]{1,0:T(8,128)(2,1)S(1)} %copy-done, bf16[2048,128]{1,0:T(8,128)(2,1)S(1)} %collective-permute-done.refs_1_, ...), custom_call_target="tpu_custom_call" | custom-call | flops 3000000000 | bytes 9000000 | tf_op jit(solution)/shard_map/pallas_call | solution.py:130
  20.9 0.5 collective-permute-start.5
  21.5 2.2 %shard_map.47.refs_0_ = f32[1024,256]{1,0:T(8,128)S(1)} custom-call(s32[12]{0:T(128)S(1)} %pad_add_fusion.facts, bf16[1024,2048]{1,0:T(8,128)(2,1)S(1)} %bitcast_multiply_fusion.a_ref, bf16[2048,128]{1,0:T(8,128)(2,1)S(1)} %copy-done, bf16[2048,128]{1,0:T(8,128)(2,1)S(1)} %collective-permute-done.refs_1_, ...), custom_call_target="tpu_custom_call" | custom-call | flops 3000000000 | bytes 9000000 | tf_op jit(solution)/shard_map/pallas_call | solution.py:130
  23.7 1.2 %collective-permute-done.7.refs_4_ = bf16[1024,128]{1,0:T(8,128)(2,1)S(1)} collective-permute-done((bf16[1024,128]{1,0:T(8,128)(2,1)S(1)}, bf16[1024,128]{1,0:T(8,128)(2,1)S(1)}, u32[]{:S(2)}, u32[]{:S(2)}) %collective-permute-start.7) | collective-permute-done | bytes 262176 | tf_op jit(solution)/shard_map/ppermute | solution.py:228
  24.9 0.0 collective-permute-done.6.refs_3_
  24.9 0.0 collective-permute-start.8
  24.9 0.5 collective-permute-start.9
  25.4 0.5 collective-permute-start.10
  25.9 4.4 %collective-permute-done.5.refs_1_ = s16[1040,128]{1,0:T(8,128)(2,1)S(1)} collective-permute-done((s16[1040,128]{1,0:T(8,128)(2,1)S(1)}, s16[1040,128]{1,0:T(8,128)(2,1)S(1)}, u32[]{:S(2)}, u32[]{:S(2)}) %collective-permute-start.5) | collective-permute-done | bytes 266272 | tf_op jit(solution)/shard_map/ppermute | solution.py:231
  30.2 0.0 collective-permute-done.8.refs_8_
  30.2 0.0 collective-permute-done.9.refs_9_
  30.2 3.8 %shard_map.48 = (s16[1040,128]{1,0:T(8,128)(2,1)S(1)}, s16[1040,128]{1,0:T(8,128)(2,1)S(1)}, f32[1024,256]{1,0:T(8,128)S(1)}) custom-call(s32[12]{0:T(128)S(1)} %pad_add_fusion.facts, bf16[1024,2048]{1,0:T(8,128)(2,1)S(1)} %bitcast_multiply_fusion.a_ref, bf16[2048,128]{1,0:T(8,128)(2,1)S(1)} %copy-done, bf16[2048,128]{1,0:T(8,128)(2,1)S(1)} %collective-permute-done.refs_1_, ...), custom_call_target="tpu_custom_call" | custom-call | flops 3000000000 | bytes 9000000 | tf_op jit(solution)/shard_map/pallas_call | solution.py:130
  34.1 1.3 %collective-permute-start.11 = (s16[1040,128]{1,0:T(8,128)(2,1)S(1)}, s16[1040,128]{1,0:T(8,128)(2,1)S(1)}, u32[]{:S(2)}, u32[]{:S(2)}) collective-permute-start(s16[1040,128]{1,0:T(8,128)(2,1)S(1)} %get-tuple-element.32), channel_id=1, source_target_pairs={{0,1},{3,2},{2,3},{4,5},{7,6},{6,7},{8,9},{11,10},{12,13},{15,14},... | collective-permute-start | bytes 798728 | tf_op jit(solution)/shard_map/ppermute | solution.py:231
  35.4 1.3 %collective-permute-start.12 = (s16[1040,128]{1,0:T(8,128)(2,1)S(1)}, s16[1040,128]{1,0:T(8,128)(2,1)S(1)}, u32[]{:S(2)}, u32[]{:S(2)}) collective-permute-start(s16[1040,128]{1,0:T(8,128)(2,1)S(1)} %get-tuple-element.33), channel_id=1, source_target_pairs={{0,1},{3,2},{2,3},{4,5},{7,6},{6,7},{8,9},{11,10},{12,13},{15,14},... | collective-permute-start | bytes 798728 | tf_op jit(solution)/shard_map/ppermute | solution.py:231
  36.7 0.0 collective-permute-done.10.refs_2_
  36.7 1.0 %shard_map.49 = s16[1040,256]{1,0:T(8,128)(2,1)S(1)} custom-call(s32[12]{0:T(128)S(1)} %pad_add_fusion.facts, f32[1024,256]{1,0:T(8,128)S(1)} %shard_map.47.refs_0_, s16[1040,128]{1,0:T(8,128)(2,1)S(1)} %collective-permute-done.5.refs_1_, s16[1040,128]{1,0:T(8,128)(2,1)S(1)} %collective-permute-done.10.refs_2_), custom_call_target="tpu_custom_call" | custom-call | flops 3000000000 | bytes 9000000 | tf_op jit(solution)/shard_map/pallas_call | solution.py:181
  37.7 5.6 %collective-permute-start.13 = (s16[1040,256]{1,0:T(8,128)(2,1)S(1)}, s16[1040,256]{1,0:T(8,128)(2,1)S(1)}, u32[]{:S(2)}, u32[]{:S(2)}) collective-permute-start(s16[1040,256]{1,0:T(8,128)(2,1)S(1)} %shard_map.49), channel_id=1, source_target_pairs={{1,2},{2,0},{5,6},{6,4},{9,11},{10,8},{13,15},{14,12},{17,19},{18,... | collective-permute-start | bytes 1597448 | tf_op jit(solution)/shard_map/ppermute | solution.py:231
  43.3 3.7 %shard_map.50 = (s16[1040,256]{1,0:T(8,128)(2,1)S(1)}, f32[1024,256]{1,0:T(8,128)S(1)}) custom-call(s32[12]{0:T(128)S(1)} %pad_add_fusion.facts, bf16[1024,2048]{1,0:T(8,128)(2,1)S(1)} %bitcast_multiply_fusion.a_ref, bf16[2048,128]{1,0:T(8,128)(2,1)S(1)} %copy-done, bf16[2048,128]{1,0:T(8,128)(2,1)S(1)} %collective-permute-done.refs_1_, ...), custom_call_target="tpu_custom_call" | custom-call | flops 3000000000 | bytes 9000000 | tf_op jit(solution)/shard_map/pallas_call | solution.py:130
  47.1 0.9 %shard_map.51 = s16[1040,128]{1,0:T(8,128)(2,1)S(1)} custom-call(s32[12]{0:T(128)S(1)} %pad_add_fusion.facts, f32[1024,256]{1,0:T(8,128)S(1)} %get-tuple-element.38.refs_0_, s16[1040,128]{1,0:T(8,128)(2,1)S(1)} %collective-permute-done.11.refs_1_.refs_3_), custom_call_target="tpu_custom_call" | custom-call | flops 3000000000 | bytes 9000000 | tf_op jit(solution)/shard_map/pallas_call | solution.py:181
  47.9 2.3 %collective-permute-start.15 = (s16[1040,128]{1,0:T(8,128)(2,1)S(1)}, s16[1040,128]{1,0:T(8,128)(2,1)S(1)}, u32[]{:S(2)}, u32[]{:S(2)}) collective-permute-start(s16[1040,128]{1,0:T(8,128)(2,1)S(1)} %shard_map.51), channel_id=1, source_target_pairs={{1,3},{2,1},{5,7},{6,5},{9,10},{10,9},{13,14},{14,13},{17,18},{18,... | collective-permute-start | bytes 798728 | tf_op jit(solution)/shard_map/ppermute | solution.py:231
  50.3 1.3 %collective-permute-start.14 = (s16[1040,256]{1,0:T(8,128)(2,1)S(1)}, s16[1040,256]{1,0:T(8,128)(2,1)S(1)}, u32[]{:S(2)}, u32[]{:S(2)}) collective-permute-start(s16[1040,256]{1,0:T(8,128)(2,1)S(1)} %get-tuple-element.42), channel_id=1, source_target_pairs={{0,1},{3,2},{4,5},{7,6},{8,9},{11,10},{12,13},{15,14},{16,17},{19,... | collective-permute-start | bytes 1597448 | tf_op jit(solution)/shard_map/ppermute | solution.py:231
  51.6 0.0 collective-permute-done.12.refs_1_.refs_4_
  51.6 0.9 %shard_map.52 = s16[1040,128]{1,0:T(8,128)(2,1)S(1)} custom-call(s32[12]{0:T(128)S(1)} %pad_add_fusion.facts, f32[1024,256]{1,0:T(8,128)S(1)} %get-tuple-element.38.refs_0_, s16[1040,128]{1,0:T(8,128)(2,1)S(1)} %collective-permute-done.12.refs_1_.refs_4_), custom_call_target="tpu_custom_call" | custom-call | flops 3000000000 | bytes 9000000 | tf_op jit(solution)/shard_map/pallas_call | solution.py:181
  52.5 3.5 %collective-permute-start.16 = (s16[1040,128]{1,0:T(8,128)(2,1)S(1)}, s16[1040,128]{1,0:T(8,128)(2,1)S(1)}, u32[]{:S(2)}, u32[]{:S(2)}) collective-permute-start(s16[1040,128]{1,0:T(8,128)(2,1)S(1)} %shard_map.52), channel_id=1, source_target_pairs={{1,3},{2,1},{5,7},{6,5},{9,10},{10,9},{13,14},{14,13},{17,18},{18,... | collective-permute-start | bytes 798728 | tf_op jit(solution)/shard_map/ppermute | solution.py:231
  56.0 0.0 collective-permute-done.13.refs_5_
  56.0 1.1 %shard_map.53.refs_0_ = f32[1024,256]{1,0:T(8,128)S(1)} custom-call(s32[12]{0:T(128)S(1)} %pad_add_fusion.facts, f32[1024,256]{1,0:T(8,128)S(1)} %get-tuple-element.41.refs_0_, s16[1040,128]{1,0:T(8,128)(2,1)S(1)} %collective-permute-done.5.refs_1_, s16[1040,128]{1,0:T(8,128)(2,1)S(1)} %collective-permute-done.10.refs_2_, ...), custom_call_target="tpu_custom_call" | custom-call | flops 3000000000 | bytes 9000000 | tf_op jit(solution)/shard_map/pallas_call | solution.py:181
  57.1 5.4 %collective-permute-done.15.refs_2_ = s16[1040,128]{1,0:T(8,128)(2,1)S(1)} collective-permute-done((s16[1040,128]{1,0:T(8,128)(2,1)S(1)}, s16[1040,128]{1,0:T(8,128)(2,1)S(1)}, u32[]{:S(2)}, u32[]{:S(2)}) %collective-permute-start.15) | collective-permute-done | bytes 266272 | tf_op jit(solution)/shard_map/ppermute | solution.py:231
  62.4 2.9 %collective-permute-done.16.refs_3_ = s16[1040,128]{1,0:T(8,128)(2,1)S(1)} collective-permute-done((s16[1040,128]{1,0:T(8,128)(2,1)S(1)}, s16[1040,128]{1,0:T(8,128)(2,1)S(1)}, u32[]{:S(2)}, u32[]{:S(2)}) %collective-permute-start.16) | collective-permute-done | bytes 266272 | tf_op jit(solution)/shard_map/ppermute | solution.py:231
  65.3 0.0 collective-permute-done.14.refs_1_
  65.3 1.7 %shard_map.54 = bf16[1024,256]{1,0:T(8,128)(2,1)} custom-call(s32[12]{0:T(128)S(1)} %pad_add_fusion.facts, f32[1024,256]{1,0:T(8,128)S(1)} %shard_map.53.refs_0_, s16[1040,256]{1,0:T(8,128)(2,1)S(1)} %collective-permute-done.14.refs_1_, s16[1040,128]{1,0:T(8,128)(2,1)S(1)} %collective-permute-done.15.refs_2_, ...), custom_call_target="tpu_custom_call" | custom-call | flops 3000000000 | bytes 9000000 | tf_op jit(solution)/shard_map/pallas_call | solution.py:181
  (6 shorter events, 0.0 us)
Async XLA Ops:
  0.0 17.5 %collective-permute-start.2 = (bf16[2048,128]{1,0:T(8,128)(2,1)}, bf16[2048,128]{1,0:T(8,128)(2,1)S(1)}, u32[]{:S(2)}, u32[]{:S(2)}) collective-permute-start(bf16[2048,128]{1,0:T(8,128)(2,1)} %refs_0_.7), channel_id=1, source_target_pairs={{0,4},{4,0},{8,12},{12,8},{16,20},{20,16},{24,28},{28,24},{1,5},{5... | collective-permute-start | bytes 1572872 | tf_op jit(solution)/shard_map/ppermute | solution.py:228
  0.0 14.5 %collective-permute-start.1 = (bf16[2048,128]{1,0:T(8,128)(2,1)}, bf16[2048,128]{1,0:T(8,128)(2,1)S(1)}, u32[]{:S(2)}, u32[]{:S(2)}) collective-permute-start(bf16[2048,128]{1,0:T(8,128)(2,1)} %refs_0_.7), channel_id=1, source_target_pairs={{0,16},{4,20},{8,24},{12,28},{16,0},{20,4},{24,8},{28,12},{1,17},{... | collective-permute-start | bytes 1572872 | tf_op jit(solution)/shard_map/ppermute | solution.py:228
  1.5 14.3 %collective-permute-start = (bf16[2048,128]{1,0:T(8,128)(2,1)}, bf16[2048,128]{1,0:T(8,128)(2,1)S(1)}, u32[]{:S(2)}, u32[]{:S(2)}) collective-permute-start(bf16[2048,128]{1,0:T(8,128)(2,1)} %refs_0_.7), channel_id=1, source_target_pairs={{0,8},{4,12},{8,0},{12,4},{16,24},{20,28},{24,16},{28,20},{1,9},{5... | collective-permute-start | bytes 1572872 | tf_op jit(solution)/shard_map/ppermute | solution.py:228
  2.7 2.2 %copy-start.1 = (bf16[1024,2048]{1,0:T(8,128)(2,1)S(1)}, bf16[1024,2048]{1,0:T(8,128)(2,1)}, u32[]{:S(2)}) copy-start(bf16[1024,2048]{1,0:T(8,128)(2,1)} %param.4) | copy-start | bytes 12582916
  5.0 13.5 %copy-start = (bf16[2048,128]{1,0:T(8,128)(2,1)S(1)}, bf16[2048,128]{1,0:T(8,128)(2,1)}, u32[]{:S(2)}) copy-start(bf16[2048,128]{1,0:T(8,128)(2,1)} %refs_0_.7) | copy-start | bytes 1572868
  15.8 1.9 %collective-permute-start.3 = (bf16[2048,128]{1,0:T(8,128)(2,1)S(1)}, bf16[2048,128]{1,0:T(8,128)(2,1)S(1)}, u32[]{:S(2)}, u32[]{:S(2)}) collective-permute-start(bf16[2048,128]{1,0:T(8,128)(2,1)S(1)} %collective-permute-done.refs_1_), channel_id=1, source_target_pairs={{0,4},{4,0},{8,12},{12,8},{16,20},{20,16},{24,28},{28,24},{1,5},{5... | collective-permute-start | bytes 1572872 | tf_op jit(solution)/shard_map/ppermute | solution.py:228
  15.8 2.7 %collective-permute-start.4 = (bf16[2048,128]{1,0:T(8,128)(2,1)S(1)}, bf16[2048,128]{1,0:T(8,128)(2,1)S(1)}, u32[]{:S(2)}, u32[]{:S(2)}) collective-permute-start(bf16[2048,128]{1,0:T(8,128)(2,1)S(1)} %collective-permute-done.1.refs_2_), channel_id=1, source_target_pairs={{0,4},{4,0},{8,12},{12,8},{16,20},{20,16},{24,28},{28,24},{1,5},{5... | collective-permute-start | bytes 1572872 | tf_op jit(solution)/shard_map/ppermute | solution.py:228
  16.4 8.5 %collective-permute-start.6 = (bf16[1024,128]{1,0:T(8,128)(2,1)S(1)}, bf16[1024,128]{1,0:T(8,128)(2,1)S(1)}, u32[]{:S(2)}, u32[]{:S(2)}) collective-permute-start(bf16[1024,128]{1,0:T(8,128)(2,1)S(1)} %slice.6), channel_id=1, source_target_pairs={{0,8},{4,12},{8,0},{12,4},{16,24},{20,28},{24,16},{28,20},{1,9},{5... | collective-permute-start | bytes 786440 | tf_op jit(solution)/shard_map/ppermute | solution.py:228
  17.0 7.9 %collective-permute-start.7 = (bf16[1024,128]{1,0:T(8,128)(2,1)S(1)}, bf16[1024,128]{1,0:T(8,128)(2,1)S(1)}, u32[]{:S(2)}, u32[]{:S(2)}) collective-permute-start(bf16[1024,128]{1,0:T(8,128)(2,1)S(1)} %slice.7), channel_id=1, source_target_pairs={{0,16},{4,20},{8,24},{12,28},{16,0},{20,4},{24,8},{28,12},{1,17},{... | collective-permute-start | bytes 786440 | tf_op jit(solution)/shard_map/ppermute | solution.py:228
  20.9 9.3 %collective-permute-start.5 = (s16[1040,128]{1,0:T(8,128)(2,1)S(1)}, s16[1040,128]{1,0:T(8,128)(2,1)S(1)}, u32[]{:S(2)}, u32[]{:S(2)}) collective-permute-start(s16[1040,128]{1,0:T(8,128)(2,1)S(1)} %get-tuple-element.28), channel_id=1, source_target_pairs={{0,1},{1,0},{2,3},{3,2},{4,5},{5,4},{6,7},{7,6},{8,9},{9,8},{10,11... | collective-permute-start | bytes 798728 | tf_op jit(solution)/shard_map/ppermute | solution.py:231
  24.9 5.4 %collective-permute-start.8 = (bf16[1024,128]{1,0:T(8,128)(2,1)S(1)}, bf16[1024,128]{1,0:T(8,128)(2,1)S(1)}, u32[]{:S(2)}, u32[]{:S(2)}) collective-permute-start(bf16[1024,128]{1,0:T(8,128)(2,1)S(1)} %collective-permute-done.6.refs_3_), channel_id=1, source_target_pairs={{0,4},{4,0},{8,12},{12,8},{16,20},{20,16},{24,28},{28,24},{1,5},{5... | collective-permute-start | bytes 786440 | tf_op jit(solution)/shard_map/ppermute | solution.py:228
  24.9 5.4 %collective-permute-start.9 = (bf16[1024,128]{1,0:T(8,128)(2,1)S(1)}, bf16[1024,128]{1,0:T(8,128)(2,1)S(1)}, u32[]{:S(2)}, u32[]{:S(2)}) collective-permute-start(bf16[1024,128]{1,0:T(8,128)(2,1)S(1)} %collective-permute-done.7.refs_4_), channel_id=1, source_target_pairs={{0,4},{4,0},{8,12},{12,8},{16,20},{20,16},{24,28},{28,24},{1,5},{5... | collective-permute-start | bytes 786440 | tf_op jit(solution)/shard_map/ppermute | solution.py:228
  25.4 11.3 %collective-permute-start.10 = (s16[1040,128]{1,0:T(8,128)(2,1)S(1)}, s16[1040,128]{1,0:T(8,128)(2,1)S(1)}, u32[]{:S(2)}, u32[]{:S(2)}) collective-permute-start(s16[1040,128]{1,0:T(8,128)(2,1)S(1)} %get-tuple-element.26), channel_id=1, source_target_pairs={{0,1},{1,0},{2,3},{3,2},{4,5},{5,4},{6,7},{7,6},{8,9},{9,8},{10,11... | collective-permute-start | bytes 798728 | tf_op jit(solution)/shard_map/ppermute | solution.py:231
  34.1 13.0 %collective-permute-start.11 = (s16[1040,128]{1,0:T(8,128)(2,1)S(1)}, s16[1040,128]{1,0:T(8,128)(2,1)S(1)}, u32[]{:S(2)}, u32[]{:S(2)}) collective-permute-start(s16[1040,128]{1,0:T(8,128)(2,1)S(1)} %get-tuple-element.32), channel_id=1, source_target_pairs={{0,1},{3,2},{2,3},{4,5},{7,6},{6,7},{8,9},{11,10},{12,13},{15,14},... | collective-permute-start | bytes 798728 | tf_op jit(solution)/shard_map/ppermute | solution.py:231
  35.4 16.2 %collective-permute-start.12 = (s16[1040,128]{1,0:T(8,128)(2,1)S(1)}, s16[1040,128]{1,0:T(8,128)(2,1)S(1)}, u32[]{:S(2)}, u32[]{:S(2)}) collective-permute-start(s16[1040,128]{1,0:T(8,128)(2,1)S(1)} %get-tuple-element.33), channel_id=1, source_target_pairs={{0,1},{3,2},{2,3},{4,5},{7,6},{6,7},{8,9},{11,10},{12,13},{15,14},... | collective-permute-start | bytes 798728 | tf_op jit(solution)/shard_map/ppermute | solution.py:231
  37.7 18.3 %collective-permute-start.13 = (s16[1040,256]{1,0:T(8,128)(2,1)S(1)}, s16[1040,256]{1,0:T(8,128)(2,1)S(1)}, u32[]{:S(2)}, u32[]{:S(2)}) collective-permute-start(s16[1040,256]{1,0:T(8,128)(2,1)S(1)} %shard_map.49), channel_id=1, source_target_pairs={{1,2},{2,0},{5,6},{6,4},{9,11},{10,8},{13,15},{14,12},{17,19},{18,... | collective-permute-start | bytes 1597448 | tf_op jit(solution)/shard_map/ppermute | solution.py:231
  47.9 14.5 %collective-permute-start.15 = (s16[1040,128]{1,0:T(8,128)(2,1)S(1)}, s16[1040,128]{1,0:T(8,128)(2,1)S(1)}, u32[]{:S(2)}, u32[]{:S(2)}) collective-permute-start(s16[1040,128]{1,0:T(8,128)(2,1)S(1)} %shard_map.51), channel_id=1, source_target_pairs={{1,3},{2,1},{5,7},{6,5},{9,10},{10,9},{13,14},{14,13},{17,18},{18,... | collective-permute-start | bytes 798728 | tf_op jit(solution)/shard_map/ppermute | solution.py:231
  50.3 15.0 %collective-permute-start.14 = (s16[1040,256]{1,0:T(8,128)(2,1)S(1)}, s16[1040,256]{1,0:T(8,128)(2,1)S(1)}, u32[]{:S(2)}, u32[]{:S(2)}) collective-permute-start(s16[1040,256]{1,0:T(8,128)(2,1)S(1)} %get-tuple-element.42), channel_id=1, source_target_pairs={{0,1},{3,2},{4,5},{7,6},{8,9},{11,10},{12,13},{15,14},{16,17},{19,... | collective-permute-start | bytes 1597448 | tf_op jit(solution)/shard_map/ppermute | solution.py:231
  52.5 12.9 %collective-permute-start.16 = (s16[1040,128]{1,0:T(8,128)(2,1)S(1)}, s16[1040,128]{1,0:T(8,128)(2,1)S(1)}, u32[]{:S(2)}, u32[]{:S(2)}) collective-permute-start(s16[1040,128]{1,0:T(8,128)(2,1)S(1)} %shard_map.52), channel_id=1, source_target_pairs={{1,3},{2,1},{5,7},{6,5},{9,10},{10,9},{13,14},{14,13},{17,18},{18,... | collective-permute-start | bytes 798728 | tf_op jit(solution)/shard_map/ppermute | solution.py:231

commit v2 on v0

--- a/solution.py
+++ b/solution.py
@@ -197,17 +197,16 @@
     late = chip == (0 if at < 2 else 3)
     passed = (near, far) if late else (far, near)
     home = 0 if at < 2 else 3
+    early = chip != (3 if at < 2 else 0)
     if end:
-        first, second, third, relayed = passed[0], passed[1], 3 - near, (chip, chip)
+        first, second, third, relayed = passed[0], passed[1], 3 - near, chip
     else:
-        straight = chip ^ home != 3
-        first, second = (home, chip) if straight else (chip, home)
-        third, relayed = chip, passed
-    early = chip != (3 if at < 2 else 0)
-    return (first, second, third, *relayed, at, 1, int(end and early), int(end and not early), int(not end))
-
-
-FIRST, SECOND, THIRD, RELAY_ONE, RELAY_TWO, HERE, ALWAYS, EARLY, LATE, INNER, CORE, CHIP = range(12)
+        first, second = home if early else chip, passed[1]
+        third, relayed = chip if early else home, passed[0]
+    return (first, second, third, relayed, at, 1, int(end and early), int(not (end and early)))
+
+
+FIRST, SECOND, THIRD, RELAY, HERE, ALWAYS, EARLY, OTHERS, CORE, CHIP = range(10)
 
 
 def line_pairs(choose):
@@ -233,14 +232,17 @@
 
     inward = [(0, 1), (3, 2)]
 
-    def second_pairs(p):
+    def straight_pairs(p):
+        return [(0, 3 if p == 0 else 2), (3, 0 if p == 3 else 1)]
+
+    def share_pairs(p):
+        return [(1, 3 if p == 0 else 2), (2, 0 if p == 3 else 1)]
+
+    def relay_pairs(p):
+        return [(1, 2 if p == 0 else 3), (2, 1 if p == 3 else 0)]
+
+    def third_pairs(p):
         return inward + [(1, 0)] * (p == 3) + [(2, 3)] * (p == 0)
-
-    def relay_one(p):
-        return [(1, 2 if p == 0 else 3), (2, 1 if p == 3 else 0)]
-
-    def relay_two(p):
-        return [(1, 3 if p == 0 else 2), (2, 0 if p == 3 else 1)]
 
     by_x, by_y, twin = across(integrals, 2), across(integrals, 4), across(integrals, 1)
     plans = jnp.asarray([plan_of(p, z) for p in range(4) for z in range(4)], jnp.int32)
@@ -254,25 +256,22 @@
     coded, plain = ("coded",), ("plain",)
     out_left, out_right = multiply(facts, masked, straight, (FIRST,), (("left", "right"),))
     one = along(out_left, pairs), along(out_right, pairs)
-    (share_one,) = multiply(after(facts, out_right), masked, straight, (RELAY_ONE,), (plain,))
+    (share_one,) = multiply(after(facts, out_right), masked, straight, (RELAY,), (plain,))
     columns = (*straight[:3], by_both, *straight[3:], tuple(across(after(x, share_one), 1) for x in by_both))
     (out_two,) = multiply(after(facts, share_one, one[0]), masked, columns, (SECOND,), (coded,))
-    two = along(out_two, second_pairs)
-    out_relay_one = add(after(facts, out_two), [(share_one, ALWAYS), (one, ALWAYS)])
-    relayed_one = along(out_relay_one, relay_one)
-    out_three, share_two = multiply(
-        after(facts, out_relay_one), masked, columns, (THIRD, RELAY_TWO), (coded, plain)
-    )
-    three = along(out_three, lambda p: inward)
-    out_relay_two = add(after(facts, out_three), [(share_two, ALWAYS), (two, ALWAYS)])
-    relayed_two = along(out_relay_two, relay_two)
-    (own,) = multiply(after(facts, out_relay_two), masked, columns, (HERE,), (plain,))
+    two = along(out_two, straight_pairs)
+    shared = along(out_two, share_pairs)
+    out_relay = add(after(facts, out_two), [(share_one, ALWAYS), (one, ALWAYS)])
+    relayed = along(out_relay, relay_pairs)
+    (out_three,) = multiply(after(facts, out_relay), masked, columns, (THIRD,), (coded,))
+    three = along(out_three, third_pairs)
+    (own,) = multiply(after(facts, out_three, two, shared), masked, columns, (HERE,), (plain,))
     most = add(
         facts,
-        [(own, ALWAYS), (one, EARLY), (two, LATE), (relayed_one, ALWAYS)],
+        [(own, ALWAYS), (one, EARLY), (two, ALWAYS), (shared, ALWAYS), (relayed, ALWAYS)],
         jnp.float32,
     )
-    return add(facts, [(most, ALWAYS), (three, INNER), (relayed_two, ALWAYS)], jnp.bfloat16)
+    return add(facts, [(most, ALWAYS), (three, OTHERS)], jnp.bfloat16)
 
 
 def solution(mesh):

time: 65.6 us -> 74.6 us (1.14)
  the two profiles are of different devices: /device:TPU:10 before, /device:TPU:0 now
where the time goes in v2:
time: 74.6 us; the launch traced here: 74.3 us
  waiting for transfers between devices  32.5 us (44%)
  starting transfers between devices  21.7 us (29%)
  Pallas kernels  15.4 us (21%)
  local copies, waits for them, and re-layouts  2.83 us (4%)
  other arithmetic  1.67 us (2%)
    ppermute x6, waiting for transfers between devices, along(): return lax.ppermute(block, ('row', 'col'), line_pairs(choose))  23.8 us
    ppermute x6, starting transfers between devices, along(): return lax.ppermute(block, ('row', 'col'), line_pairs(choose))  14.8 us
    pallas_call x5, Pallas kernels, multiply(): pl.pallas_call(functools.partial(multiply_kernel, slots, kinds, rows, wid...  11.7 us
    ppermute x9, waiting for transfers between devices, across(): return lax.ppermute(block, 'row', [(i, i ^ bit) for i in range(8)])  8.78 us
    ppermute x9, starting transfers between devices, across(): return lax.ppermute(block, 'row', [(i, i ^ bit) for i in range(8)])  6.91 us
    pallas_call x3, Pallas kernels, add(): pl.pallas_call(functools.partial(add_kernel, tuple(((weight, len(x)) for...  3.72 us
    unnamed x4, local copies, waits for them, and re-layouts  1.5 us
  transfers between devices with their start and end apart: 15, of which 6 were waited for; matrix products, arithmetic and copies ran while one was open for 4% of the time, Pallas kernels for 19%

profile of v2, /device:TPU:0, one launch (start us, length us, event | category | flops | bytes accessed | tf_op | source)
XLA Modules:
  0.0 74.3 jit_solution(12958541405374882724)
XLA Ops:
  0.0 2.9 %collective-permute-start = (bf16[2048,128]{1,0:T(8,128)(2,1)}, bf16[2048,128]{1,0:T(8,128)(2,1)S(1)}, u32[]{:S(2)}, u32[]{:S(2)}) collective-permute-start(bf16[2048,128]{1,0:T(8,128)(2,1)} %refs_0_.9), channel_id=1, source_target_pairs={{0,8},{4,12},{8,0},{12,4},{16,24},{20,28},{24,16},{28,20},{1,9},{5... | collective-permute-start | bytes 1572872 | tf_op jit(solution)/shard_map/ppermute | solution.py:225
  2.9 1.5 %collective-permute-start.1 = (bf16[2048,128]{1,0:T(8,128)(2,1)}, bf16[2048,128]{1,0:T(8,128)(2,1)S(1)}, u32[]{:S(2)}, u32[]{:S(2)}) collective-permute-start(bf16[2048,128]{1,0:T(8,128)(2,1)} %refs_0_.9), channel_id=1, source_target_pairs={{0,16},{4,20},{8,24},{12,28},{16,0},{20,4},{24,8},{28,12},{1,17},{... | collective-permute-start | bytes 1572872 | tf_op jit(solution)/shard_map/ppermute | solution.py:225
  4.5 0.0 collective-permute-start.2
  4.5 0.7 convert_element_type.3
  5.2 0.7 dynamic-slice_bitcast_fusion
  5.8 0.0 copy-start.1
  5.8 0.1 pad_add_fusion.facts
  5.9 0.6 mul.15
  6.5 1.5 %copy-done.1 = bf16[1024,2048]{1,0:T(8,128)(2,1)S(1)} copy-done((bf16[1024,2048]{1,0:T(8,128)(2,1)S(1)}, bf16[1024,2048]{1,0:T(8,128)(2,1)}, u32[]{:S(2)}) %copy-start.1) | copy-done | bytes 4194328
  8.0 0.0 copy-start
  8.0 0.9 %bitcast_multiply_fusion.a_ref = bf16[1024,2048]{1,0:T(8,128)(2,1)S(1)} fusion(bf16[1024,2048]{1,0:T(8,128)(2,1)S(1)} %copy-done.1, bf16[128,8,16,128]{3,2,1,0:T(8,128)(2,1)S(1)} %bitcast.8), kind=kLoop, calls=%fused_computation | loop fusion | flops 2097152 | bytes 12582912 | tf_op jit(solution)/shard_map/mul | solution.py:24
  8.9 6.1 %collective-permute-done.refs_1_ = bf16[2048,128]{1,0:T(8,128)(2,1)S(1)} collective-permute-done((bf16[2048,128]{1,0:T(8,128)(2,1)}, bf16[2048,128]{1,0:T(8,128)(2,1)S(1)}, u32[]{:S(2)}, u32[]{:S(2)}) %collective-permute-start) | collective-permute-done | bytes 524320 | tf_op jit(solution)/shard_map/ppermute | solution.py:225
  15.1 0.0 collective-permute-start.3
  15.1 1.5 %collective-permute-done.1.refs_2_ = bf16[2048,128]{1,0:T(8,128)(2,1)S(1)} collective-permute-done((bf16[2048,128]{1,0:T(8,128)(2,1)}, bf16[2048,128]{1,0:T(8,128)(2,1)S(1)}, u32[]{:S(2)}, u32[]{:S(2)}) %collective-permute-start.1) | collective-permute-done | bytes 524320 | tf_op jit(solution)/shard_map/ppermute | solution.py:225
  16.5 0.0 collective-permute-start.4
  16.6 1.6 %collective-permute-start.7 = (bf16[1024,128]{1,0:T(8,128)(2,1)S(1)}, bf16[1024,128]{1,0:T(8,128)(2,1)S(1)}, u32[]{:S(2)}, u32[]{:S(2)}) collective-permute-start(bf16[1024,128]{1,0:T(8,128)(2,1)S(1)} %slice.7), channel_id=1, source_target_pairs={{0,16},{4,20},{8,24},{12,28},{16,0},{20,4},{24,8},{28,12},{1,17},{... | collective-permute-start | bytes 786440 | tf_op jit(solution)/shard_map/ppermute | solution.py:225
  18.2 0.8 %collective-permute-start.6 = (bf16[1024,128]{1,0:T(8,128)(2,1)S(1)}, bf16[1024,128]{1,0:T(8,128)(2,1)S(1)}, u32[]{:S(2)}, u32[]{:S(2)}) collective-permute-start(bf16[1024,128]{1,0:T(8,128)(2,1)S(1)} %slice.6), channel_id=1, source_target_pairs={{0,8},{4,12},{8,0},{12,4},{16,24},{20,28},{24,16},{28,20},{1,9},{5... | collective-permute-start | bytes 786440 | tf_op jit(solution)/shard_map/ppermute | solution.py:225
  19.0 0.0 collective-permute-done.2.refs_3_.refs_5_
  19.0 0.0 collective-permute-done.3.refs_4_.refs_6_
  19.0 0.0 collective-permute-done.4.refs_5_.refs_7_
  19.0 0.0 copy-done
  19.0 2.5 %shard_map.46 = (s16[1040,128]{1,0:T(8,128)(2,1)S(1)}, s16[1040,128]{1,0:T(8,128)(2,1)S(1)}) custom-call(s32[10]{0:T(128)S(1)} %pad_add_fusion.facts, bf16[1024,2048]{1,0:T(8,128)(2,1)S(1)} %bitcast_multiply_fusion.a_ref, bf16[2048,128]{1,0:T(8,128)(2,1)S(1)} %copy-done, bf16[2048,128]{1,0:T(8,128)(2,1)S(1)} %collective-permute-done.refs_1_, ...), custom_call_target="tpu_custom_call" | custom-call | flops 3000000000 | bytes 9000000 | tf_op jit(solution)/shard_map/pallas_call | solution.py:130
  21.5 1.6 %collective-permute-start.5 = (s16[1040,128]{1,0:T(8,128)(2,1)S(1)}, s16[1040,128]{1,0:T(8,128)(2,1)S(1)}, u32[]{:S(2)}, u32[]{:S(2)}) collective-permute-start(s16[1040,128]{1,0:T(8,128)(2,1)S(1)} %get-tuple-element.20), channel_id=1, source_target_pairs={{0,1},{1,0},{2,3},{3,2},{4,5},{5,4},{6,7},{7,6},{8,9},{9,8},{10,11... | collective-permute-start | bytes 798728 | tf_op jit(solution)/shard_map/ppermute | solution.py:228
  23.1 2.2 %shard_map.47.refs_0_ = f32[1024,256]{1,0:T(8,128)S(1)} custom-call(s32[10]{0:T(128)S(1)} %pad_add_fusion.facts, bf16[1024,2048]{1,0:T(8,128)(2,1)S(1)} %bitcast_multiply_fusion.a_ref, bf16[2048,128]{1,0:T(8,128)(2,1)S(1)} %copy-done, bf16[2048,128]{1,0:T(8,128)(2,1)S(1)} %collective-permute-done.refs_1_, ...), custom_call_target="tpu_custom_call" | custom-call | flops 3000000000 | bytes 9000000 | tf_op jit(solution)/shard_map/pallas_call | solution.py:130
  25.4 0.0 collective-permute-done.7.refs_4_
  25.4 0.1 collective-permute-start.9
  25.4 1.2 %collective-permute-done.6.refs_3_ = bf16[1024,128]{1,0:T(8,128)(2,1)S(1)} collective-permute-done((bf16[1024,128]{1,0:T(8,128)(2,1)S(1)}, bf16[1024,128]{1,0:T(8,128)(2,1)S(1)}, u32[]{:S(2)}, u32[]{:S(2)}) %collective-permute-start.6) | collective-permute-done | bytes 262176 | tf_op jit(solution)/shard_map/ppermute | solution.py:225
  26.6 0.0 collective-permute-start.8
  26.6 1.6 %collective-permute-start.10 = (s16[1040,128]{1,0:T(8,128)(2,1)S(1)}, s16[1040,128]{1,0:T(8,128)(2,1)S(1)}, u32[]{:S(2)}, u32[]{:S(2)}) collective-permute-start(s16[1040,128]{1,0:T(8,128)(2,1)S(1)} %get-tuple-element.18), channel_id=1, source_target_pairs={{0,1},{1,0},{2,3},{3,2},{4,5},{5,4},{6,7},{7,6},{8,9},{9,8},{10,11... | collective-permute-start | bytes 798728 | tf_op jit(solution)/shard_map/ppermute | solution.py:228
  28.2 1.3 %collective-permute-done.5.refs_1_ = s16[1040,128]{1,0:T(8,128)(2,1)S(1)} collective-permute-done((s16[1040,128]{1,0:T(8,128)(2,1)S(1)}, s16[1040,128]{1,0:T(8,128)(2,1)S(1)}, u32[]{:S(2)}, u32[]{:S(2)}) %collective-permute-start.5) | collective-permute-done | bytes 266272 | tf_op jit(solution)/shard_map/ppermute | solution.py:228
  29.5 0.0 collective-permute-done.9.refs_9_
  29.5 0.0 collective-permute-done.8.refs_8_
  29.5 2.4 %shard_map.48 = s16[1040,256]{1,0:T(8,128)(2,1)S(1)} custom-call(s32[10]{0:T(128)S(1)} %pad_add_fusion.facts, bf16[1024,2048]{1,0:T(8,128)(2,1)S(1)} %bitcast_multiply_fusion.a_ref, bf16[2048,128]{1,0:T(8,128)(2,1)S(1)} %copy-done, bf16[2048,128]{1,0:T(8,128)(2,1)S(1)} %collective-permute-done.refs_1_, bf16[2048,128]{1,0:T(8,128)(2,1)S(1)} %collective-permute-done.1.refs_2_, ...), custom_call_target="tpu_custom_call" | custom-call | flops 3000000000 | bytes 9000000 | tf_op jit(solution)/shard_map/pallas_call | solution.py:130
  31.9 5.5 %collective-permute-start.11 = (s16[1040,256]{1,0:T(8,128)(2,1)S(1)}, s16[1040,256]{1,0:T(8,128)(2,1)S(1)}, u32[]{:S(2)}, u32[]{:S(2)}) collective-permute-start(s16[1040,256]{1,0:T(8,128)(2,1)S(1)} %shard_map.48), channel_id=1, source_target_pairs={{0,3},{3,1},{4,7},{7,5},{8,10},{11,9},{12,14},{15,13},{16,18},{19,... | collective-permute-start | bytes 1597448 | tf_op jit(solution)/shard_map/ppermute | solution.py:228
  37.5 0.7 collective-permute-start.12
  38.2 0.0 collective-permute-done.10.refs_2_
  38.2 1.0 %shard_map.49 = s16[1040,256]{1,0:T(8,128)(2,1)S(1)} custom-call(s32[10]{0:T(128)S(1)} %pad_add_fusion.facts, f32[1024,256]{1,0:T(8,128)S(1)} %shard_map.47.refs_0_, s16[1040,128]{1,0:T(8,128)(2,1)S(1)} %collective-permute-done.5.refs_1_, s16[1040,128]{1,0:T(8,128)(2,1)S(1)} %collective-permute-done.10.refs_2_), custom_call_target="tpu_custom_call" | custom-call | flops 3000000000 | bytes 9000000 | tf_op jit(solution)/shard_map/pallas_call | solution.py:179
  39.2 1.3 %collective-permute-start.13 = (s16[1040,256]{1,0:T(8,128)(2,1)S(1)}, s16[1040,256]{1,0:T(8,128)(2,1)S(1)}, u32[]{:S(2)}, u32[]{:S(2)}) collective-permute-start(s16[1040,256]{1,0:T(8,128)(2,1)S(1)} %shard_map.49), channel_id=1, source_target_pairs={{1,2},{2,0},{5,6},{6,4},{9,11},{10,8},{13,15},{14,12},{17,19},{18,... | collective-permute-start | bytes 1597448 | tf_op jit(solution)/shard_map/ppermute | solution.py:228
  40.5 2.4 %shard_map.50 = s16[1040,256]{1,0:T(8,128)(2,1)S(1)} custom-call(s32[10]{0:T(128)S(1)} %pad_add_fusion.facts, bf16[1024,2048]{1,0:T(8,128)(2,1)S(1)} %bitcast_multiply_fusion.a_ref, bf16[2048,128]{1,0:T(8,128)(2,1)S(1)} %copy-done, bf16[2048,128]{1,0:T(8,128)(2,1)S(1)} %collective-permute-done.refs_1_, bf16[2048,128]{1,0:T(8,128)(2,1)S(1)} %collective-permute-done.1.refs_2_, ...), custom_call_target="tpu_custom_call" | custom-call | flops 3000000000 | bytes 9000000 | tf_op jit(solution)/shard_map/pallas_call | solution.py:130
  42.9 4.1 %collective-permute-start.14 = (s16[1040,256]{1,0:T(8,128)(2,1)S(1)}, s16[1040,256]{1,0:T(8,128)(2,1)S(1)}, u32[]{:S(2)}, u32[]{:S(2)}) collective-permute-start(s16[1040,256]{1,0:T(8,128)(2,1)S(1)} %shard_map.50), channel_id=1, source_target_pairs={{0,1},{3,2},{2,3},{4,5},{7,6},{6,7},{8,9},{11,10},{12,13},{15,14},... | collective-permute-start | bytes 1597448 | tf_op jit(solution)/shard_map/ppermute | solution.py:228
  46.9 3.1 %collective-permute-done.11.refs_3_ = s16[1040,256]{1,0:T(8,128)(2,1)S(1)} collective-permute-done((s16[1040,256]{1,0:T(8,128)(2,1)S(1)}, s16[1040,256]{1,0:T(8,128)(2,1)S(1)}, u32[]{:S(2)}, u32[]{:S(2)}) %collective-permute-start.11) | collective-permute-done | bytes 532512 | tf_op jit(solution)/shard_map/ppermute | solution.py:228
  50.0 0.0 collective-permute-done.12.refs_4_
  50.0 2.2 %shard_map.51.refs_0_ = f32[1024,256]{1,0:T(8,128)S(1)} custom-call(s32[10]{0:T(128)S(1)} %pad_add_fusion.facts, bf16[1024,2048]{1,0:T(8,128)(2,1)S(1)} %bitcast_multiply_fusion.a_ref, bf16[2048,128]{1,0:T(8,128)(2,1)S(1)} %copy-done, bf16[2048,128]{1,0:T(8,128)(2,1)S(1)} %collective-permute-done.refs_1_, ...), custom_call_target="tpu_custom_call" | custom-call | flops 3000000000 | bytes 9000000 | tf_op jit(solution)/shard_map/pallas_call | solution.py:130
  52.3 19.3 %collective-permute-done.13.refs_5_ = s16[1040,256]{1,0:T(8,128)(2,1)S(1)} collective-permute-done((s16[1040,256]{1,0:T(8,128)(2,1)S(1)}, s16[1040,256]{1,0:T(8,128)(2,1)S(1)}, u32[]{:S(2)}, u32[]{:S(2)}) %collective-permute-start.13) | collective-permute-done | bytes 532512 | tf_op jit(solution)/shard_map/ppermute | solution.py:228
  71.6 1.2 %shard_map.52.refs_0_ = f32[1024,256]{1,0:T(8,128)S(1)} custom-call(s32[10]{0:T(128)S(1)} %pad_add_fusion.facts, f32[1024,256]{1,0:T(8,128)S(1)} %shard_map.51.refs_0_, s16[1040,128]{1,0:T(8,128)(2,1)S(1)} %collective-permute-done.5.refs_1_, s16[1040,128]{1,0:T(8,128)(2,1)S(1)} %collective-permute-done.10.refs_2_, ...), custom_call_target="tpu_custom_call" | custom-call | flops 3000000000 | bytes 9000000 | tf_op jit(solution)/shard_map/pallas_call | solution.py:179
  72.8 0.0 collective-permute-done.14.refs_1_
  72.8 1.5 %shard_map.53 = bf16[1024,256]{1,0:T(8,128)(2,1)} custom-call(s32[10]{0:T(128)S(1)} %pad_add_fusion.facts, f32[1024,256]{1,0:T(8,128)S(1)} %shard_map.52.refs_0_, s16[1040,256]{1,0:T(8,128)(2,1)S(1)} %collective-permute-done.14.refs_1_), custom_call_target="tpu_custom_call" | custom-call | flops 3000000000 | bytes 9000000 | tf_op jit(solution)/shard_map/pallas_call | solution.py:179
  (2 shorter events, 0.0 us)
Async XLA Ops:
  0.0 15.1 %collective-permute-start = (bf16[2048,128]{1,0:T(8,128)(2,1)}, bf16[2048,128]{1,0:T(8,128)(2,1)S(1)}, u32[]{:S(2)}, u32[]{:S(2)}) collective-permute-start(bf16[2048,128]{1,0:T(8,128)(2,1)} %refs_0_.9), channel_id=1, source_target_pairs={{0,8},{4,12},{8,0},{12,4},{16,24},{20,28},{24,16},{28,20},{1,9},{5... | collective-permute-start | bytes 1572872 | tf_op jit(solution)/shard_map/ppermute | solution.py:225
  2.9 13.6 %collective-permute-start.1 = (bf16[2048,128]{1,0:T(8,128)(2,1)}, bf16[2048,128]{1,0:T(8,128)(2,1)S(1)}, u32[]{:S(2)}, u32[]{:S(2)}) collective-permute-start(bf16[2048,128]{1,0:T(8,128)(2,1)} %refs_0_.9), channel_id=1, source_target_pairs={{0,16},{4,20},{8,24},{12,28},{16,0},{20,4},{24,8},{28,12},{1,17},{... | collective-permute-start | bytes 1572872 | tf_op jit(solution)/shard_map/ppermute | solution.py:225
  4.5 14.5 %collective-permute-start.2 = (bf16[2048,128]{1,0:T(8,128)(2,1)}, bf16[2048,128]{1,0:T(8,128)(2,1)S(1)}, u32[]{:S(2)}, u32[]{:S(2)}) collective-permute-start(bf16[2048,128]{1,0:T(8,128)(2,1)} %refs_0_.9), channel_id=1, source_target_pairs={{0,4},{4,0},{8,12},{12,8},{16,20},{20,16},{24,28},{28,24},{1,5},{5... | collective-permute-start | bytes 1572872 | tf_op jit(solution)/shard_map/ppermute | solution.py:225
  5.8 2.2 %copy-start.1 = (bf16[1024,2048]{1,0:T(8,128)(2,1)S(1)}, bf16[1024,2048]{1,0:T(8,128)(2,1)}, u32[]{:S(2)}) copy-start(bf16[1024,2048]{1,0:T(8,128)(2,1)} %param.4) | copy-start | bytes 12582916
  8.0 10.9 %copy-start = (bf16[2048,128]{1,0:T(8,128)(2,1)S(1)}, bf16[2048,128]{1,0:T(8,128)(2,1)}, u32[]{:S(2)}) copy-start(bf16[2048,128]{1,0:T(8,128)(2,1)} %refs_0_.9) | copy-start | bytes 1572868
  15.1 3.9 %collective-permute-start.3 = (bf16[2048,128]{1,0:T(8,128)(2,1)S(1)}, bf16[2048,128]{1,0:T(8,128)(2,1)S(1)}, u32[]{:S(2)}, u32[]{:S(2)}) collective-permute-start(bf16[2048,128]{1,0:T(8,128)(2,1)S(1)} %collective-permute-done.refs_1_), channel_id=1, source_target_pairs={{0,4},{4,0},{8,12},{12,8},{16,20},{20,16},{24,28},{28,24},{1,5},{5... | collective-permute-start | bytes 1572872 | tf_op jit(solution)/shard_map/ppermute | solution.py:225
  16.5 2.4 %collective-permute-start.4 = (bf16[2048,128]{1,0:T(8,128)(2,1)S(1)}, bf16[2048,128]{1,0:T(8,128)(2,1)S(1)}, u32[]{:S(2)}, u32[]{:S(2)}) collective-permute-start(bf16[2048,128]{1,0:T(8,128)(2,1)S(1)} %collective-permute-done.1.refs_2_), channel_id=1, source_target_pairs={{0,4},{4,0},{8,12},{12,8},{16,20},{20,16},{24,28},{28,24},{1,5},{5... | collective-permute-start | bytes 1572872 | tf_op jit(solution)/shard_map/ppermute | solution.py:225
  16.6 8.8 %collective-permute-start.7 = (bf16[1024,128]{1,0:T(8,128)(2,1)S(1)}, bf16[1024,128]{1,0:T(8,128)(2,1)S(1)}, u32[]{:S(2)}, u32[]{:S(2)}) collective-permute-start(bf16[1024,128]{1,0:T(8,128)(2,1)S(1)} %slice.7), channel_id=1, source_target_pairs={{0,16},{4,20},{8,24},{12,28},{16,0},{20,4},{24,8},{28,12},{1,17},{... | collective-permute-start | bytes 786440 | tf_op jit(solution)/shard_map/ppermute | solution.py:225
  18.2 8.4 %collective-permute-start.6 = (bf16[1024,128]{1,0:T(8,128)(2,1)S(1)}, bf16[1024,128]{1,0:T(8,128)(2,1)S(1)}, u32[]{:S(2)}, u32[]{:S(2)}) collective-permute-start(bf16[1024,128]{1,0:T(8,128)(2,1)S(1)} %slice.6), channel_id=1, source_target_pairs={{0,8},{4,12},{8,0},{12,4},{16,24},{20,28},{24,16},{28,20},{1,9},{5... | collective-permute-start | bytes 786440 | tf_op jit(solution)/shard_map/ppermute | solution.py:225
  21.5 8.1 %collective-permute-start.5 = (s16[1040,128]{1,0:T(8,128)(2,1)S(1)}, s16[1040,128]{1,0:T(8,128)(2,1)S(1)}, u32[]{:S(2)}, u32[]{:S(2)}) collective-permute-start(s16[1040,128]{1,0:T(8,128)(2,1)S(1)} %get-tuple-element.20), channel_id=1, source_target_pairs={{0,1},{1,0},{2,3},{3,2},{4,5},{5,4},{6,7},{7,6},{8,9},{9,8},{10,11... | collective-permute-start | bytes 798728 | tf_op jit(solution)/shard_map/ppermute | solution.py:228
  25.4 4.2 %collective-permute-start.9 = (bf16[1024,128]{1,0:T(8,128)(2,1)S(1)}, bf16[1024,128]{1,0:T(8,128)(2,1)S(1)}, u32[]{:S(2)}, u32[]{:S(2)}) collective-permute-start(bf16[1024,128]{1,0:T(8,128)(2,1)S(1)} %collective-permute-done.7.refs_4_), channel_id=1, source_target_pairs={{0,4},{4,0},{8,12},{12,8},{16,20},{20,16},{24,28},{28,24},{1,5},{5... | collective-permute-start | bytes 786440 | tf_op jit(solution)/shard_map/ppermute | solution.py:225
  26.6 2.9 %collective-permute-start.8 = (bf16[1024,128]{1,0:T(8,128)(2,1)S(1)}, bf16[1024,128]{1,0:T(8,128)(2,1)S(1)}, u32[]{:S(2)}, u32[]{:S(2)}) collective-permute-start(bf16[1024,128]{1,0:T(8,128)(2,1)S(1)} %collective-permute-done.6.refs_3_), channel_id=1, source_target_pairs={{0,4},{4,0},{8,12},{12,8},{16,20},{20,16},{24,28},{28,24},{1,5},{5... | collective-permute-start | bytes 786440 | tf_op jit(solution)/shard_map/ppermute | solution.py:225
  26.6 11.6 %collective-permute-start.10 = (s16[1040,128]{1,0:T(8,128)(2,1)S(1)}, s16[1040,128]{1,0:T(8,128)(2,1)S(1)}, u32[]{:S(2)}, u32[]{:S(2)}) collective-permute-start(s16[1040,128]{1,0:T(8,128)(2,1)S(1)} %get-tuple-element.18), channel_id=1, source_target_pairs={{0,1},{1,0},{2,3},{3,2},{4,5},{5,4},{6,7},{7,6},{8,9},{9,8},{10,11... | collective-permute-start | bytes 798728 | tf_op jit(solution)/shard_map/ppermute | solution.py:228
  31.9 18.1 %collective-permute-start.11 = (s16[1040,256]{1,0:T(8,128)(2,1)S(1)}, s16[1040,256]{1,0:T(8,128)(2,1)S(1)}, u32[]{:S(2)}, u32[]{:S(2)}) collective-permute-start(s16[1040,256]{1,0:T(8,128)(2,1)S(1)} %shard_map.48), channel_id=1, source_target_pairs={{0,3},{3,1},{4,7},{7,5},{8,10},{11,9},{12,14},{15,13},{16,18},{19,... | collective-permute-start | bytes 1597448 | tf_op jit(solution)/shard_map/ppermute | solution.py:228
  37.5 12.6 %collective-permute-start.12 = (s16[1040,256]{1,0:T(8,128)(2,1)S(1)}, s16[1040,256]{1,0:T(8,128)(2,1)S(1)}, u32[]{:S(2)}, u32[]{:S(2)}) collective-permute-start(s16[1040,256]{1,0:T(8,128)(2,1)S(1)} %shard_map.48), channel_id=1, source_target_pairs={{1,3},{2,1},{5,7},{6,5},{9,10},{10,9},{13,14},{14,13},{17,18},{18,... | collective-permute-start | bytes 1597448 | tf_op jit(solution)/shard_map/ppermute | solution.py:228
  39.2 32.4 %collective-permute-start.13 = (s16[1040,256]{1,0:T(8,128)(2,1)S(1)}, s16[1040,256]{1,0:T(8,128)(2,1)S(1)}, u32[]{:S(2)}, u32[]{:S(2)}) collective-permute-start(s16[1040,256]{1,0:T(8,128)(2,1)S(1)} %shard_map.49), channel_id=1, source_target_pairs={{1,2},{2,0},{5,6},{6,4},{9,11},{10,8},{13,15},{14,12},{17,19},{18,... | collective-permute-start | bytes 1597448 | tf_op jit(solution)/shard_map/ppermute | solution.py:228
  42.9 30.0 %collective-permute-start.14 = (s16[1040,256]{1,0:T(8,128)(2,1)S(1)}, s16[1040,256]{1,0:T(8,128)(2,1)S(1)}, u32[]{:S(2)}, u32[]{:S(2)}) collective-permute-start(s16[1040,256]{1,0:T(8,128)(2,1)S(1)} %shard_map.50), channel_id=1, source_target_pairs={{0,1},{3,2},{2,3},{4,5},{7,6},{6,7},{8,9},{11,10},{12,13},{15,14},... | collective-permute-start | bytes 1597448 | tf_op jit(solution)/shard_map/ppermute | solution.py:228

commit v3 on v0

--- a/solution.py
+++ b/solution.py
@@ -242,10 +242,11 @@
     def relay_two(p):
         return [(1, 3 if p == 0 else 2), (2, 0 if p == 3 else 1)]
 
-    by_x, by_y, twin = across(integrals, 2), across(integrals, 4), across(integrals, 1)
+    by_x, by_y = across(integrals, 2), across(integrals, 4)
     plans = jnp.asarray([plan_of(p, z) for p in range(4) for z in range(4)], jnp.int32)
     planned = lax.dynamic_slice_in_dim(plans, chip * 4 + at, 1)[0]
     facts = jnp.concatenate([planned, jnp.stack([core, chip]).astype(jnp.int32)])
+    twin = across(after(integrals, facts), 1)
     masked = apply_mask(amplitudes, tile_mask)
     by_x, by_y = after(by_x, masked, facts), after(by_y, masked, facts)
     half = integrals.shape[0] // 2
@@ -258,12 +259,12 @@
     columns = (*straight[:3], by_both, *straight[3:], tuple(across(after(x, share_one), 1) for x in by_both))
     (out_two,) = multiply(after(facts, share_one, one[0]), masked, columns, (SECOND,), (coded,))
     two = along(out_two, second_pairs)
-    out_relay_one = add(after(facts, out_two), [(share_one, ALWAYS), (one, ALWAYS)])
+    out_three, share_two = multiply(
+        after(facts, out_two), masked, columns, (THIRD, RELAY_TWO), (coded, plain)
+    )
+    out_relay_one = add(after(facts, out_three), [(share_one, ALWAYS), (one, ALWAYS)])
     relayed_one = along(out_relay_one, relay_one)
-    out_three, share_two = multiply(
-        after(facts, out_relay_one), masked, columns, (THIRD, RELAY_TWO), (coded, plain)
-    )
-    three = along(out_three, lambda p: inward)
+    three = along(after(out_three, out_relay_one), lambda p: inward)
     out_relay_two = add(after(facts, out_three), [(share_two, ALWAYS), (two, ALWAYS)])
     relayed_two = along(out_relay_two, relay_two)
     (own,) = multiply(after(facts, out_relay_two), masked, columns, (HERE,), (plain,))

time: 65.6 us -> 67.5 us (1.029); the launches traced: 64.5 us -> 67.3 us
  waiting for transfers between devices: 25.7 us -> 27.9 us
  starting transfers between devices: 17.1 us -> 18 us
    ppermute x6, waiting for transfers between devices: 13.6 us -> 16.1 us  [along(): return lax.ppermute(block, ('row', 'col'), line_pairs(choose))]
    ppermute x6, starting transfers between devices: 12.9 us -> 13.8 us  [along(): return lax.ppermute(block, ('row', 'col'), line_pairs(choose))]
  transfers between devices with their start and end apart: 15 -> 15, of which waited for: 10 -> 10; matrix products, arithmetic and copies ran while one was open for 5% -> 5% of each run, Pallas kernels for 25% -> 24%
where the time goes in v3:
time: 67.5 us; the launch traced here: 67.3 us
  waiting for transfers between devices  27.9 us (41%)
  starting transfers between devices  18 us (27%)
  Pallas kernels  17.8 us (26%)
  other arithmetic  1.91 us (3%)
  local copies, waits for them, and re-layouts  1.5 us (2%)
    ppermute x6, waiting for transfers between devices, along(): return lax.ppermute(block, ('row', 'col'), line_pairs(choose))  16.1 us
    ppermute x6, starting transfers between devices, along(): return lax.ppermute(block, ('row', 'col'), line_pairs(choose))  13.8 us
    pallas_call x5, Pallas kernels, multiply(): pl.pallas_call(functools.partial(multiply_kernel, slots, kinds, rows, wid...  13.1 us
    ppermute x9, waiting for transfers between devices, across(): return lax.ppermute(block, 'row', [(i, i ^ bit) for i in range(8)])  11.8 us
    pallas_call x4, Pallas kernels, add(): pl.pallas_call(functools.partial(add_kernel, tuple(((weight, len(x)) for...  4.7 us
    ppermute x9, starting transfers between devices, across(): return lax.ppermute(block, 'row', [(i, i ^ bit) for i in range(8)])  4.19 us
  transfers between devices with their start and end apart: 15, of which 10 were waited for; matrix products, arithmetic and copies ran while one was open for 5% of the time, Pallas kernels for 24%

profile of v3, /device:TPU:10, one launch (start us, length us, event | category | flops | bytes accessed | tf_op | source)
XLA Modules:
  0.0 67.3 jit_solution(12160673441959099996)
XLA Ops:
  0.0 1.5 %collective-permute-start.1 = (bf16[2048,128]{1,0:T(8,128)(2,1)}, bf16[2048,128]{1,0:T(8,128)(2,1)S(1)}, u32[]{:S(2)}, u32[]{:S(2)}) collective-permute-start(bf16[2048,128]{1,0:T(8,128)(2,1)} %refs_0_.9), channel_id=1, source_target_pairs={{0,16},{4,20},{8,24},{12,28},{16,0},{20,4},{24,8},{28,12},{1,17},{... | collective-permute-start | bytes 1572872 | tf_op jit(solution)/shard_map/ppermute | solution.py:226
  1.5 0.5 collective-permute-start
  2.1 0.0 copy-start.1
  2.1 0.8 %dynamic-slice_bitcast_fusion = s32[10]{0:T(128)S(1)} fusion(s32[16,10]{1,0:T(8,128)} %constant.40.clone, s32[]{:T(128)S(6)} %select_n.15), kind=kLoop, calls=%fused_computation.2 | loop fusion | bytes 84 | tf_op jit(solution)/shard_map/squeeze | solution.py:247
  2.9 0.1 pad_add_fusion.facts
  3.0 0.0 collective-permute-start.2
  3.0 0.9 %convert_element_type.3 = bf16[8,16]{1,0:T(8,128)(2,1)S(1)} convert(s32[8,16]{1,0:T(8,128)} %param.6) | non-fusion elementwise | flops 128 | bytes 768 | tf_op jit(solution)/shard_map/convert_element_type | solution.py:23
  3.9 0.6 mul.15
  4.5 0.0 copy-done.1
  4.5 0.0 copy-start
  4.6 0.9 %bitcast_multiply_fusion.a_ref = bf16[1024,2048]{1,0:T(8,128)(2,1)S(1)} fusion(bf16[1024,2048]{1,0:T(8,128)(2,1)S(1)} %copy-done.1, bf16[128,8,16,128]{3,2,1,0:T(8,128)(2,1)S(1)} %bitcast.8), kind=kLoop, calls=%fused_computation | loop fusion | flops 2097152 | bytes 12582912 | tf_op jit(solution)/shard_map/mul | solution.py:24
  5.5 8.4 %collective-permute-done.1.refs_2_ = bf16[2048,128]{1,0:T(8,128)(2,1)S(1)} collective-permute-done((bf16[2048,128]{1,0:T(8,128)(2,1)}, bf16[2048,128]{1,0:T(8,128)(2,1)S(1)}, u32[]{:S(2)}, u32[]{:S(2)}) %collective-permute-start.1) | collective-permute-done | bytes 524320 | tf_op jit(solution)/shard_map/ppermute | solution.py:226
  13.9 1.2 %collective-permute-done.refs_1_ = bf16[2048,128]{1,0:T(8,128)(2,1)S(1)} collective-permute-done((bf16[2048,128]{1,0:T(8,128)(2,1)}, bf16[2048,128]{1,0:T(8,128)(2,1)S(1)}, u32[]{:S(2)}, u32[]{:S(2)}) %collective-permute-start) | collective-permute-done | bytes 524320 | tf_op jit(solution)/shard_map/ppermute | solution.py:226
  15.1 0.0 collective-permute-start.3
  15.1 0.5 collective-permute-start.4
  15.7 0.6 collective-permute-start.6
  16.3 0.5 collective-permute-start.7
  16.8 0.0 collective-permute-done.2.refs_3_.refs_5_
  16.8 0.2 collective-permute-done.3.refs_4_.refs_6_
  17.0 0.7 %collective-permute-done.4.refs_5_.refs_7_ = bf16[2048,128]{1,0:T(8,128)(2,1)S(1)} collective-permute-done((bf16[2048,128]{1,0:T(8,128)(2,1)S(1)}, bf16[2048,128]{1,0:T(8,128)(2,1)S(1)}, u32[]{:S(2)}, u32[]{:S(2)}) %collective-permute-start.4) | collective-permute-done | bytes 524320 | tf_op jit(solution)/shard_map/ppermute | solution.py:226
  17.8 0.0 copy-done
  17.8 2.5 %shard_map.46 = (s16[1040,128]{1,0:T(8,128)(2,1)S(1)}, s16[1040,128]{1,0:T(8,128)(2,1)S(1)}) custom-call(s32[12]{0:T(128)S(1)} %pad_add_fusion.facts, bf16[1024,2048]{1,0:T(8,128)(2,1)S(1)} %bitcast_multiply_fusion.a_ref, bf16[2048,128]{1,0:T(8,128)(2,1)S(1)} %copy-done, bf16[2048,128]{1,0:T(8,128)(2,1)S(1)} %collective-permute-done.refs_1_, ...), custom_call_target="tpu_custom_call" | custom-call | flops 3000000000 | bytes 9000000 | tf_op jit(solution)/shard_map/pallas_call | solution.py:130
  20.3 0.5 collective-permute-start.5
  20.8 2.2 %shard_map.47.refs_0_ = f32[1024,256]{1,0:T(8,128)S(1)} custom-call(s32[12]{0:T(128)S(1)} %pad_add_fusion.facts, bf16[1024,2048]{1,0:T(8,128)(2,1)S(1)} %bitcast_multiply_fusion.a_ref, bf16[2048,128]{1,0:T(8,128)(2,1)S(1)} %copy-done, bf16[2048,128]{1,0:T(8,128)(2,1)S(1)} %collective-permute-done.refs_1_, ...), custom_call_target="tpu_custom_call" | custom-call | flops 3000000000 | bytes 9000000 | tf_op jit(solution)/shard_map/pallas_call | solution.py:130
  23.0 1.2 %collective-permute-done.7.refs_4_ = bf16[1024,128]{1,0:T(8,128)(2,1)S(1)} collective-permute-done((bf16[1024,128]{1,0:T(8,128)(2,1)S(1)}, bf16[1024,128]{1,0:T(8,128)(2,1)S(1)}, u32[]{:S(2)}, u32[]{:S(2)}) %collective-permute-start.7) | collective-permute-done | bytes 262176 | tf_op jit(solution)/shard_map/ppermute | solution.py:226
  24.2 0.0 collective-permute-done.6.refs_3_
  24.2 0.0 collective-permute-start.8
  24.2 0.5 collective-permute-start.9
  24.7 0.5 collective-permute-start.11
  25.2 4.4 %collective-permute-done.5.refs_1_ = s16[1040,128]{1,0:T(8,128)(2,1)S(1)} collective-permute-done((s16[1040,128]{1,0:T(8,128)(2,1)S(1)}, s16[1040,128]{1,0:T(8,128)(2,1)S(1)}, u32[]{:S(2)}, u32[]{:S(2)}) %collective-permute-start.5) | collective-permute-done | bytes 266272 | tf_op jit(solution)/shard_map/ppermute | solution.py:229
  29.6 0.0 collective-permute-done.8.refs_8_
  29.6 0.0 collective-permute-done.9.refs_9_
  29.6 2.4 %shard_map.48 = s16[1040,256]{1,0:T(8,128)(2,1)S(1)} custom-call(s32[12]{0:T(128)S(1)} %pad_add_fusion.facts, bf16[1024,2048]{1,0:T(8,128)(2,1)S(1)} %bitcast_multiply_fusion.a_ref, bf16[2048,128]{1,0:T(8,128)(2,1)S(1)} %copy-done, bf16[2048,128]{1,0:T(8,128)(2,1)S(1)} %collective-permute-done.refs_1_, bf16[2048,128]{1,0:T(8,128)(2,1)S(1)} %collective-permute-done.1.refs_2_, ...), custom_call_target="tpu_custom_call" | custom-call | flops 3000000000 | bytes 9000000 | tf_op jit(solution)/shard_map/pallas_call | solution.py:130
  32.0 1.3 %collective-permute-start.10 = (s16[1040,256]{1,0:T(8,128)(2,1)S(1)}, s16[1040,256]{1,0:T(8,128)(2,1)S(1)}, u32[]{:S(2)}, u32[]{:S(2)}) collective-permute-start(s16[1040,256]{1,0:T(8,128)(2,1)S(1)} %shard_map.48), channel_id=1, source_target_pairs={{0,1},{3,2},{2,3},{4,5},{7,6},{6,7},{8,9},{11,10},{12,13},{15,14},... | collective-permute-start | bytes 1597448 | tf_op jit(solution)/shard_map/ppermute | solution.py:229
  33.3 3.7 %shard_map.49 = (s16[1040,256]{1,0:T(8,128)(2,1)S(1)}, f32[1024,256]{1,0:T(8,128)S(1)}) custom-call(s32[12]{0:T(128)S(1)} %pad_add_fusion.facts, bf16[1024,2048]{1,0:T(8,128)(2,1)S(1)} %bitcast_multiply_fusion.a_ref, bf16[2048,128]{1,0:T(8,128)(2,1)S(1)} %copy-done, bf16[2048,128]{1,0:T(8,128)(2,1)S(1)} %collective-permute-done.refs_1_, ...), custom_call_target="tpu_custom_call" | custom-call | flops 3000000000 | bytes 9000000 | tf_op jit(solution)/shard_map/pallas_call | solution.py:130
  37.0 0.0 collective-permute-done.11.refs_2_
  37.0 1.0 %shard_map.52 = s16[1040,256]{1,0:T(8,128)(2,1)S(1)} custom-call(s32[12]{0:T(128)S(1)} %pad_add_fusion.facts, f32[1024,256]{1,0:T(8,128)S(1)} %shard_map.47.refs_0_, s16[1040,128]{1,0:T(8,128)(2,1)S(1)} %collective-permute-done.5.refs_1_, s16[1040,128]{1,0:T(8,128)(2,1)S(1)} %collective-permute-done.11.refs_2_), custom_call_target="tpu_custom_call" | custom-call | flops 3000000000 | bytes 9000000 | tf_op jit(solution)/shard_map/pallas_call | solution.py:179
  38.0 5.6 %collective-permute-start.12 = (s16[1040,256]{1,0:T(8,128)(2,1)S(1)}, s16[1040,256]{1,0:T(8,128)(2,1)S(1)}, u32[]{:S(2)}, u32[]{:S(2)}) collective-permute-start(s16[1040,256]{1,0:T(8,128)(2,1)S(1)} %shard_map.52), channel_id=1, source_target_pairs={{1,2},{2,0},{5,6},{6,4},{9,11},{10,8},{13,15},{14,12},{17,19},{18,... | collective-permute-start | bytes 1597448 | tf_op jit(solution)/shard_map/ppermute | solution.py:229
  43.6 1.3 %collective-permute-start.13 = (s16[1040,256]{1,0:T(8,128)(2,1)S(1)}, s16[1040,256]{1,0:T(8,128)(2,1)S(1)}, u32[]{:S(2)}, u32[]{:S(2)}) collective-permute-start(s16[1040,256]{1,0:T(8,128)(2,1)S(1)} %get-tuple-element.34), channel_id=1, source_target_pairs={{0,1},{3,2},{4,5},{7,6},{8,9},{11,10},{12,13},{15,14},{16,17},{19,... | collective-permute-start | bytes 1597448 | tf_op jit(solution)/shard_map/ppermute | solution.py:229
  44.9 1.6 %collective-permute-done.10.refs_1_.refs_3_ = s16[1040,256]{1,0:T(8,128)(2,1)S(1)} collective-permute-done((s16[1040,256]{1,0:T(8,128)(2,1)S(1)}, s16[1040,256]{1,0:T(8,128)(2,1)S(1)}, u32[]{:S(2)}, u32[]{:S(2)}) %collective-permute-start.10) | collective-permute-done | bytes 532512 | tf_op jit(solution)/shard_map/ppermute | solution.py:229
  46.6 1.0 %shard_map.50 = s16[1040,256]{1,0:T(8,128)(2,1)S(1)} custom-call(s32[12]{0:T(128)S(1)} %pad_add_fusion.facts, f32[1024,256]{1,0:T(8,128)S(1)} %get-tuple-element.32.refs_0_, s16[1040,256]{1,0:T(8,128)(2,1)S(1)} %collective-permute-done.10.refs_1_.refs_3_), custom_call_target="tpu_custom_call" | custom-call | flops 3000000000 | bytes 9000000 | tf_op jit(solution)/shard_map/pallas_call | solution.py:179
  47.6 4.6 %collective-permute-start.14 = (s16[1040,256]{1,0:T(8,128)(2,1)S(1)}, s16[1040,256]{1,0:T(8,128)(2,1)S(1)}, u32[]{:S(2)}, u32[]{:S(2)}) collective-permute-start(s16[1040,256]{1,0:T(8,128)(2,1)S(1)} %shard_map.50), channel_id=1, source_target_pairs={{1,3},{2,1},{5,7},{6,5},{9,10},{10,9},{13,14},{14,13},{17,18},{18,... | collective-permute-start | bytes 1597448 | tf_op jit(solution)/shard_map/ppermute | solution.py:229
  52.2 2.2 %shard_map.51.refs_0_ = f32[1024,256]{1,0:T(8,128)S(1)} custom-call(s32[12]{0:T(128)S(1)} %pad_add_fusion.facts, bf16[1024,2048]{1,0:T(8,128)(2,1)S(1)} %bitcast_multiply_fusion.a_ref, bf16[2048,128]{1,0:T(8,128)(2,1)S(1)} %copy-done, bf16[2048,128]{1,0:T(8,128)(2,1)S(1)} %collective-permute-done.refs_1_, ...), custom_call_target="tpu_custom_call" | custom-call | flops 3000000000 | bytes 9000000 | tf_op jit(solution)/shard_map/pallas_call | solution.py:130
  54.5 1.7 %collective-permute-done.12.refs_4_ = s16[1040,256]{1,0:T(8,128)(2,1)S(1)} collective-permute-done((s16[1040,256]{1,0:T(8,128)(2,1)S(1)}, s16[1040,256]{1,0:T(8,128)(2,1)S(1)}, u32[]{:S(2)}, u32[]{:S(2)}) %collective-permute-start.12) | collective-permute-done | bytes 532512 | tf_op jit(solution)/shard_map/ppermute | solution.py:229
  56.1 1.1 %shard_map.53.refs_0_ = f32[1024,256]{1,0:T(8,128)S(1)} custom-call(s32[12]{0:T(128)S(1)} %pad_add_fusion.facts, f32[1024,256]{1,0:T(8,128)S(1)} %shard_map.51.refs_0_, s16[1040,128]{1,0:T(8,128)(2,1)S(1)} %collective-permute-done.5.refs_1_, s16[1040,128]{1,0:T(8,128)(2,1)S(1)} %collective-permute-done.11.refs_2_, ...), custom_call_target="tpu_custom_call" | custom-call | flops 3000000000 | bytes 9000000 | tf_op jit(solution)/shard_map/pallas_call | solution.py:179
  57.2 0.5 collective-permute-done.13.refs_1_
  57.8 7.9 %collective-permute-done.14.refs_2_ = s16[1040,256]{1,0:T(8,128)(2,1)S(1)} collective-permute-done((s16[1040,256]{1,0:T(8,128)(2,1)S(1)}, s16[1040,256]{1,0:T(8,128)(2,1)S(1)}, u32[]{:S(2)}, u32[]{:S(2)}) %collective-permute-start.14) | collective-permute-done | bytes 532512 | tf_op jit(solution)/shard_map/ppermute | solution.py:229
  65.6 1.6 %shard_map.54 = bf16[1024,256]{1,0:T(8,128)(2,1)} custom-call(s32[12]{0:T(128)S(1)} %pad_add_fusion.facts, f32[1024,256]{1,0:T(8,128)S(1)} %shard_map.53.refs_0_, s16[1040,256]{1,0:T(8,128)(2,1)S(1)} %collective-permute-done.13.refs_1_, s16[1040,256]{1,0:T(8,128)(2,1)S(1)} %collective-permute-done.14.refs_2_), custom_call_target="tpu_custom_call" | custom-call | flops 3000000000 | bytes 9000000 | tf_op jit(solution)/shard_map/pallas_call | solution.py:179
  (2 shorter events, 0.0 us)
Async XLA Ops:
  0.0 13.9 %collective-permute-start.1 = (bf16[2048,128]{1,0:T(8,128)(2,1)}, bf16[2048,128]{1,0:T(8,128)(2,1)S(1)}, u32[]{:S(2)}, u32[]{:S(2)}) collective-permute-start(bf16[2048,128]{1,0:T(8,128)(2,1)} %refs_0_.9), channel_id=1, source_target_pairs={{0,16},{4,20},{8,24},{12,28},{16,0},{20,4},{24,8},{28,12},{1,17},{... | collective-permute-start | bytes 1572872 | tf_op jit(solution)/shard_map/ppermute | solution.py:226
  1.5 13.6 %collective-permute-start = (bf16[2048,128]{1,0:T(8,128)(2,1)}, bf16[2048,128]{1,0:T(8,128)(2,1)S(1)}, u32[]{:S(2)}, u32[]{:S(2)}) collective-permute-start(bf16[2048,128]{1,0:T(8,128)(2,1)} %refs_0_.9), channel_id=1, source_target_pairs={{0,8},{4,12},{8,0},{12,4},{16,24},{20,28},{24,16},{28,20},{1,9},{5... | collective-permute-start | bytes 1572872 | tf_op jit(solution)/shard_map/ppermute | solution.py:226
  2.1 2.5 %copy-start.1 = (bf16[1024,2048]{1,0:T(8,128)(2,1)S(1)}, bf16[1024,2048]{1,0:T(8,128)(2,1)}, u32[]{:S(2)}) copy-start(bf16[1024,2048]{1,0:T(8,128)(2,1)} %param.4) | copy-start | bytes 12582916
  3.0 13.8 %collective-permute-start.2 = (bf16[2048,128]{1,0:T(8,128)(2,1)}, bf16[2048,128]{1,0:T(8,128)(2,1)S(1)}, u32[]{:S(2)}, u32[]{:S(2)}) collective-permute-start(bf16[2048,128]{1,0:T(8,128)(2,1)} %refs_0_.9), channel_id=1, source_target_pairs={{0,4},{4,0},{8,12},{12,8},{16,20},{20,16},{24,28},{28,24},{1,5},{5... | collective-permute-start | bytes 1572872 | tf_op jit(solution)/shard_map/ppermute | solution.py:226
  4.5 13.2 %copy-start = (bf16[2048,128]{1,0:T(8,128)(2,1)S(1)}, bf16[2048,128]{1,0:T(8,128)(2,1)}, u32[]{:S(2)}) copy-start(bf16[2048,128]{1,0:T(8,128)(2,1)} %refs_0_.9) | copy-start | bytes 1572868
  15.1 1.9 %collective-permute-start.3 = (bf16[2048,128]{1,0:T(8,128)(2,1)S(1)}, bf16[2048,128]{1,0:T(8,128)(2,1)S(1)}, u32[]{:S(2)}, u32[]{:S(2)}) collective-permute-start(bf16[2048,128]{1,0:T(8,128)(2,1)S(1)} %collective-permute-done.refs_1_), channel_id=1, source_target_pairs={{0,4},{4,0},{8,12},{12,8},{16,20},{20,16},{24,28},{28,24},{1,5},{5... | collective-permute-start | bytes 1572872 | tf_op jit(solution)/shard_map/ppermute | solution.py:226
  15.1 2.7 %collective-permute-start.4 = (bf16[2048,128]{1,0:T(8,128)(2,1)S(1)}, bf16[2048,128]{1,0:T(8,128)(2,1)S(1)}, u32[]{:S(2)}, u32[]{:S(2)}) collective-permute-start(bf16[2048,128]{1,0:T(8,128)(2,1)S(1)} %collective-permute-done.1.refs_2_), channel_id=1, source_target_pairs={{0,4},{4,0},{8,12},{12,8},{16,20},{20,16},{24,28},{28,24},{1,5},{5... | collective-permute-start | bytes 1572872 | tf_op jit(solution)/shard_map/ppermute | solution.py:226
  15.7 8.5 %collective-permute-start.6 = (bf16[1024,128]{1,0:T(8,128)(2,1)S(1)}, bf16[1024,128]{1,0:T(8,128)(2,1)S(1)}, u32[]{:S(2)}, u32[]{:S(2)}) collective-permute-start(bf16[1024,128]{1,0:T(8,128)(2,1)S(1)} %slice.6), channel_id=1, source_target_pairs={{0,8},{4,12},{8,0},{12,4},{16,24},{20,28},{24,16},{28,20},{1,9},{5... | collective-permute-start | bytes 786440 | tf_op jit(solution)/shard_map/ppermute | solution.py:226
  16.3 7.9 %collective-permute-start.7 = (bf16[1024,128]{1,0:T(8,128)(2,1)S(1)}, bf16[1024,128]{1,0:T(8,128)(2,1)S(1)}, u32[]{:S(2)}, u32[]{:S(2)}) collective-permute-start(bf16[1024,128]{1,0:T(8,128)(2,1)S(1)} %slice.7), channel_id=1, source_target_pairs={{0,16},{4,20},{8,24},{12,28},{16,0},{20,4},{24,8},{28,12},{1,17},{... | collective-permute-start | bytes 786440 | tf_op jit(solution)/shard_map/ppermute | solution.py:226
  20.3 9.3 %collective-permute-start.5 = (s16[1040,128]{1,0:T(8,128)(2,1)S(1)}, s16[1040,128]{1,0:T(8,128)(2,1)S(1)}, u32[]{:S(2)}, u32[]{:S(2)}) collective-permute-start(s16[1040,128]{1,0:T(8,128)(2,1)S(1)} %get-tuple-element.25), channel_id=1, source_target_pairs={{0,1},{1,0},{2,3},{3,2},{4,5},{5,4},{6,7},{7,6},{8,9},{9,8},{10,11... | collective-permute-start | bytes 798728 | tf_op jit(solution)/shard_map/ppermute | solution.py:229
  24.2 5.4 %collective-permute-start.8 = (bf16[1024,128]{1,0:T(8,128)(2,1)S(1)}, bf16[1024,128]{1,0:T(8,128)(2,1)S(1)}, u32[]{:S(2)}, u32[]{:S(2)}) collective-permute-start(bf16[1024,128]{1,0:T(8,128)(2,1)S(1)} %collective-permute-done.6.refs_3_), channel_id=1, source_target_pairs={{0,4},{4,0},{8,12},{12,8},{16,20},{20,16},{24,28},{28,24},{1,5},{5... | collective-permute-start | bytes 786440 | tf_op jit(solution)/shard_map/ppermute | solution.py:226
  24.2 5.4 %collective-permute-start.9 = (bf16[1024,128]{1,0:T(8,128)(2,1)S(1)}, bf16[1024,128]{1,0:T(8,128)(2,1)S(1)}, u32[]{:S(2)}, u32[]{:S(2)}) collective-permute-start(bf16[1024,128]{1,0:T(8,128)(2,1)S(1)} %collective-permute-done.7.refs_4_), channel_id=1, source_target_pairs={{0,4},{4,0},{8,12},{12,8},{16,20},{20,16},{24,28},{28,24},{1,5},{5... | collective-permute-start | bytes 786440 | tf_op jit(solution)/shard_map/ppermute | solution.py:226
  24.7 12.3 %collective-permute-start.11 = (s16[1040,128]{1,0:T(8,128)(2,1)S(1)}, s16[1040,128]{1,0:T(8,128)(2,1)S(1)}, u32[]{:S(2)}, u32[]{:S(2)}) collective-permute-start(s16[1040,128]{1,0:T(8,128)(2,1)S(1)} %get-tuple-element.23), channel_id=1, source_target_pairs={{0,1},{1,0},{2,3},{3,2},{4,5},{5,4},{6,7},{7,6},{8,9},{9,8},{10,11... | collective-permute-start | bytes 798728 | tf_op jit(solution)/shard_map/ppermute | solution.py:229
  32.0 14.6 %collective-permute-start.10 = (s16[1040,256]{1,0:T(8,128)(2,1)S(1)}, s16[1040,256]{1,0:T(8,128)(2,1)S(1)}, u32[]{:S(2)}, u32[]{:S(2)}) collective-permute-start(s16[1040,256]{1,0:T(8,128)(2,1)S(1)} %shard_map.48), channel_id=1, source_target_pairs={{0,1},{3,2},{2,3},{4,5},{7,6},{6,7},{8,9},{11,10},{12,13},{15,14},... | collective-permute-start | bytes 1597448 | tf_op jit(solution)/shard_map/ppermute | solution.py:229
  38.0 18.1 %collective-permute-start.12 = (s16[1040,256]{1,0:T(8,128)(2,1)S(1)}, s16[1040,256]{1,0:T(8,128)(2,1)S(1)}, u32[]{:S(2)}, u32[]{:S(2)}) collective-permute-start(s16[1040,256]{1,0:T(8,128)(2,1)S(1)} %shard_map.52), channel_id=1, source_target_pairs={{1,2},{2,0},{5,6},{6,4},{9,11},{10,8},{13,15},{14,12},{17,19},{18,... | collective-permute-start | bytes 1597448 | tf_op jit(solution)/shard_map/ppermute | solution.py:229
  43.6 14.1 %collective-permute-start.13 = (s16[1040,256]{1,0:T(8,128)(2,1)S(1)}, s16[1040,256]{1,0:T(8,128)(2,1)S(1)}, u32[]{:S(2)}, u32[]{:S(2)}) collective-permute-start(s16[1040,256]{1,0:T(8,128)(2,1)S(1)} %get-tuple-element.34), channel_id=1, source_target_pairs={{0,1},{3,2},{4,5},{7,6},{8,9},{11,10},{12,13},{15,14},{16,17},{19,... | collective-permute-start | bytes 1597448 | tf_op jit(solution)/shard_map/ppermute | solution.py:229
  47.6 18.1 %collective-permute-start.14 = (s16[1040,256]{1,0:T(8,128)(2,1)S(1)}, s16[1040,256]{1,0:T(8,128)(2,1)S(1)}, u32[]{:S(2)}, u32[]{:S(2)}) collective-permute-start(s16[1040,256]{1,0:T(8,128)(2,1)S(1)} %shard_map.50), channel_id=1, source_target_pairs={{1,3},{2,1},{5,7},{6,5},{9,10},{10,9},{13,14},{14,13},{17,18},{18,... | collective-permute-start | bytes 1597448 | tf_op jit(solution)/shard_map/ppermute | solution.py:229

commit v4 on v0

--- a/solution.py
+++ b/solution.py
@@ -242,10 +242,11 @@
     def relay_two(p):
         return [(1, 3 if p == 0 else 2), (2, 0 if p == 3 else 1)]
 
-    by_x, by_y, twin = across(integrals, 2), across(integrals, 4), across(integrals, 1)
+    by_x, by_y = across(integrals, 2), across(integrals, 4)
     plans = jnp.asarray([plan_of(p, z) for p in range(4) for z in range(4)], jnp.int32)
     planned = lax.dynamic_slice_in_dim(plans, chip * 4 + at, 1)[0]
     facts = jnp.concatenate([planned, jnp.stack([core, chip]).astype(jnp.int32)])
+    twin = across(after(integrals, facts), 1)
     masked = apply_mask(amplitudes, tile_mask)
     by_x, by_y = after(by_x, masked, facts), after(by_y, masked, facts)
     half = integrals.shape[0] // 2

time: 65.6 us -> 65 us (level)
  local copies, waits for them, and re-layouts: 2.16 us -> 1.5 us
    unnamed x4, local copies, waits for them, and re-layouts: 0.67 us -> 0.01 us
where the time goes in v4:
time: 65 us; the launch traced here: 63.8 us
  waiting for transfers between devices  25.4 us (39%)
  Pallas kernels  17.7 us (27%)
  starting transfers between devices  17.1 us (26%)
  other arithmetic  1.91 us (3%)
  local copies, waits for them, and re-layouts  1.5 us (2%)
    ppermute x6, waiting for transfers between devices, along(): return lax.ppermute(block, ('row', 'col'), line_pairs(choose))  13.6 us
    pallas_call x5, Pallas kernels, multiply(): pl.pallas_call(functools.partial(multiply_kernel, slots, kinds, rows, wid...  13.1 us
    ppermute x6, starting transfers between devices, along(): return lax.ppermute(block, ('row', 'col'), line_pairs(choose))  12.9 us
    ppermute x9, waiting for transfers between devices, across(): return lax.ppermute(block, 'row', [(i, i ^ bit) for i in range(8)])  11.8 us
    pallas_call x4, Pallas kernels, add(): pl.pallas_call(functools.partial(add_kernel, tuple(((weight, len(x)) for...  4.68 us
    ppermute x9, starting transfers between devices, across(): return lax.ppermute(block, 'row', [(i, i ^ bit) for i in range(8)])  4.19 us
  transfers between devices with their start and end apart: 15, of which 10 were waited for; matrix products, arithmetic and copies ran while one was open for 5% of the time, Pallas kernels for 25%

profile of v4, /device:TPU:10, one launch (start us, length us, event | category | flops | bytes accessed | tf_op | source)
XLA Modules:
  0.0 63.8 jit_solution(2924414538223568461)
XLA Ops:
  0.0 1.5 %collective-permute-start.1 = (bf16[2048,128]{1,0:T(8,128)(2,1)}, bf16[2048,128]{1,0:T(8,128)(2,1)S(1)}, u32[]{:S(2)}, u32[]{:S(2)}) collective-permute-start(bf16[2048,128]{1,0:T(8,128)(2,1)} %refs_0_.9), channel_id=1, source_target_pairs={{0,16},{4,20},{8,24},{12,28},{16,0},{20,4},{24,8},{28,12},{1,17},{... | collective-permute-start | bytes 1572872 | tf_op jit(solution)/shard_map/ppermute | solution.py:226
  1.5 0.5 collective-permute-start
  2.1 0.0 copy-start.1
  2.1 0.8 %dynamic-slice_bitcast_fusion = s32[10]{0:T(128)S(1)} fusion(s32[16,10]{1,0:T(8,128)} %constant.40.clone, s32[]{:T(128)S(6)} %select_n.15), kind=kLoop, calls=%fused_computation.2 | loop fusion | bytes 84 | tf_op jit(solution)/shard_map/squeeze | solution.py:247
  2.9 0.1 pad_add_fusion.facts
  3.0 0.0 collective-permute-start.2
  3.0 0.9 %convert_element_type.3 = bf16[8,16]{1,0:T(8,128)(2,1)S(1)} convert(s32[8,16]{1,0:T(8,128)} %param.6) | non-fusion elementwise | flops 128 | bytes 768 | tf_op jit(solution)/shard_map/convert_element_type | solution.py:23
  3.9 0.6 mul.15
  4.5 0.0 copy-done.1
  4.5 0.0 copy-start
  4.6 0.9 %bitcast_multiply_fusion.a_ref = bf16[1024,2048]{1,0:T(8,128)(2,1)S(1)} fusion(bf16[1024,2048]{1,0:T(8,128)(2,1)S(1)} %copy-done.1, bf16[128,8,16,128]{3,2,1,0:T(8,128)(2,1)S(1)} %bitcast.8), kind=kLoop, calls=%fused_computation | loop fusion | flops 2097152 | bytes 12582912 | tf_op jit(solution)/shard_map/mul | solution.py:24
  5.5 8.4 %collective-permute-done.1.refs_2_ = bf16[2048,128]{1,0:T(8,128)(2,1)S(1)} collective-permute-done((bf16[2048,128]{1,0:T(8,128)(2,1)}, bf16[2048,128]{1,0:T(8,128)(2,1)S(1)}, u32[]{:S(2)}, u32[]{:S(2)}) %collective-permute-start.1) | collective-permute-done | bytes 524320 | tf_op jit(solution)/shard_map/ppermute | solution.py:226
  13.9 1.2 %collective-permute-done.refs_1_ = bf16[2048,128]{1,0:T(8,128)(2,1)S(1)} collective-permute-done((bf16[2048,128]{1,0:T(8,128)(2,1)}, bf16[2048,128]{1,0:T(8,128)(2,1)S(1)}, u32[]{:S(2)}, u32[]{:S(2)}) %collective-permute-start) | collective-permute-done | bytes 524320 | tf_op jit(solution)/shard_map/ppermute | solution.py:226
  15.1 0.0 collective-permute-start.3
  15.1 0.5 collective-permute-start.4
  15.7 0.6 collective-permute-start.6
  16.3 0.5 collective-permute-start.7
  16.8 0.0 collective-permute-done.2.refs_3_.refs_5_
  16.8 0.2 collective-permute-done.3.refs_4_.refs_6_
  17.0 0.7 %collective-permute-done.4.refs_5_.refs_7_ = bf16[2048,128]{1,0:T(8,128)(2,1)S(1)} collective-permute-done((bf16[2048,128]{1,0:T(8,128)(2,1)S(1)}, bf16[2048,128]{1,0:T(8,128)(2,1)S(1)}, u32[]{:S(2)}, u32[]{:S(2)}) %collective-permute-start.4) | collective-permute-done | bytes 524320 | tf_op jit(solution)/shard_map/ppermute | solution.py:226
  17.8 0.0 copy-done
  17.8 2.5 %shard_map.46 = (s16[1040,128]{1,0:T(8,128)(2,1)S(1)}, s16[1040,128]{1,0:T(8,128)(2,1)S(1)}) custom-call(s32[12]{0:T(128)S(1)} %pad_add_fusion.facts, bf16[1024,2048]{1,0:T(8,128)(2,1)S(1)} %bitcast_multiply_fusion.a_ref, bf16[2048,128]{1,0:T(8,128)(2,1)S(1)} %copy-done, bf16[2048,128]{1,0:T(8,128)(2,1)S(1)} %collective-permute-done.refs_1_, ...), custom_call_target="tpu_custom_call" | custom-call | flops 3000000000 | bytes 9000000 | tf_op jit(solution)/shard_map/pallas_call | solution.py:130
  20.3 0.5 collective-permute-start.5
  20.8 2.2 %shard_map.47.refs_0_ = f32[1024,256]{1,0:T(8,128)S(1)} custom-call(s32[12]{0:T(128)S(1)} %pad_add_fusion.facts, bf16[1024,2048]{1,0:T(8,128)(2,1)S(1)} %bitcast_multiply_fusion.a_ref, bf16[2048,128]{1,0:T(8,128)(2,1)S(1)} %copy-done, bf16[2048,128]{1,0:T(8,128)(2,1)S(1)} %collective-permute-done.refs_1_, ...), custom_call_target="tpu_custom_call" | custom-call | flops 3000000000 | bytes 9000000 | tf_op jit(solution)/shard_map/pallas_call | solution.py:130
  23.0 1.2 %collective-permute-done.7.refs_4_ = bf16[1024,128]{1,0:T(8,128)(2,1)S(1)} collective-permute-done((bf16[1024,128]{1,0:T(8,128)(2,1)S(1)}, bf16[1024,128]{1,0:T(8,128)(2,1)S(1)}, u32[]{:S(2)}, u32[]{:S(2)}) %collective-permute-start.7) | collective-permute-done | bytes 262176 | tf_op jit(solution)/shard_map/ppermute | solution.py:226
  24.2 0.0 collective-permute-done.6.refs_3_
  24.2 0.0 collective-permute-start.8
  24.2 0.5 collective-permute-start.9
  24.7 0.5 collective-permute-start.10
  25.2 4.4 %collective-permute-done.5.refs_1_ = s16[1040,128]{1,0:T(8,128)(2,1)S(1)} collective-permute-done((s16[1040,128]{1,0:T(8,128)(2,1)S(1)}, s16[1040,128]{1,0:T(8,128)(2,1)S(1)}, u32[]{:S(2)}, u32[]{:S(2)}) %collective-permute-start.5) | collective-permute-done | bytes 266272 | tf_op jit(solution)/shard_map/ppermute | solution.py:229
  29.6 0.0 collective-permute-done.8.refs_8_
  29.6 0.0 collective-permute-done.9.refs_9_
  29.6 2.4 %shard_map.48 = s16[1040,256]{1,0:T(8,128)(2,1)S(1)} custom-call(s32[12]{0:T(128)S(1)} %pad_add_fusion.facts, bf16[1024,2048]{1,0:T(8,128)(2,1)S(1)} %bitcast_multiply_fusion.a_ref, bf16[2048,128]{1,0:T(8,128)(2,1)S(1)} %copy-done, bf16[2048,128]{1,0:T(8,128)(2,1)S(1)} %collective-permute-done.refs_1_, bf16[2048,128]{1,0:T(8,128)(2,1)S(1)} %collective-permute-done.1.refs_2_, ...), custom_call_target="tpu_custom_call" | custom-call | flops 3000000000 | bytes 9000000 | tf_op jit(solution)/shard_map/pallas_call | solution.py:130
  32.0 1.3 %collective-permute-start.11 = (s16[1040,256]{1,0:T(8,128)(2,1)S(1)}, s16[1040,256]{1,0:T(8,128)(2,1)S(1)}, u32[]{:S(2)}, u32[]{:S(2)}) collective-permute-start(s16[1040,256]{1,0:T(8,128)(2,1)S(1)} %shard_map.48), channel_id=1, source_target_pairs={{0,1},{3,2},{2,3},{4,5},{7,6},{6,7},{8,9},{11,10},{12,13},{15,14},... | collective-permute-start | bytes 1597448 | tf_op jit(solution)/shard_map/ppermute | solution.py:229
  33.3 1.2 %collective-permute-done.10.refs_2_ = s16[1040,128]{1,0:T(8,128)(2,1)S(1)} collective-permute-done((s16[1040,128]{1,0:T(8,128)(2,1)S(1)}, s16[1040,128]{1,0:T(8,128)(2,1)S(1)}, u32[]{:S(2)}, u32[]{:S(2)}) %collective-permute-start.10) | collective-permute-done | bytes 266272 | tf_op jit(solution)/shard_map/ppermute | solution.py:229
  34.5 1.0 %shard_map.49 = s16[1040,256]{1,0:T(8,128)(2,1)S(1)} custom-call(s32[12]{0:T(128)S(1)} %pad_add_fusion.facts, f32[1024,256]{1,0:T(8,128)S(1)} %shard_map.47.refs_0_, s16[1040,128]{1,0:T(8,128)(2,1)S(1)} %collective-permute-done.5.refs_1_, s16[1040,128]{1,0:T(8,128)(2,1)S(1)} %collective-permute-done.10.refs_2_), custom_call_target="tpu_custom_call" | custom-call | flops 3000000000 | bytes 9000000 | tf_op jit(solution)/shard_map/pallas_call | solution.py:179
  35.4 4.5 %collective-permute-start.12 = (s16[1040,256]{1,0:T(8,128)(2,1)S(1)}, s16[1040,256]{1,0:T(8,128)(2,1)S(1)}, u32[]{:S(2)}, u32[]{:S(2)}) collective-permute-start(s16[1040,256]{1,0:T(8,128)(2,1)S(1)} %shard_map.49), channel_id=1, source_target_pairs={{1,2},{2,0},{5,6},{6,4},{9,11},{10,8},{13,15},{14,12},{17,19},{18,... | collective-permute-start | bytes 1597448 | tf_op jit(solution)/shard_map/ppermute | solution.py:229
  40.0 3.7 %shard_map.50 = (s16[1040,256]{1,0:T(8,128)(2,1)S(1)}, f32[1024,256]{1,0:T(8,128)S(1)}) custom-call(s32[12]{0:T(128)S(1)} %pad_add_fusion.facts, bf16[1024,2048]{1,0:T(8,128)(2,1)S(1)} %bitcast_multiply_fusion.a_ref, bf16[2048,128]{1,0:T(8,128)(2,1)S(1)} %copy-done, bf16[2048,128]{1,0:T(8,128)(2,1)S(1)} %collective-permute-done.refs_1_, ...), custom_call_target="tpu_custom_call" | custom-call | flops 3000000000 | bytes 9000000 | tf_op jit(solution)/shard_map/pallas_call | solution.py:130
  43.7 1.3 %collective-permute-start.13 = (s16[1040,256]{1,0:T(8,128)(2,1)S(1)}, s16[1040,256]{1,0:T(8,128)(2,1)S(1)}, u32[]{:S(2)}, u32[]{:S(2)}) collective-permute-start(s16[1040,256]{1,0:T(8,128)(2,1)S(1)} %get-tuple-element.31), channel_id=1, source_target_pairs={{0,1},{3,2},{4,5},{7,6},{8,9},{11,10},{12,13},{15,14},{16,17},{19,... | collective-permute-start | bytes 1597448 | tf_op jit(solution)/shard_map/ppermute | solution.py:229
  45.0 1.3 %collective-permute-done.11.refs_1_.refs_3_ = s16[1040,256]{1,0:T(8,128)(2,1)S(1)} collective-permute-done((s16[1040,256]{1,0:T(8,128)(2,1)S(1)}, s16[1040,256]{1,0:T(8,128)(2,1)S(1)}, u32[]{:S(2)}, u32[]{:S(2)}) %collective-permute-start.11) | collective-permute-done | bytes 532512 | tf_op jit(solution)/shard_map/ppermute | solution.py:229
  46.4 1.0 %shard_map.51 = s16[1040,256]{1,0:T(8,128)(2,1)S(1)} custom-call(s32[12]{0:T(128)S(1)} %pad_add_fusion.facts, f32[1024,256]{1,0:T(8,128)S(1)} %get-tuple-element.33.refs_0_, s16[1040,256]{1,0:T(8,128)(2,1)S(1)} %collective-permute-done.11.refs_1_.refs_3_), custom_call_target="tpu_custom_call" | custom-call | flops 3000000000 | bytes 9000000 | tf_op jit(solution)/shard_map/pallas_call | solution.py:179
  47.3 4.8 %collective-permute-start.14 = (s16[1040,256]{1,0:T(8,128)(2,1)S(1)}, s16[1040,256]{1,0:T(8,128)(2,1)S(1)}, u32[]{:S(2)}, u32[]{:S(2)}) collective-permute-start(s16[1040,256]{1,0:T(8,128)(2,1)S(1)} %shard_map.51), channel_id=1, source_target_pairs={{1,3},{2,1},{5,7},{6,5},{9,10},{10,9},{13,14},{14,13},{17,18},{18,... | collective-permute-start | bytes 1597448 | tf_op jit(solution)/shard_map/ppermute | solution.py:229
  52.2 2.2 %shard_map.52.refs_0_ = f32[1024,256]{1,0:T(8,128)S(1)} custom-call(s32[12]{0:T(128)S(1)} %pad_add_fusion.facts, bf16[1024,2048]{1,0:T(8,128)(2,1)S(1)} %bitcast_multiply_fusion.a_ref, bf16[2048,128]{1,0:T(8,128)(2,1)S(1)} %copy-done, bf16[2048,128]{1,0:T(8,128)(2,1)S(1)} %collective-permute-done.refs_1_, ...), custom_call_target="tpu_custom_call" | custom-call | flops 3000000000 | bytes 9000000 | tf_op jit(solution)/shard_map/pallas_call | solution.py:130
  54.4 0.0 collective-permute-done.12.refs_4_
  54.4 1.1 %shard_map.53.refs_0_ = f32[1024,256]{1,0:T(8,128)S(1)} custom-call(s32[12]{0:T(128)S(1)} %pad_add_fusion.facts, f32[1024,256]{1,0:T(8,128)S(1)} %shard_map.52.refs_0_, s16[1040,128]{1,0:T(8,128)(2,1)S(1)} %collective-permute-done.5.refs_1_, s16[1040,128]{1,0:T(8,128)(2,1)S(1)} %collective-permute-done.10.refs_2_, ...), custom_call_target="tpu_custom_call" | custom-call | flops 3000000000 | bytes 9000000 | tf_op jit(solution)/shard_map/pallas_call | solution.py:179
  55.5 3.1 %collective-permute-done.13.refs_1_ = s16[1040,256]{1,0:T(8,128)(2,1)S(1)} collective-permute-done((s16[1040,256]{1,0:T(8,128)(2,1)S(1)}, s16[1040,256]{1,0:T(8,128)(2,1)S(1)}, u32[]{:S(2)}, u32[]{:S(2)}) %collective-permute-start.13) | collective-permute-done | bytes 532512 | tf_op jit(solution)/shard_map/ppermute | solution.py:229
  58.6 3.5 %collective-permute-done.14.refs_2_ = s16[1040,256]{1,0:T(8,128)(2,1)S(1)} collective-permute-done((s16[1040,256]{1,0:T(8,128)(2,1)S(1)}, s16[1040,256]{1,0:T(8,128)(2,1)S(1)}, u32[]{:S(2)}, u32[]{:S(2)}) %collective-permute-start.14) | collective-permute-done | bytes 532512 | tf_op jit(solution)/shard_map/ppermute | solution.py:229
  62.2 1.6 %shard_map.54 = bf16[1024,256]{1,0:T(8,128)(2,1)} custom-call(s32[12]{0:T(128)S(1)} %pad_add_fusion.facts, f32[1024,256]{1,0:T(8,128)S(1)} %shard_map.53.refs_0_, s16[1040,256]{1,0:T(8,128)(2,1)S(1)} %collective-permute-done.13.refs_1_, s16[1040,256]{1,0:T(8,128)(2,1)S(1)} %collective-permute-done.14.refs_2_), custom_call_target="tpu_custom_call" | custom-call | flops 3000000000 | bytes 9000000 | tf_op jit(solution)/shard_map/pallas_call | solution.py:179
  (2 shorter events, 0.0 us)
Async XLA Ops:
  0.0 13.9 %collective-permute-start.1 = (bf16[2048,128]{1,0:T(8,128)(2,1)}, bf16[2048,128]{1,0:T(8,128)(2,1)S(1)}, u32[]{:S(2)}, u32[]{:S(2)}) collective-permute-start(bf16[2048,128]{1,0:T(8,128)(2,1)} %refs_0_.9), channel_id=1, source_target_pairs={{0,16},{4,20},{8,24},{12,28},{16,0},{20,4},{24,8},{28,12},{1,17},{... | collective-permute-start | bytes 1572872 | tf_op jit(solution)/shard_map/ppermute | solution.py:226
  1.5 13.6 %collective-permute-start = (bf16[2048,128]{1,0:T(8,128)(2,1)}, bf16[2048,128]{1,0:T(8,128)(2,1)S(1)}, u32[]{:S(2)}, u32[]{:S(2)}) collective-permute-start(bf16[2048,128]{1,0:T(8,128)(2,1)} %refs_0_.9), channel_id=1, source_target_pairs={{0,8},{4,12},{8,0},{12,4},{16,24},{20,28},{24,16},{28,20},{1,9},{5... | collective-permute-start | bytes 1572872 | tf_op jit(solution)/shard_map/ppermute | solution.py:226
  2.1 2.5 %copy-start.1 = (bf16[1024,2048]{1,0:T(8,128)(2,1)S(1)}, bf16[1024,2048]{1,0:T(8,128)(2,1)}, u32[]{:S(2)}) copy-start(bf16[1024,2048]{1,0:T(8,128)(2,1)} %param.4) | copy-start | bytes 12582916
  3.0 13.8 %collective-permute-start.2 = (bf16[2048,128]{1,0:T(8,128)(2,1)}, bf16[2048,128]{1,0:T(8,128)(2,1)S(1)}, u32[]{:S(2)}, u32[]{:S(2)}) collective-permute-start(bf16[2048,128]{1,0:T(8,128)(2,1)} %refs_0_.9), channel_id=1, source_target_pairs={{0,4},{4,0},{8,12},{12,8},{16,20},{20,16},{24,28},{28,24},{1,5},{5... | collective-permute-start | bytes 1572872 | tf_op jit(solution)/shard_map/ppermute | solution.py:226
  4.5 13.2 %copy-start = (bf16[2048,128]{1,0:T(8,128)(2,1)S(1)}, bf16[2048,128]{1,0:T(8,128)(2,1)}, u32[]{:S(2)}) copy-start(bf16[2048,128]{1,0:T(8,128)(2,1)} %refs_0_.9) | copy-start | bytes 1572868
  15.1 1.9 %collective-permute-start.3 = (bf16[2048,128]{1,0:T(8,128)(2,1)S(1)}, bf16[2048,128]{1,0:T(8,128)(2,1)S(1)}, u32[]{:S(2)}, u32[]{:S(2)}) collective-permute-start(bf16[2048,128]{1,0:T(8,128)(2,1)S(1)} %collective-permute-done.refs_1_), channel_id=1, source_target_pairs={{0,4},{4,0},{8,12},{12,8},{16,20},{20,16},{24,28},{28,24},{1,5},{5... | collective-permute-start | bytes 1572872 | tf_op jit(solution)/shard_map/ppermute | solution.py:226
  15.1 2.7 %collective-permute-start.4 = (bf16[2048,128]{1,0:T(8,128)(2,1)S(1)}, bf16[2048,128]{1,0:T(8,128)(2,1)S(1)}, u32[]{:S(2)}, u32[]{:S(2)}) collective-permute-start(bf16[2048,128]{1,0:T(8,128)(2,1)S(1)} %collective-permute-done.1.refs_2_), channel_id=1, source_target_pairs={{0,4},{4,0},{8,12},{12,8},{16,20},{20,16},{24,28},{28,24},{1,5},{5... | collective-permute-start | bytes 1572872 | tf_op jit(solution)/shard_map/ppermute | solution.py:226
  15.7 8.5 %collective-permute-start.6 = (bf16[1024,128]{1,0:T(8,128)(2,1)S(1)}, bf16[1024,128]{1,0:T(8,128)(2,1)S(1)}, u32[]{:S(2)}, u32[]{:S(2)}) collective-permute-start(bf16[1024,128]{1,0:T(8,128)(2,1)S(1)} %slice.6), channel_id=1, source_target_pairs={{0,8},{4,12},{8,0},{12,4},{16,24},{20,28},{24,16},{28,20},{1,9},{5... | collective-permute-start | bytes 786440 | tf_op jit(solution)/shard_map/ppermute | solution.py:226
  16.3 7.9 %collective-permute-start.7 = (bf16[1024,128]{1,0:T(8,128)(2,1)S(1)}, bf16[1024,128]{1,0:T(8,128)(2,1)S(1)}, u32[]{:S(2)}, u32[]{:S(2)}) collective-permute-start(bf16[1024,128]{1,0:T(8,128)(2,1)S(1)} %slice.7), channel_id=1, source_target_pairs={{0,16},{4,20},{8,24},{12,28},{16,0},{20,4},{24,8},{28,12},{1,17},{... | collective-permute-start | bytes 786440 | tf_op jit(solution)/shard_map/ppermute | solution.py:226
  20.3 9.3 %collective-permute-start.5 = (s16[1040,128]{1,0:T(8,128)(2,1)S(1)}, s16[1040,128]{1,0:T(8,128)(2,1)S(1)}, u32[]{:S(2)}, u32[]{:S(2)}) collective-permute-start(s16[1040,128]{1,0:T(8,128)(2,1)S(1)} %get-tuple-element.25), channel_id=1, source_target_pairs={{0,1},{1,0},{2,3},{3,2},{4,5},{5,4},{6,7},{7,6},{8,9},{9,8},{10,11... | collective-permute-start | bytes 798728 | tf_op jit(solution)/shard_map/ppermute | solution.py:229
  24.2 5.4 %collective-permute-start.8 = (bf16[1024,128]{1,0:T(8,128)(2,1)S(1)}, bf16[1024,128]{1,0:T(8,128)(2,1)S(1)}, u32[]{:S(2)}, u32[]{:S(2)}) collective-permute-start(bf16[1024,128]{1,0:T(8,128)(2,1)S(1)} %collective-permute-done.6.refs_3_), channel_id=1, source_target_pairs={{0,4},{4,0},{8,12},{12,8},{16,20},{20,16},{24,28},{28,24},{1,5},{5... | collective-permute-start | bytes 786440 | tf_op jit(solution)/shard_map/ppermute | solution.py:226
  24.2 5.4 %collective-permute-start.9 = (bf16[1024,128]{1,0:T(8,128)(2,1)S(1)}, bf16[1024,128]{1,0:T(8,128)(2,1)S(1)}, u32[]{:S(2)}, u32[]{:S(2)}) collective-permute-start(bf16[1024,128]{1,0:T(8,128)(2,1)S(1)} %collective-permute-done.7.refs_4_), channel_id=1, source_target_pairs={{0,4},{4,0},{8,12},{12,8},{16,20},{20,16},{24,28},{28,24},{1,5},{5... | collective-permute-start | bytes 786440 | tf_op jit(solution)/shard_map/ppermute | solution.py:226
  24.7 9.7 %collective-permute-start.10 = (s16[1040,128]{1,0:T(8,128)(2,1)S(1)}, s16[1040,128]{1,0:T(8,128)(2,1)S(1)}, u32[]{:S(2)}, u32[]{:S(2)}) collective-permute-start(s16[1040,128]{1,0:T(8,128)(2,1)S(1)} %get-tuple-element.23), channel_id=1, source_target_pairs={{0,1},{1,0},{2,3},{3,2},{4,5},{5,4},{6,7},{7,6},{8,9},{9,8},{10,11... | collective-permute-start | bytes 798728 | tf_op jit(solution)/shard_map/ppermute | solution.py:229
  32.0 14.4 %collective-permute-start.11 = (s16[1040,256]{1,0:T(8,128)(2,1)S(1)}, s16[1040,256]{1,0:T(8,128)(2,1)S(1)}, u32[]{:S(2)}, u32[]{:S(2)}) collective-permute-start(s16[1040,256]{1,0:T(8,128)(2,1)S(1)} %shard_map.48), channel_id=1, source_target_pairs={{0,1},{3,2},{2,3},{4,5},{7,6},{6,7},{8,9},{11,10},{12,13},{15,14},... | collective-permute-start | bytes 1597448 | tf_op jit(solution)/shard_map/ppermute | solution.py:229
  35.4 19.0 %collective-permute-start.12 = (s16[1040,256]{1,0:T(8,128)(2,1)S(1)}, s16[1040,256]{1,0:T(8,128)(2,1)S(1)}, u32[]{:S(2)}, u32[]{:S(2)}) collective-permute-start(s16[1040,256]{1,0:T(8,128)(2,1)S(1)} %shard_map.49), channel_id=1, source_target_pairs={{1,2},{2,0},{5,6},{6,4},{9,11},{10,8},{13,15},{14,12},{17,19},{18,... | collective-permute-start | bytes 1597448 | tf_op jit(solution)/shard_map/ppermute | solution.py:229
  43.7 14.9 %collective-permute-start.13 = (s16[1040,256]{1,0:T(8,128)(2,1)S(1)}, s16[1040,256]{1,0:T(8,128)(2,1)S(1)}, u32[]{:S(2)}, u32[]{:S(2)}) collective-permute-start(s16[1040,256]{1,0:T(8,128)(2,1)S(1)} %get-tuple-element.31), channel_id=1, source_target_pairs={{0,1},{3,2},{4,5},{7,6},{8,9},{11,10},{12,13},{15,14},{16,17},{19,... | collective-permute-start | bytes 1597448 | tf_op jit(solution)/shard_map/ppermute | solution.py:229
  47.3 14.8 %collective-permute-start.14 = (s16[1040,256]{1,0:T(8,128)(2,1)S(1)}, s16[1040,256]{1,0:T(8,128)(2,1)S(1)}, u32[]{:S(2)}, u32[]{:S(2)}) collective-permute-start(s16[1040,256]{1,0:T(8,128)(2,1)S(1)} %shard_map.51), channel_id=1, source_target_pairs={{1,3},{2,1},{5,7},{6,5},{9,10},{10,9},{13,14},{14,13},{17,18},{18,... | collective-permute-start | bytes 1597448 | tf_op jit(solution)/shard_map/ppermute | solution.py:229

commit v5 on v4

--- a/solution.py
+++ b/solution.py
@@ -270,10 +270,10 @@
     (own,) = multiply(after(facts, out_relay_two), masked, columns, (HERE,), (plain,))
     most = add(
         facts,
-        [(own, ALWAYS), (one, EARLY), (two, LATE), (relayed_one, ALWAYS)],
+        [(own, ALWAYS), (one, EARLY), (two, LATE), (relayed_one, ALWAYS), (three, INNER)],
         jnp.float32,
     )
-    return add(facts, [(most, ALWAYS), (three, INNER), (relayed_two, ALWAYS)], jnp.bfloat16)
+    return add(facts, [(most, ALWAYS), (relayed_two, ALWAYS)], jnp.bfloat16)
 
 
 def solution(mesh):

time: 65 us -> 64.8 us (level)
  transfers between devices with their start and end apart: 15 -> 15, of which waited for: 10 -> 10; matrix products, arithmetic and copies ran while one was open for 5% -> 5% of each run, Pallas kernels for 25% -> 26%
where the time goes in v5:
time: 64.8 us; the launch traced here: 63.7 us
  waiting for transfers between devices  25.3 us (39%)
  Pallas kernels  17.7 us (27%)
  starting transfers between devices  17.1 us (26%)
  other arithmetic  1.91 us (3%)
  local copies, waits for them, and re-layouts  1.5 us (2%)
    ppermute x6, waiting for transfers between devices, along(): return lax.ppermute(block, ('row', 'col'), line_pairs(choose))  13.4 us
    pallas_call x5, Pallas kernels, multiply(): pl.pallas_call(functools.partial(multiply_kernel, slots, kinds, rows, wid...  13.1 us
    ppermute x6, starting transfers between devices, along(): return lax.ppermute(block, ('row', 'col'), line_pairs(choose))  12.9 us
    ppermute x9, waiting for transfers between devices, across(): return lax.ppermute(block, 'row', [(i, i ^ bit) for i in range(8)])  11.8 us
    pallas_call x4, Pallas kernels, add(): pl.pallas_call(functools.partial(add_kernel, tuple(((weight, len(x)) for...  4.68 us
    ppermute x9, starting transfers between devices, across(): return lax.ppermute(block, 'row', [(i, i ^ bit) for i in range(8)])  4.19 us
  transfers between devices with their start and end apart: 15, of which 10 were waited for; matrix products, arithmetic and copies ran while one was open for 5% of the time, Pallas kernels for 26%

profile of v5, /device:TPU:10, one launch (start us, length us, event | category | flops | bytes accessed | tf_op | source)
XLA Modules:
  0.0 63.7 jit_solution(16176290198776222542)
XLA Ops:
  0.0 1.5 %collective-permute-start.1 = (bf16[2048,128]{1,0:T(8,128)(2,1)}, bf16[2048,128]{1,0:T(8,128)(2,1)S(1)}, u32[]{:S(2)}, u32[]{:S(2)}) collective-permute-start(bf16[2048,128]{1,0:T(8,128)(2,1)} %refs_0_.9), channel_id=1, source_target_pairs={{0,16},{4,20},{8,24},{12,28},{16,0},{20,4},{24,8},{28,12},{1,17},{... | collective-permute-start | bytes 1572872 | tf_op jit(solution)/shard_map/ppermute | solution.py:226
  1.5 0.5 collective-permute-start
  2.1 0.0 copy-start.1
  2.1 0.8 %dynamic-slice_bitcast_fusion = s32[10]{0:T(128)S(1)} fusion(s32[16,10]{1,0:T(8,128)} %constant.40.clone, s32[]{:T(128)S(6)} %select_n.15), kind=kLoop, calls=%fused_computation.2 | loop fusion | bytes 84 | tf_op jit(solution)/shard_map/squeeze | solution.py:247
  2.9 0.1 pad_add_fusion.facts
  3.0 0.0 collective-permute-start.2
  3.0 0.9 %convert_element_type.3 = bf16[8,16]{1,0:T(8,128)(2,1)S(1)} convert(s32[8,16]{1,0:T(8,128)} %param.6) | non-fusion elementwise | flops 128 | bytes 768 | tf_op jit(solution)/shard_map/convert_element_type | solution.py:23
  3.9 0.6 mul.15
  4.5 0.0 copy-done.1
  4.5 0.0 copy-start
  4.6 0.9 %bitcast_multiply_fusion.a_ref = bf16[1024,2048]{1,0:T(8,128)(2,1)S(1)} fusion(bf16[1024,2048]{1,0:T(8,128)(2,1)S(1)} %copy-done.1, bf16[128,8,16,128]{3,2,1,0:T(8,128)(2,1)S(1)} %bitcast.8), kind=kLoop, calls=%fused_computation | loop fusion | flops 2097152 | bytes 12582912 | tf_op jit(solution)/shard_map/mul | solution.py:24
  5.5 8.4 %collective-permute-done.1.refs_2_ = bf16[2048,128]{1,0:T(8,128)(2,1)S(1)} collective-permute-done((bf16[2048,128]{1,0:T(8,128)(2,1)}, bf16[2048,128]{1,0:T(8,128)(2,1)S(1)}, u32[]{:S(2)}, u32[]{:S(2)}) %collective-permute-start.1) | collective-permute-done | bytes 524320 | tf_op jit(solution)/shard_map/ppermute | solution.py:226
  13.9 1.2 %collective-permute-done.refs_1_ = bf16[2048,128]{1,0:T(8,128)(2,1)S(1)} collective-permute-done((bf16[2048,128]{1,0:T(8,128)(2,1)}, bf16[2048,128]{1,0:T(8,128)(2,1)S(1)}, u32[]{:S(2)}, u32[]{:S(2)}) %collective-permute-start) | collective-permute-done | bytes 524320 | tf_op jit(solution)/shard_map/ppermute | solution.py:226
  15.1 0.0 collective-permute-start.3
  15.1 0.5 collective-permute-start.4
  15.7 0.6 collective-permute-start.6
  16.3 0.5 collective-permute-start.7
  16.8 0.0 collective-permute-done.2.refs_3_.refs_5_
  16.8 0.2 collective-permute-done.3.refs_4_.refs_6_
  17.0 0.7 %collective-permute-done.4.refs_5_.refs_7_ = bf16[2048,128]{1,0:T(8,128)(2,1)S(1)} collective-permute-done((bf16[2048,128]{1,0:T(8,128)(2,1)S(1)}, bf16[2048,128]{1,0:T(8,128)(2,1)S(1)}, u32[]{:S(2)}, u32[]{:S(2)}) %collective-permute-start.4) | collective-permute-done | bytes 524320 | tf_op jit(solution)/shard_map/ppermute | solution.py:226
  17.8 0.0 copy-done
  17.8 2.5 %shard_map.46 = (s16[1040,128]{1,0:T(8,128)(2,1)S(1)}, s16[1040,128]{1,0:T(8,128)(2,1)S(1)}) custom-call(s32[12]{0:T(128)S(1)} %pad_add_fusion.facts, bf16[1024,2048]{1,0:T(8,128)(2,1)S(1)} %bitcast_multiply_fusion.a_ref, bf16[2048,128]{1,0:T(8,128)(2,1)S(1)} %copy-done, bf16[2048,128]{1,0:T(8,128)(2,1)S(1)} %collective-permute-done.refs_1_, ...), custom_call_target="tpu_custom_call" | custom-call | flops 3000000000 | bytes 9000000 | tf_op jit(solution)/shard_map/pallas_call | solution.py:130
  20.3 0.5 collective-permute-start.5
  20.8 2.2 %shard_map.47.refs_0_ = f32[1024,256]{1,0:T(8,128)S(1)} custom-call(s32[12]{0:T(128)S(1)} %pad_add_fusion.facts, bf16[1024,2048]{1,0:T(8,128)(2,1)S(1)} %bitcast_multiply_fusion.a_ref, bf16[2048,128]{1,0:T(8,128)(2,1)S(1)} %copy-done, bf16[2048,128]{1,0:T(8,128)(2,1)S(1)} %collective-permute-done.refs_1_, ...), custom_call_target="tpu_custom_call" | custom-call | flops 3000000000 | bytes 9000000 | tf_op jit(solution)/shard_map/pallas_call | solution.py:130
  23.0 1.2 %collective-permute-done.7.refs_4_ = bf16[1024,128]{1,0:T(8,128)(2,1)S(1)} collective-permute-done((bf16[1024,128]{1,0:T(8,128)(2,1)S(1)}, bf16[1024,128]{1,0:T(8,128)(2,1)S(1)}, u32[]{:S(2)}, u32[]{:S(2)}) %collective-permute-start.7) | collective-permute-done | bytes 262176 | tf_op jit(solution)/shard_map/ppermute | solution.py:226
  24.2 0.0 collective-permute-done.6.refs_3_
  24.2 0.0 collective-permute-start.8
  24.2 0.5 collective-permute-start.9
  24.7 0.5 collective-permute-start.10
  25.2 4.4 %collective-permute-done.5.refs_1_ = s16[1040,128]{1,0:T(8,128)(2,1)S(1)} collective-permute-done((s16[1040,128]{1,0:T(8,128)(2,1)S(1)}, s16[1040,128]{1,0:T(8,128)(2,1)S(1)}, u32[]{:S(2)}, u32[]{:S(2)}) %collective-permute-start.5) | collective-permute-done | bytes 266272 | tf_op jit(solution)/shard_map/ppermute | solution.py:229
  29.6 0.0 collective-permute-done.8.refs_8_
  29.6 0.0 collective-permute-done.9.refs_9_
  29.6 2.4 %shard_map.48 = s16[1040,256]{1,0:T(8,128)(2,1)S(1)} custom-call(s32[12]{0:T(128)S(1)} %pad_add_fusion.facts, bf16[1024,2048]{1,0:T(8,128)(2,1)S(1)} %bitcast_multiply_fusion.a_ref, bf16[2048,128]{1,0:T(8,128)(2,1)S(1)} %copy-done, bf16[2048,128]{1,0:T(8,128)(2,1)S(1)} %collective-permute-done.refs_1_, bf16[2048,128]{1,0:T(8,128)(2,1)S(1)} %collective-permute-done.1.refs_2_, ...), custom_call_target="tpu_custom_call" | custom-call | flops 3000000000 | bytes 9000000 | tf_op jit(solution)/shard_map/pallas_call | solution.py:130
  32.0 1.3 %collective-permute-start.11 = (s16[1040,256]{1,0:T(8,128)(2,1)S(1)}, s16[1040,256]{1,0:T(8,128)(2,1)S(1)}, u32[]{:S(2)}, u32[]{:S(2)}) collective-permute-start(s16[1040,256]{1,0:T(8,128)(2,1)S(1)} %shard_map.48), channel_id=1, source_target_pairs={{0,1},{3,2},{2,3},{4,5},{7,6},{6,7},{8,9},{11,10},{12,13},{15,14},... | collective-permute-start | bytes 1597448 | tf_op jit(solution)/shard_map/ppermute | solution.py:229
  33.3 1.2 %collective-permute-done.10.refs_2_ = s16[1040,128]{1,0:T(8,128)(2,1)S(1)} collective-permute-done((s16[1040,128]{1,0:T(8,128)(2,1)S(1)}, s16[1040,128]{1,0:T(8,128)(2,1)S(1)}, u32[]{:S(2)}, u32[]{:S(2)}) %collective-permute-start.10) | collective-permute-done | bytes 266272 | tf_op jit(solution)/shard_map/ppermute | solution.py:229
  34.5 1.0 %shard_map.49 = s16[1040,256]{1,0:T(8,128)(2,1)S(1)} custom-call(s32[12]{0:T(128)S(1)} %pad_add_fusion.facts, f32[1024,256]{1,0:T(8,128)S(1)} %shard_map.47.refs_0_, s16[1040,128]{1,0:T(8,128)(2,1)S(1)} %collective-permute-done.5.refs_1_, s16[1040,128]{1,0:T(8,128)(2,1)S(1)} %collective-permute-done.10.refs_2_), custom_call_target="tpu_custom_call" | custom-call | flops 3000000000 | bytes 9000000 | tf_op jit(solution)/shard_map/pallas_call | solution.py:179
  35.4 4.5 %collective-permute-start.12 = (s16[1040,256]{1,0:T(8,128)(2,1)S(1)}, s16[1040,256]{1,0:T(8,128)(2,1)S(1)}, u32[]{:S(2)}, u32[]{:S(2)}) collective-permute-start(s16[1040,256]{1,0:T(8,128)(2,1)S(1)} %shard_map.49), channel_id=1, source_target_pairs={{1,2},{2,0},{5,6},{6,4},{9,11},{10,8},{13,15},{14,12},{17,19},{18,... | collective-permute-start | bytes 1597448 | tf_op jit(solution)/shard_map/ppermute | solution.py:229
  40.0 3.7 %shard_map.50 = (s16[1040,256]{1,0:T(8,128)(2,1)S(1)}, f32[1024,256]{1,0:T(8,128)S(1)}) custom-call(s32[12]{0:T(128)S(1)} %pad_add_fusion.facts, bf16[1024,2048]{1,0:T(8,128)(2,1)S(1)} %bitcast_multiply_fusion.a_ref, bf16[2048,128]{1,0:T(8,128)(2,1)S(1)} %copy-done, bf16[2048,128]{1,0:T(8,128)(2,1)S(1)} %collective-permute-done.refs_1_, ...), custom_call_target="tpu_custom_call" | custom-call | flops 3000000000 | bytes 9000000 | tf_op jit(solution)/shard_map/pallas_call | solution.py:130
  43.7 1.3 %collective-permute-start.13 = (s16[1040,256]{1,0:T(8,128)(2,1)S(1)}, s16[1040,256]{1,0:T(8,128)(2,1)S(1)}, u32[]{:S(2)}, u32[]{:S(2)}) collective-permute-start(s16[1040,256]{1,0:T(8,128)(2,1)S(1)} %get-tuple-element.31), channel_id=1, source_target_pairs={{0,1},{3,2},{4,5},{7,6},{8,9},{11,10},{12,13},{15,14},{16,17},{19,... | collective-permute-start | bytes 1597448 | tf_op jit(solution)/shard_map/ppermute | solution.py:229
  45.0 1.3 %collective-permute-done.11.refs_1_.refs_3_ = s16[1040,256]{1,0:T(8,128)(2,1)S(1)} collective-permute-done((s16[1040,256]{1,0:T(8,128)(2,1)S(1)}, s16[1040,256]{1,0:T(8,128)(2,1)S(1)}, u32[]{:S(2)}, u32[]{:S(2)}) %collective-permute-start.11) | collective-permute-done | bytes 532512 | tf_op jit(solution)/shard_map/ppermute | solution.py:229
  46.4 1.0 %shard_map.51 = s16[1040,256]{1,0:T(8,128)(2,1)S(1)} custom-call(s32[12]{0:T(128)S(1)} %pad_add_fusion.facts, f32[1024,256]{1,0:T(8,128)S(1)} %get-tuple-element.33.refs_0_, s16[1040,256]{1,0:T(8,128)(2,1)S(1)} %collective-permute-done.11.refs_1_.refs_3_), custom_call_target="tpu_custom_call" | custom-call | flops 3000000000 | bytes 9000000 | tf_op jit(solution)/shard_map/pallas_call | solution.py:179
  47.3 4.8 %collective-permute-start.14 = (s16[1040,256]{1,0:T(8,128)(2,1)S(1)}, s16[1040,256]{1,0:T(8,128)(2,1)S(1)}, u32[]{:S(2)}, u32[]{:S(2)}) collective-permute-start(s16[1040,256]{1,0:T(8,128)(2,1)S(1)} %shard_map.51), channel_id=1, source_target_pairs={{1,3},{2,1},{5,7},{6,5},{9,10},{10,9},{13,14},{14,13},{17,18},{18,... | collective-permute-start | bytes 1597448 | tf_op jit(solution)/shard_map/ppermute | solution.py:229
  52.2 2.2 %shard_map.52.refs_0_ = f32[1024,256]{1,0:T(8,128)S(1)} custom-call(s32[12]{0:T(128)S(1)} %pad_add_fusion.facts, bf16[1024,2048]{1,0:T(8,128)(2,1)S(1)} %bitcast_multiply_fusion.a_ref, bf16[2048,128]{1,0:T(8,128)(2,1)S(1)} %copy-done, bf16[2048,128]{1,0:T(8,128)(2,1)S(1)} %collective-permute-done.refs_1_, ...), custom_call_target="tpu_custom_call" | custom-call | flops 3000000000 | bytes 9000000 | tf_op jit(solution)/shard_map/pallas_call | solution.py:130
  54.4 0.0 collective-permute-done.12.refs_4_
  54.4 4.2 %collective-permute-done.13.refs_5_ = s16[1040,256]{1,0:T(8,128)(2,1)S(1)} collective-permute-done((s16[1040,256]{1,0:T(8,128)(2,1)S(1)}, s16[1040,256]{1,0:T(8,128)(2,1)S(1)}, u32[]{:S(2)}, u32[]{:S(2)}) %collective-permute-start.13) | collective-permute-done | bytes 532512 | tf_op jit(solution)/shard_map/ppermute | solution.py:229
  58.6 1.2 %shard_map.53.refs_0_ = f32[1024,256]{1,0:T(8,128)S(1)} custom-call(s32[12]{0:T(128)S(1)} %pad_add_fusion.facts, f32[1024,256]{1,0:T(8,128)S(1)} %shard_map.52.refs_0_, s16[1040,128]{1,0:T(8,128)(2,1)S(1)} %collective-permute-done.5.refs_1_, s16[1040,128]{1,0:T(8,128)(2,1)S(1)} %collective-permute-done.10.refs_2_, ...), custom_call_target="tpu_custom_call" | custom-call | flops 3000000000 | bytes 9000000 | tf_op jit(solution)/shard_map/pallas_call | solution.py:179
  59.9 2.3 %collective-permute-done.14.refs_1_ = s16[1040,256]{1,0:T(8,128)(2,1)S(1)} collective-permute-done((s16[1040,256]{1,0:T(8,128)(2,1)S(1)}, s16[1040,256]{1,0:T(8,128)(2,1)S(1)}, u32[]{:S(2)}, u32[]{:S(2)}) %collective-permute-start.14) | collective-permute-done | bytes 532512 | tf_op jit(solution)/shard_map/ppermute | solution.py:229
  62.2 1.5 %shard_map.54 = bf16[1024,256]{1,0:T(8,128)(2,1)} custom-call(s32[12]{0:T(128)S(1)} %pad_add_fusion.facts, f32[1024,256]{1,0:T(8,128)S(1)} %shard_map.53.refs_0_, s16[1040,256]{1,0:T(8,128)(2,1)S(1)} %collective-permute-done.14.refs_1_), custom_call_target="tpu_custom_call" | custom-call | flops 3000000000 | bytes 9000000 | tf_op jit(solution)/shard_map/pallas_call | solution.py:179
  (2 shorter events, 0.0 us)
Async XLA Ops:
  0.0 13.9 %collective-permute-start.1 = (bf16[2048,128]{1,0:T(8,128)(2,1)}, bf16[2048,128]{1,0:T(8,128)(2,1)S(1)}, u32[]{:S(2)}, u32[]{:S(2)}) collective-permute-start(bf16[2048,128]{1,0:T(8,128)(2,1)} %refs_0_.9), channel_id=1, source_target_pairs={{0,16},{4,20},{8,24},{12,28},{16,0},{20,4},{24,8},{28,12},{1,17},{... | collective-permute-start | bytes 1572872 | tf_op jit(solution)/shard_map/ppermute | solution.py:226
  1.5 13.6 %collective-permute-start = (bf16[2048,128]{1,0:T(8,128)(2,1)}, bf16[2048,128]{1,0:T(8,128)(2,1)S(1)}, u32[]{:S(2)}, u32[]{:S(2)}) collective-permute-start(bf16[2048,128]{1,0:T(8,128)(2,1)} %refs_0_.9), channel_id=1, source_target_pairs={{0,8},{4,12},{8,0},{12,4},{16,24},{20,28},{24,16},{28,20},{1,9},{5... | collective-permute-start | bytes 1572872 | tf_op jit(solution)/shard_map/ppermute | solution.py:226
  2.1 2.5 %copy-start.1 = (bf16[1024,2048]{1,0:T(8,128)(2,1)S(1)}, bf16[1024,2048]{1,0:T(8,128)(2,1)}, u32[]{:S(2)}) copy-start(bf16[1024,2048]{1,0:T(8,128)(2,1)} %param.4) | copy-start | bytes 12582916
  3.0 13.8 %collective-permute-start.2 = (bf16[2048,128]{1,0:T(8,128)(2,1)}, bf16[2048,128]{1,0:T(8,128)(2,1)S(1)}, u32[]{:S(2)}, u32[]{:S(2)}) collective-permute-start(bf16[2048,128]{1,0:T(8,128)(2,1)} %refs_0_.9), channel_id=1, source_target_pairs={{0,4},{4,0},{8,12},{12,8},{16,20},{20,16},{24,28},{28,24},{1,5},{5... | collective-permute-start | bytes 1572872 | tf_op jit(solution)/shard_map/ppermute | solution.py:226
  4.5 13.2 %copy-start = (bf16[2048,128]{1,0:T(8,128)(2,1)S(1)}, bf16[2048,128]{1,0:T(8,128)(2,1)}, u32[]{:S(2)}) copy-start(bf16[2048,128]{1,0:T(8,128)(2,1)} %refs_0_.9) | copy-start | bytes 1572868
  15.1 1.9 %collective-permute-start.3 = (bf16[2048,128]{1,0:T(8,128)(2,1)S(1)}, bf16[2048,128]{1,0:T(8,128)(2,1)S(1)}, u32[]{:S(2)}, u32[]{:S(2)}) collective-permute-start(bf16[2048,128]{1,0:T(8,128)(2,1)S(1)} %collective-permute-done.refs_1_), channel_id=1, source_target_pairs={{0,4},{4,0},{8,12},{12,8},{16,20},{20,16},{24,28},{28,24},{1,5},{5... | collective-permute-start | bytes 1572872 | tf_op jit(solution)/shard_map/ppermute | solution.py:226
  15.1 2.7 %collective-permute-start.4 = (bf16[2048,128]{1,0:T(8,128)(2,1)S(1)}, bf16[2048,128]{1,0:T(8,128)(2,1)S(1)}, u32[]{:S(2)}, u32[]{:S(2)}) collective-permute-start(bf16[2048,128]{1,0:T(8,128)(2,1)S(1)} %collective-permute-done.1.refs_2_), channel_id=1, source_target_pairs={{0,4},{4,0},{8,12},{12,8},{16,20},{20,16},{24,28},{28,24},{1,5},{5... | collective-permute-start | bytes 1572872 | tf_op jit(solution)/shard_map/ppermute | solution.py:226
  15.7 8.5 %collective-permute-start.6 = (bf16[1024,128]{1,0:T(8,128)(2,1)S(1)}, bf16[1024,128]{1,0:T(8,128)(2,1)S(1)}, u32[]{:S(2)}, u32[]{:S(2)}) collective-permute-start(bf16[1024,128]{1,0:T(8,128)(2,1)S(1)} %slice.6), channel_id=1, source_target_pairs={{0,8},{4,12},{8,0},{12,4},{16,24},{20,28},{24,16},{28,20},{1,9},{5... | collective-permute-start | bytes 786440 | tf_op jit(solution)/shard_map/ppermute | solution.py:226
  16.3 7.9 %collective-permute-start.7 = (bf16[1024,128]{1,0:T(8,128)(2,1)S(1)}, bf16[1024,128]{1,0:T(8,128)(2,1)S(1)}, u32[]{:S(2)}, u32[]{:S(2)}) collective-permute-start(bf16[1024,128]{1,0:T(8,128)(2,1)S(1)} %slice.7), channel_id=1, source_target_pairs={{0,16},{4,20},{8,24},{12,28},{16,0},{20,4},{24,8},{28,12},{1,17},{... | collective-permute-start | bytes 786440 | tf_op jit(solution)/shard_map/ppermute | solution.py:226
  20.3 9.3 %collective-permute-start.5 = (s16[1040,128]{1,0:T(8,128)(2,1)S(1)}, s16[1040,128]{1,0:T(8,128)(2,1)S(1)}, u32[]{:S(2)}, u32[]{:S(2)}) collective-permute-start(s16[1040,128]{1,0:T(8,128)(2,1)S(1)} %get-tuple-element.25), channel_id=1, source_target_pairs={{0,1},{1,0},{2,3},{3,2},{4,5},{5,4},{6,7},{7,6},{8,9},{9,8},{10,11... | collective-permute-start | bytes 798728 | tf_op jit(solution)/shard_map/ppermute | solution.py:229
  24.2 5.4 %collective-permute-start.8 = (bf16[1024,128]{1,0:T(8,128)(2,1)S(1)}, bf16[1024,128]{1,0:T(8,128)(2,1)S(1)}, u32[]{:S(2)}, u32[]{:S(2)}) collective-permute-start(bf16[1024,128]{1,0:T(8,128)(2,1)S(1)} %collective-permute-done.6.refs_3_), channel_id=1, source_target_pairs={{0,4},{4,0},{8,12},{12,8},{16,20},{20,16},{24,28},{28,24},{1,5},{5... | collective-permute-start | bytes 786440 | tf_op jit(solution)/shard_map/ppermute | solution.py:226
  24.2 5.4 %collective-permute-start.9 = (bf16[1024,128]{1,0:T(8,128)(2,1)S(1)}, bf16[1024,128]{1,0:T(8,128)(2,1)S(1)}, u32[]{:S(2)}, u32[]{:S(2)}) collective-permute-start(bf16[1024,128]{1,0:T(8,128)(2,1)S(1)} %collective-permute-done.7.refs_4_), channel_id=1, source_target_pairs={{0,4},{4,0},{8,12},{12,8},{16,20},{20,16},{24,28},{28,24},{1,5},{5... | collective-permute-start | bytes 786440 | tf_op jit(solution)/shard_map/ppermute | solution.py:226
  24.7 9.7 %collective-permute-start.10 = (s16[1040,128]{1,0:T(8,128)(2,1)S(1)}, s16[1040,128]{1,0:T(8,128)(2,1)S(1)}, u32[]{:S(2)}, u32[]{:S(2)}) collective-permute-start(s16[1040,128]{1,0:T(8,128)(2,1)S(1)} %get-tuple-element.23), channel_id=1, source_target_pairs={{0,1},{1,0},{2,3},{3,2},{4,5},{5,4},{6,7},{7,6},{8,9},{9,8},{10,11... | collective-permute-start | bytes 798728 | tf_op jit(solution)/shard_map/ppermute | solution.py:229
  32.0 14.4 %collective-permute-start.11 = (s16[1040,256]{1,0:T(8,128)(2,1)S(1)}, s16[1040,256]{1,0:T(8,128)(2,1)S(1)}, u32[]{:S(2)}, u32[]{:S(2)}) collective-permute-start(s16[1040,256]{1,0:T(8,128)(2,1)S(1)} %shard_map.48), channel_id=1, source_target_pairs={{0,1},{3,2},{2,3},{4,5},{7,6},{6,7},{8,9},{11,10},{12,13},{15,14},... | collective-permute-start | bytes 1597448 | tf_op jit(solution)/shard_map/ppermute | solution.py:229
  35.4 19.0 %collective-permute-start.12 = (s16[1040,256]{1,0:T(8,128)(2,1)S(1)}, s16[1040,256]{1,0:T(8,128)(2,1)S(1)}, u32[]{:S(2)}, u32[]{:S(2)}) collective-permute-start(s16[1040,256]{1,0:T(8,128)(2,1)S(1)} %shard_map.49), channel_id=1, source_target_pairs={{1,2},{2,0},{5,6},{6,4},{9,11},{10,8},{13,15},{14,12},{17,19},{18,... | collective-permute-start | bytes 1597448 | tf_op jit(solution)/shard_map/ppermute | solution.py:229
  43.7 14.9 %collective-permute-start.13 = (s16[1040,256]{1,0:T(8,128)(2,1)S(1)}, s16[1040,256]{1,0:T(8,128)(2,1)S(1)}, u32[]{:S(2)}, u32[]{:S(2)}) collective-permute-start(s16[1040,256]{1,0:T(8,128)(2,1)S(1)} %get-tuple-element.31), channel_id=1, source_target_pairs={{0,1},{3,2},{4,5},{7,6},{8,9},{11,10},{12,13},{15,14},{16,17},{19,... | collective-permute-start | bytes 1597448 | tf_op jit(solution)/shard_map/ppermute | solution.py:229
  47.3 14.8 %collective-permute-start.14 = (s16[1040,256]{1,0:T(8,128)(2,1)S(1)}, s16[1040,256]{1,0:T(8,128)(2,1)S(1)}, u32[]{:S(2)}, u32[]{:S(2)}) collective-permute-start(s16[1040,256]{1,0:T(8,128)(2,1)S(1)} %shard_map.51), channel_id=1, source_target_pairs={{1,3},{2,1},{5,7},{6,5},{9,10},{10,9},{13,14},{14,13},{17,18},{18,... | collective-permute-start | bytes 1597448 | tf_op jit(solution)/shard_map/ppermute | solution.py:229

commit v6 on v5

--- a/solution.py
+++ b/solution.py
@@ -12,7 +12,7 @@
 LEVELS = 32767.0
 STEPS_PER_OCTAVE = 64.0
 BLOCK_ROWS = 512
-ADD_ROWS = 512
+ADD_ROWS = 256
 
 
 def apply_mask(amplitudes, tile_mask):

time: 64.8 us -> 65.4 us (level)
  Pallas kernels: 17.7 us -> 18.4 us
  transfers between devices with their start and end apart: 15 -> 15, of which waited for: 10 -> 10; matrix products, arithmetic and copies ran while one was open for 5% -> 5% of each run, Pallas kernels for 26% -> 25%
where the time goes in v6:
time: 65.4 us; the launch traced here: 64.3 us
  waiting for transfers between devices  25.2 us (39%)
  Pallas kernels  18.4 us (28%)
  starting transfers between devices  17.1 us (26%)
  other arithmetic  1.91 us (3%)
  local copies, waits for them, and re-layouts  1.5 us (2%)
    ppermute x6, waiting for transfers between devices, along(): return lax.ppermute(block, ('row', 'col'), line_pairs(choose))  13.4 us
    pallas_call x5, Pallas kernels, multiply(): pl.pallas_call(functools.partial(multiply_kernel, slots, kinds, rows, wid...  13.1 us
    ppermute x6, starting transfers between devices, along(): return lax.ppermute(block, ('row', 'col'), line_pairs(choose))  12.9 us
    ppermute x9, waiting for transfers between devices, across(): return lax.ppermute(block, 'row', [(i, i ^ bit) for i in range(8)])  11.8 us
    pallas_call x4, Pallas kernels, add(): pl.pallas_call(functools.partial(add_kernel, tuple(((weight, len(x)) for...  5.32 us
    ppermute x9, starting transfers between devices, across(): return lax.ppermute(block, 'row', [(i, i ^ bit) for i in range(8)])  4.19 us
  transfers between devices with their start and end apart: 15, of which 10 were waited for; matrix products, arithmetic and copies ran while one was open for 5% of the time, Pallas kernels for 25%

profile of v6, /device:TPU:10, one launch (start us, length us, event | category | flops | bytes accessed | tf_op | source)
XLA Modules:
  0.0 64.3 jit_solution(14909841010453542297)
XLA Ops:
  0.0 1.5 %collective-permute-start.1 = (bf16[2048,128]{1,0:T(8,128)(2,1)}, bf16[2048,128]{1,0:T(8,128)(2,1)S(1)}, u32[]{:S(2)}, u32[]{:S(2)}) collective-permute-start(bf16[2048,128]{1,0:T(8,128)(2,1)} %refs_0_.9), channel_id=1, source_target_pairs={{0,16},{4,20},{8,24},{12,28},{16,0},{20,4},{24,8},{28,12},{1,17},{... | collective-permute-start | bytes 1572872 | tf_op jit(solution)/shard_map/ppermute | solution.py:226
  1.5 0.5 collective-permute-start
  2.1 0.0 copy-start.1
  2.1 0.8 %dynamic-slice_bitcast_fusion = s32[10]{0:T(128)S(1)} fusion(s32[16,10]{1,0:T(8,128)} %constant.40.clone, s32[]{:T(128)S(6)} %select_n.15), kind=kLoop, calls=%fused_computation.2 | loop fusion | bytes 84 | tf_op jit(solution)/shard_map/squeeze | solution.py:247
  2.9 0.1 pad_add_fusion.facts
  3.0 0.0 collective-permute-start.2
  3.0 0.9 %convert_element_type.3 = bf16[8,16]{1,0:T(8,128)(2,1)S(1)} convert(s32[8,16]{1,0:T(8,128)} %param.6) | non-fusion elementwise | flops 128 | bytes 768 | tf_op jit(solution)/shard_map/convert_element_type | solution.py:23
  3.9 0.6 mul.15
  4.5 0.0 copy-done.1
  4.5 0.0 copy-start
  4.6 0.9 %bitcast_multiply_fusion.a_ref = bf16[1024,2048]{1,0:T(8,128)(2,1)S(1)} fusion(bf16[1024,2048]{1,0:T(8,128)(2,1)S(1)} %copy-done.1, bf16[128,8,16,128]{3,2,1,0:T(8,128)(2,1)S(1)} %bitcast.8), kind=kLoop, calls=%fused_computation | loop fusion | flops 2097152 | bytes 12582912 | tf_op jit(solution)/shard_map/mul | solution.py:24
  5.5 8.4 %collective-permute-done.1.refs_2_ = bf16[2048,128]{1,0:T(8,128)(2,1)S(1)} collective-permute-done((bf16[2048,128]{1,0:T(8,128)(2,1)}, bf16[2048,128]{1,0:T(8,128)(2,1)S(1)}, u32[]{:S(2)}, u32[]{:S(2)}) %collective-permute-start.1) | collective-permute-done | bytes 524320 | tf_op jit(solution)/shard_map/ppermute | solution.py:226
  13.9 1.2 %collective-permute-done.refs_1_ = bf16[2048,128]{1,0:T(8,128)(2,1)S(1)} collective-permute-done((bf16[2048,128]{1,0:T(8,128)(2,1)}, bf16[2048,128]{1,0:T(8,128)(2,1)S(1)}, u32[]{:S(2)}, u32[]{:S(2)}) %collective-permute-start) | collective-permute-done | bytes 524320 | tf_op jit(solution)/shard_map/ppermute | solution.py:226
  15.1 0.0 collective-permute-start.3
  15.1 0.5 collective-permute-start.4
  15.7 0.6 collective-permute-start.6
  16.3 0.5 collective-permute-start.7
  16.8 0.0 collective-permute-done.2.refs_3_.refs_5_
  16.8 0.2 collective-permute-done.3.refs_4_.refs_6_
  17.0 0.7 %collective-permute-done.4.refs_5_.refs_7_ = bf16[2048,128]{1,0:T(8,128)(2,1)S(1)} collective-permute-done((bf16[2048,128]{1,0:T(8,128)(2,1)S(1)}, bf16[2048,128]{1,0:T(8,128)(2,1)S(1)}, u32[]{:S(2)}, u32[]{:S(2)}) %collective-permute-start.4) | collective-permute-done | bytes 524320 | tf_op jit(solution)/shard_map/ppermute | solution.py:226
  17.8 0.0 copy-done
  17.8 2.5 %shard_map.46 = (s16[1040,128]{1,0:T(8,128)(2,1)S(1)}, s16[1040,128]{1,0:T(8,128)(2,1)S(1)}) custom-call(s32[12]{0:T(128)S(1)} %pad_add_fusion.facts, bf16[1024,2048]{1,0:T(8,128)(2,1)S(1)} %bitcast_multiply_fusion.a_ref, bf16[2048,128]{1,0:T(8,128)(2,1)S(1)} %copy-done, bf16[2048,128]{1,0:T(8,128)(2,1)S(1)} %collective-permute-done.refs_1_, ...), custom_call_target="tpu_custom_call" | custom-call | flops 3000000000 | bytes 9000000 | tf_op jit(solution)/shard_map/pallas_call | solution.py:130
  20.3 0.5 collective-permute-start.5
  20.8 2.2 %shard_map.47.refs_0_ = f32[1024,256]{1,0:T(8,128)S(1)} custom-call(s32[12]{0:T(128)S(1)} %pad_add_fusion.facts, bf16[1024,2048]{1,0:T(8,128)(2,1)S(1)} %bitcast_multiply_fusion.a_ref, bf16[2048,128]{1,0:T(8,128)(2,1)S(1)} %copy-done, bf16[2048,128]{1,0:T(8,128)(2,1)S(1)} %collective-permute-done.refs_1_, ...), custom_call_target="tpu_custom_call" | custom-call | flops 3000000000 | bytes 9000000 | tf_op jit(solution)/shard_map/pallas_call | solution.py:130
  23.0 1.2 %collective-permute-done.7.refs_4_ = bf16[1024,128]{1,0:T(8,128)(2,1)S(1)} collective-permute-done((bf16[1024,128]{1,0:T(8,128)(2,1)S(1)}, bf16[1024,128]{1,0:T(8,128)(2,1)S(1)}, u32[]{:S(2)}, u32[]{:S(2)}) %collective-permute-start.7) | collective-permute-done | bytes 262176 | tf_op jit(solution)/shard_map/ppermute | solution.py:226
  24.2 0.0 collective-permute-done.6.refs_3_
  24.2 0.0 collective-permute-start.8
  24.2 0.5 collective-permute-start.9
  24.7 0.5 collective-permute-start.10
  25.2 4.4 %collective-permute-done.5.refs_1_ = s16[1040,128]{1,0:T(8,128)(2,1)S(1)} collective-permute-done((s16[1040,128]{1,0:T(8,128)(2,1)S(1)}, s16[1040,128]{1,0:T(8,128)(2,1)S(1)}, u32[]{:S(2)}, u32[]{:S(2)}) %collective-permute-start.5) | collective-permute-done | bytes 266272 | tf_op jit(solution)/shard_map/ppermute | solution.py:229
  29.6 0.0 collective-permute-done.8.refs_8_
  29.6 0.0 collective-permute-done.9.refs_9_
  29.6 2.4 %shard_map.48 = s16[1040,256]{1,0:T(8,128)(2,1)S(1)} custom-call(s32[12]{0:T(128)S(1)} %pad_add_fusion.facts, bf16[1024,2048]{1,0:T(8,128)(2,1)S(1)} %bitcast_multiply_fusion.a_ref, bf16[2048,128]{1,0:T(8,128)(2,1)S(1)} %copy-done, bf16[2048,128]{1,0:T(8,128)(2,1)S(1)} %collective-permute-done.refs_1_, bf16[2048,128]{1,0:T(8,128)(2,1)S(1)} %collective-permute-done.1.refs_2_, ...), custom_call_target="tpu_custom_call" | custom-call | flops 3000000000 | bytes 9000000 | tf_op jit(solution)/shard_map/pallas_call | solution.py:130
  32.0 1.3 %collective-permute-start.11 = (s16[1040,256]{1,0:T(8,128)(2,1)S(1)}, s16[1040,256]{1,0:T(8,128)(2,1)S(1)}, u32[]{:S(2)}, u32[]{:S(2)}) collective-permute-start(s16[1040,256]{1,0:T(8,128)(2,1)S(1)} %shard_map.48), channel_id=1, source_target_pairs={{0,1},{3,2},{2,3},{4,5},{7,6},{6,7},{8,9},{11,10},{12,13},{15,14},... | collective-permute-start | bytes 1597448 | tf_op jit(solution)/shard_map/ppermute | solution.py:229
  33.3 1.2 %collective-permute-done.10.refs_2_ = s16[1040,128]{1,0:T(8,128)(2,1)S(1)} collective-permute-done((s16[1040,128]{1,0:T(8,128)(2,1)S(1)}, s16[1040,128]{1,0:T(8,128)(2,1)S(1)}, u32[]{:S(2)}, u32[]{:S(2)}) %collective-permute-start.10) | collective-permute-done | bytes 266272 | tf_op jit(solution)/shard_map/ppermute | solution.py:229
  34.5 1.0 %shard_map.49 = s16[1040,256]{1,0:T(8,128)(2,1)S(1)} custom-call(s32[12]{0:T(128)S(1)} %pad_add_fusion.facts, f32[1024,256]{1,0:T(8,128)S(1)} %shard_map.47.refs_0_, s16[1040,128]{1,0:T(8,128)(2,1)S(1)} %collective-permute-done.5.refs_1_, s16[1040,128]{1,0:T(8,128)(2,1)S(1)} %collective-permute-done.10.refs_2_), custom_call_target="tpu_custom_call" | custom-call | flops 3000000000 | bytes 9000000 | tf_op jit(solution)/shard_map/pallas_call | solution.py:179
  35.5 4.5 %collective-permute-start.12 = (s16[1040,256]{1,0:T(8,128)(2,1)S(1)}, s16[1040,256]{1,0:T(8,128)(2,1)S(1)}, u32[]{:S(2)}, u32[]{:S(2)}) collective-permute-start(s16[1040,256]{1,0:T(8,128)(2,1)S(1)} %shard_map.49), channel_id=1, source_target_pairs={{1,2},{2,0},{5,6},{6,4},{9,11},{10,8},{13,15},{14,12},{17,19},{18,... | collective-permute-start | bytes 1597448 | tf_op jit(solution)/shard_map/ppermute | solution.py:229
  40.0 3.7 %shard_map.50 = (s16[1040,256]{1,0:T(8,128)(2,1)S(1)}, f32[1024,256]{1,0:T(8,128)S(1)}) custom-call(s32[12]{0:T(128)S(1)} %pad_add_fusion.facts, bf16[1024,2048]{1,0:T(8,128)(2,1)S(1)} %bitcast_multiply_fusion.a_ref, bf16[2048,128]{1,0:T(8,128)(2,1)S(1)} %copy-done, bf16[2048,128]{1,0:T(8,128)(2,1)S(1)} %collective-permute-done.refs_1_, ...), custom_call_target="tpu_custom_call" | custom-call | flops 3000000000 | bytes 9000000 | tf_op jit(solution)/shard_map/pallas_call | solution.py:130
  43.8 1.3 %collective-permute-start.13 = (s16[1040,256]{1,0:T(8,128)(2,1)S(1)}, s16[1040,256]{1,0:T(8,128)(2,1)S(1)}, u32[]{:S(2)}, u32[]{:S(2)}) collective-permute-start(s16[1040,256]{1,0:T(8,128)(2,1)S(1)} %get-tuple-element.31), channel_id=1, source_target_pairs={{0,1},{3,2},{4,5},{7,6},{8,9},{11,10},{12,13},{15,14},{16,17},{19,... | collective-permute-start | bytes 1597448 | tf_op jit(solution)/shard_map/ppermute | solution.py:229
  45.1 1.3 %collective-permute-done.11.refs_1_.refs_3_ = s16[1040,256]{1,0:T(8,128)(2,1)S(1)} collective-permute-done((s16[1040,256]{1,0:T(8,128)(2,1)S(1)}, s16[1040,256]{1,0:T(8,128)(2,1)S(1)}, u32[]{:S(2)}, u32[]{:S(2)}) %collective-permute-start.11) | collective-permute-done | bytes 532512 | tf_op jit(solution)/shard_map/ppermute | solution.py:229
  46.4 1.0 %shard_map.51 = s16[1040,256]{1,0:T(8,128)(2,1)S(1)} custom-call(s32[12]{0:T(128)S(1)} %pad_add_fusion.facts, f32[1024,256]{1,0:T(8,128)S(1)} %get-tuple-element.33.refs_0_, s16[1040,256]{1,0:T(8,128)(2,1)S(1)} %collective-permute-done.11.refs_1_.refs_3_), custom_call_target="tpu_custom_call" | custom-call | flops 3000000000 | bytes 9000000 | tf_op jit(solution)/shard_map/pallas_call | solution.py:179
  47.4 4.8 %collective-permute-start.14 = (s16[1040,256]{1,0:T(8,128)(2,1)S(1)}, s16[1040,256]{1,0:T(8,128)(2,1)S(1)}, u32[]{:S(2)}, u32[]{:S(2)}) collective-permute-start(s16[1040,256]{1,0:T(8,128)(2,1)S(1)} %shard_map.51), channel_id=1, source_target_pairs={{1,3},{2,1},{5,7},{6,5},{9,10},{10,9},{13,14},{14,13},{17,18},{18,... | collective-permute-start | bytes 1597448 | tf_op jit(solution)/shard_map/ppermute | solution.py:229
  52.2 2.2 %shard_map.52.refs_0_ = f32[1024,256]{1,0:T(8,128)S(1)} custom-call(s32[12]{0:T(128)S(1)} %pad_add_fusion.facts, bf16[1024,2048]{1,0:T(8,128)(2,1)S(1)} %bitcast_multiply_fusion.a_ref, bf16[2048,128]{1,0:T(8,128)(2,1)S(1)} %copy-done, bf16[2048,128]{1,0:T(8,128)(2,1)S(1)} %collective-permute-done.refs_1_, ...), custom_call_target="tpu_custom_call" | custom-call | flops 3000000000 | bytes 9000000 | tf_op jit(solution)/shard_map/pallas_call | solution.py:130
  54.4 0.0 collective-permute-done.12.refs_4_
  54.4 4.3 %collective-permute-done.13.refs_5_ = s16[1040,256]{1,0:T(8,128)(2,1)S(1)} collective-permute-done((s16[1040,256]{1,0:T(8,128)(2,1)S(1)}, s16[1040,256]{1,0:T(8,128)(2,1)S(1)}, u32[]{:S(2)}, u32[]{:S(2)}) %collective-permute-start.13) | collective-permute-done | bytes 532512 | tf_op jit(solution)/shard_map/ppermute | solution.py:229
  58.7 1.3 %shard_map.53.refs_0_ = f32[1024,256]{1,0:T(8,128)S(1)} custom-call(s32[12]{0:T(128)S(1)} %pad_add_fusion.facts, f32[1024,256]{1,0:T(8,128)S(1)} %shard_map.52.refs_0_, s16[1040,128]{1,0:T(8,128)(2,1)S(1)} %collective-permute-done.5.refs_1_, s16[1040,128]{1,0:T(8,128)(2,1)S(1)} %collective-permute-done.10.refs_2_, ...), custom_call_target="tpu_custom_call" | custom-call | flops 3000000000 | bytes 9000000 | tf_op jit(solution)/shard_map/pallas_call | solution.py:179
  60.0 2.2 %collective-permute-done.14.refs_1_ = s16[1040,256]{1,0:T(8,128)(2,1)S(1)} collective-permute-done((s16[1040,256]{1,0:T(8,128)(2,1)S(1)}, s16[1040,256]{1,0:T(8,128)(2,1)S(1)}, u32[]{:S(2)}, u32[]{:S(2)}) %collective-permute-start.14) | collective-permute-done | bytes 532512 | tf_op jit(solution)/shard_map/ppermute | solution.py:229
  62.2 2.0 %shard_map.54 = bf16[1024,256]{1,0:T(8,128)(2,1)} custom-call(s32[12]{0:T(128)S(1)} %pad_add_fusion.facts, f32[1024,256]{1,0:T(8,128)S(1)} %shard_map.53.refs_0_, s16[1040,256]{1,0:T(8,128)(2,1)S(1)} %collective-permute-done.14.refs_1_), custom_call_target="tpu_custom_call" | custom-call | flops 3000000000 | bytes 9000000 | tf_op jit(solution)/shard_map/pallas_call | solution.py:179
  (2 shorter events, 0.0 us)
Async XLA Ops:
  0.0 13.9 %collective-permute-start.1 = (bf16[2048,128]{1,0:T(8,128)(2,1)}, bf16[2048,128]{1,0:T(8,128)(2,1)S(1)}, u32[]{:S(2)}, u32[]{:S(2)}) collective-permute-start(bf16[2048,128]{1,0:T(8,128)(2,1)} %refs_0_.9), channel_id=1, source_target_pairs={{0,16},{4,20},{8,24},{12,28},{16,0},{20,4},{24,8},{28,12},{1,17},{... | collective-permute-start | bytes 1572872 | tf_op jit(solution)/shard_map/ppermute | solution.py:226
  1.5 13.6 %collective-permute-start = (bf16[2048,128]{1,0:T(8,128)(2,1)}, bf16[2048,128]{1,0:T(8,128)(2,1)S(1)}, u32[]{:S(2)}, u32[]{:S(2)}) collective-permute-start(bf16[2048,128]{1,0:T(8,128)(2,1)} %refs_0_.9), channel_id=1, source_target_pairs={{0,8},{4,12},{8,0},{12,4},{16,24},{20,28},{24,16},{28,20},{1,9},{5... | collective-permute-start | bytes 1572872 | tf_op jit(solution)/shard_map/ppermute | solution.py:226
  2.1 2.5 %copy-start.1 = (bf16[1024,2048]{1,0:T(8,128)(2,1)S(1)}, bf16[1024,2048]{1,0:T(8,128)(2,1)}, u32[]{:S(2)}) copy-start(bf16[1024,2048]{1,0:T(8,128)(2,1)} %param.4) | copy-start | bytes 12582916
  3.0 13.8 %collective-permute-start.2 = (bf16[2048,128]{1,0:T(8,128)(2,1)}, bf16[2048,128]{1,0:T(8,128)(2,1)S(1)}, u32[]{:S(2)}, u32[]{:S(2)}) collective-permute-start(bf16[2048,128]{1,0:T(8,128)(2,1)} %refs_0_.9), channel_id=1, source_target_pairs={{0,4},{4,0},{8,12},{12,8},{16,20},{20,16},{24,28},{28,24},{1,5},{5... | collective-permute-start | bytes 1572872 | tf_op jit(solution)/shard_map/ppermute | solution.py:226
  4.5 13.2 %copy-start = (bf16[2048,128]{1,0:T(8,128)(2,1)S(1)}, bf16[2048,128]{1,0:T(8,128)(2,1)}, u32[]{:S(2)}) copy-start(bf16[2048,128]{1,0:T(8,128)(2,1)} %refs_0_.9) | copy-start | bytes 1572868
  15.1 1.9 %collective-permute-start.3 = (bf16[2048,128]{1,0:T(8,128)(2,1)S(1)}, bf16[2048,128]{1,0:T(8,128)(2,1)S(1)}, u32[]{:S(2)}, u32[]{:S(2)}) collective-permute-start(bf16[2048,128]{1,0:T(8,128)(2,1)S(1)} %collective-permute-done.refs_1_), channel_id=1, source_target_pairs={{0,4},{4,0},{8,12},{12,8},{16,20},{20,16},{24,28},{28,24},{1,5},{5... | collective-permute-start | bytes 1572872 | tf_op jit(solution)/shard_map/ppermute | solution.py:226
  15.1 2.7 %collective-permute-start.4 = (bf16[2048,128]{1,0:T(8,128)(2,1)S(1)}, bf16[2048,128]{1,0:T(8,128)(2,1)S(1)}, u32[]{:S(2)}, u32[]{:S(2)}) collective-permute-start(bf16[2048,128]{1,0:T(8,128)(2,1)S(1)} %collective-permute-done.1.refs_2_), channel_id=1, source_target_pairs={{0,4},{4,0},{8,12},{12,8},{16,20},{20,16},{24,28},{28,24},{1,5},{5... | collective-permute-start | bytes 1572872 | tf_op jit(solution)/shard_map/ppermute | solution.py:226
  15.7 8.5 %collective-permute-start.6 = (bf16[1024,128]{1,0:T(8,128)(2,1)S(1)}, bf16[1024,128]{1,0:T(8,128)(2,1)S(1)}, u32[]{:S(2)}, u32[]{:S(2)}) collective-permute-start(bf16[1024,128]{1,0:T(8,128)(2,1)S(1)} %slice.6), channel_id=1, source_target_pairs={{0,8},{4,12},{8,0},{12,4},{16,24},{20,28},{24,16},{28,20},{1,9},{5... | collective-permute-start | bytes 786440 | tf_op jit(solution)/shard_map/ppermute | solution.py:226
  16.3 7.9 %collective-permute-start.7 = (bf16[1024,128]{1,0:T(8,128)(2,1)S(1)}, bf16[1024,128]{1,0:T(8,128)(2,1)S(1)}, u32[]{:S(2)}, u32[]{:S(2)}) collective-permute-start(bf16[1024,128]{1,0:T(8,128)(2,1)S(1)} %slice.7), channel_id=1, source_target_pairs={{0,16},{4,20},{8,24},{12,28},{16,0},{20,4},{24,8},{28,12},{1,17},{... | collective-permute-start | bytes 786440 | tf_op jit(solution)/shard_map/ppermute | solution.py:226
  20.3 9.3 %collective-permute-start.5 = (s16[1040,128]{1,0:T(8,128)(2,1)S(1)}, s16[1040,128]{1,0:T(8,128)(2,1)S(1)}, u32[]{:S(2)}, u32[]{:S(2)}) collective-permute-start(s16[1040,128]{1,0:T(8,128)(2,1)S(1)} %get-tuple-element.25), channel_id=1, source_target_pairs={{0,1},{1,0},{2,3},{3,2},{4,5},{5,4},{6,7},{7,6},{8,9},{9,8},{10,11... | collective-permute-start | bytes 798728 | tf_op jit(solution)/shard_map/ppermute | solution.py:229
  24.2 5.4 %collective-permute-start.8 = (bf16[1024,128]{1,0:T(8,128)(2,1)S(1)}, bf16[1024,128]{1,0:T(8,128)(2,1)S(1)}, u32[]{:S(2)}, u32[]{:S(2)}) collective-permute-start(bf16[1024,128]{1,0:T(8,128)(2,1)S(1)} %collective-permute-done.6.refs_3_), channel_id=1, source_target_pairs={{0,4},{4,0},{8,12},{12,8},{16,20},{20,16},{24,28},{28,24},{1,5},{5... | collective-permute-start | bytes 786440 | tf_op jit(solution)/shard_map/ppermute | solution.py:226
  24.2 5.4 %collective-permute-start.9 = (bf16[1024,128]{1,0:T(8,128)(2,1)S(1)}, bf16[1024,128]{1,0:T(8,128)(2,1)S(1)}, u32[]{:S(2)}, u32[]{:S(2)}) collective-permute-start(bf16[1024,128]{1,0:T(8,128)(2,1)S(1)} %collective-permute-done.7.refs_4_), channel_id=1, source_target_pairs={{0,4},{4,0},{8,12},{12,8},{16,20},{20,16},{24,28},{28,24},{1,5},{5... | collective-permute-start | bytes 786440 | tf_op jit(solution)/shard_map/ppermute | solution.py:226
  24.7 9.7 %collective-permute-start.10 = (s16[1040,128]{1,0:T(8,128)(2,1)S(1)}, s16[1040,128]{1,0:T(8,128)(2,1)S(1)}, u32[]{:S(2)}, u32[]{:S(2)}) collective-permute-start(s16[1040,128]{1,0:T(8,128)(2,1)S(1)} %get-tuple-element.23), channel_id=1, source_target_pairs={{0,1},{1,0},{2,3},{3,2},{4,5},{5,4},{6,7},{7,6},{8,9},{9,8},{10,11... | collective-permute-start | bytes 798728 | tf_op jit(solution)/shard_map/ppermute | solution.py:229
  32.0 14.4 %collective-permute-start.11 = (s16[1040,256]{1,0:T(8,128)(2,1)S(1)}, s16[1040,256]{1,0:T(8,128)(2,1)S(1)}, u32[]{:S(2)}, u32[]{:S(2)}) collective-permute-start(s16[1040,256]{1,0:T(8,128)(2,1)S(1)} %shard_map.48), channel_id=1, source_target_pairs={{0,1},{3,2},{2,3},{4,5},{7,6},{6,7},{8,9},{11,10},{12,13},{15,14},... | collective-permute-start | bytes 1597448 | tf_op jit(solution)/shard_map/ppermute | solution.py:229
  35.5 18.9 %collective-permute-start.12 = (s16[1040,256]{1,0:T(8,128)(2,1)S(1)}, s16[1040,256]{1,0:T(8,128)(2,1)S(1)}, u32[]{:S(2)}, u32[]{:S(2)}) collective-permute-start(s16[1040,256]{1,0:T(8,128)(2,1)S(1)} %shard_map.49), channel_id=1, source_target_pairs={{1,2},{2,0},{5,6},{6,4},{9,11},{10,8},{13,15},{14,12},{17,19},{18,... | collective-permute-start | bytes 1597448 | tf_op jit(solution)/shard_map/ppermute | solution.py:229
  43.8 14.9 %collective-permute-start.13 = (s16[1040,256]{1,0:T(8,128)(2,1)S(1)}, s16[1040,256]{1,0:T(8,128)(2,1)S(1)}, u32[]{:S(2)}, u32[]{:S(2)}) collective-permute-start(s16[1040,256]{1,0:T(8,128)(2,1)S(1)} %get-tuple-element.31), channel_id=1, source_target_pairs={{0,1},{3,2},{4,5},{7,6},{8,9},{11,10},{12,13},{15,14},{16,17},{19,... | collective-permute-start | bytes 1597448 | tf_op jit(solution)/shard_map/ppermute | solution.py:229
  47.4 14.8 %collective-permute-start.14 = (s16[1040,256]{1,0:T(8,128)(2,1)S(1)}, s16[1040,256]{1,0:T(8,128)(2,1)S(1)}, u32[]{:S(2)}, u32[]{:S(2)}) collective-permute-start(s16[1040,256]{1,0:T(8,128)(2,1)S(1)} %shard_map.51), channel_id=1, source_target_pairs={{1,3},{2,1},{5,7},{6,5},{9,10},{10,9},{13,14},{14,13},{17,18},{18,... | collective-permute-start | bytes 1597448 | tf_op jit(solution)/shard_map/ppermute | solution.py:229

commit v7 on v6

--- a/solution.py
+++ b/solution.py
@@ -12,7 +12,7 @@
 LEVELS = 32767.0
 STEPS_PER_OCTAVE = 64.0
 BLOCK_ROWS = 512
-ADD_ROWS = 256
+ADD_ROWS = 1024
 
 
 def apply_mask(amplitudes, tile_mask):

time: 65.4 us -> 64.8 us (level)
  Pallas kernels: 18.4 us -> 17.6 us
    pallas_call x4, Pallas kernels: 5.32 us -> 4.54 us  [add(): pl.pallas_call(functools.partial(add_kernel, tuple(((weight, len(x)) for...]
where the time goes in v7:
time: 64.8 us; the launch traced here: 63.6 us
  waiting for transfers between devices  25.3 us (39%)
  Pallas kernels  17.6 us (27%)
  starting transfers between devices  17.2 us (27%)
  other arithmetic  1.91 us (3%)
  local copies, waits for them, and re-layouts  1.5 us (2%)
    ppermute x6, waiting for transfers between devices, along(): return lax.ppermute(block, ('row', 'col'), line_pairs(choose))  13.5 us
    pallas_call x5, Pallas kernels, multiply(): pl.pallas_call(functools.partial(multiply_kernel, slots, kinds, rows, wid...  13.1 us
    ppermute x6, starting transfers between devices, along(): return lax.ppermute(block, ('row', 'col'), line_pairs(choose))  13 us
    ppermute x9, waiting for transfers between devices, across(): return lax.ppermute(block, 'row', [(i, i ^ bit) for i in range(8)])  11.8 us
    pallas_call x4, Pallas kernels, add(): pl.pallas_call(functools.partial(add_kernel, tuple(((weight, len(x)) for...  4.54 us
    ppermute x9, starting transfers between devices, across(): return lax.ppermute(block, 'row', [(i, i ^ bit) for i in range(8)])  4.19 us
  transfers between devices with their start and end apart: 15, of which 10 were waited for; matrix products, arithmetic and copies ran while one was open for 5% of the time, Pallas kernels for 25%

profile of v7, /device:TPU:10, one launch (start us, length us, event | category | flops | bytes accessed | tf_op | source)
XLA Modules:
  0.0 63.6 jit_solution(12965918984559354114)
XLA Ops:
  0.0 1.5 %collective-permute-start.1 = (bf16[2048,128]{1,0:T(8,128)(2,1)}, bf16[2048,128]{1,0:T(8,128)(2,1)S(1)}, u32[]{:S(2)}, u32[]{:S(2)}) collective-permute-start(bf16[2048,128]{1,0:T(8,128)(2,1)} %refs_0_.9), channel_id=1, source_target_pairs={{0,16},{4,20},{8,24},{12,28},{16,0},{20,4},{24,8},{28,12},{1,17},{... | collective-permute-start | bytes 1572872 | tf_op jit(solution)/shard_map/ppermute | solution.py:226
  1.5 0.5 collective-permute-start
  2.1 0.0 copy-start.1
  2.1 0.8 %dynamic-slice_bitcast_fusion = s32[10]{0:T(128)S(1)} fusion(s32[16,10]{1,0:T(8,128)} %constant.40.clone, s32[]{:T(128)S(6)} %select_n.15), kind=kLoop, calls=%fused_computation.2 | loop fusion | bytes 84 | tf_op jit(solution)/shard_map/squeeze | solution.py:247
  2.9 0.1 pad_add_fusion.facts
  3.0 0.0 collective-permute-start.2
  3.0 0.9 %convert_element_type.3 = bf16[8,16]{1,0:T(8,128)(2,1)S(1)} convert(s32[8,16]{1,0:T(8,128)} %param.6) | non-fusion elementwise | flops 128 | bytes 768 | tf_op jit(solution)/shard_map/convert_element_type | solution.py:23
  3.9 0.6 mul.15
  4.5 0.0 copy-done.1
  4.5 0.0 copy-start
  4.6 0.9 %bitcast_multiply_fusion.a_ref = bf16[1024,2048]{1,0:T(8,128)(2,1)S(1)} fusion(bf16[1024,2048]{1,0:T(8,128)(2,1)S(1)} %copy-done.1, bf16[128,8,16,128]{3,2,1,0:T(8,128)(2,1)S(1)} %bitcast.8), kind=kLoop, calls=%fused_computation | loop fusion | flops 2097152 | bytes 12582912 | tf_op jit(solution)/shard_map/mul | solution.py:24
  5.5 8.4 %collective-permute-done.1.refs_2_ = bf16[2048,128]{1,0:T(8,128)(2,1)S(1)} collective-permute-done((bf16[2048,128]{1,0:T(8,128)(2,1)}, bf16[2048,128]{1,0:T(8,128)(2,1)S(1)}, u32[]{:S(2)}, u32[]{:S(2)}) %collective-permute-start.1) | collective-permute-done | bytes 524320 | tf_op jit(solution)/shard_map/ppermute | solution.py:226
  13.9 1.2 %collective-permute-done.refs_1_ = bf16[2048,128]{1,0:T(8,128)(2,1)S(1)} collective-permute-done((bf16[2048,128]{1,0:T(8,128)(2,1)}, bf16[2048,128]{1,0:T(8,128)(2,1)S(1)}, u32[]{:S(2)}, u32[]{:S(2)}) %collective-permute-start) | collective-permute-done | bytes 524320 | tf_op jit(solution)/shard_map/ppermute | solution.py:226
  15.1 0.0 collective-permute-start.3
  15.1 0.5 collective-permute-start.4
  15.7 0.6 collective-permute-start.6
  16.3 0.5 collective-permute-start.7
  16.8 0.0 collective-permute-done.2.refs_3_.refs_5_
  16.8 0.2 collective-permute-done.3.refs_4_.refs_6_
  17.0 0.7 %collective-permute-done.4.refs_5_.refs_7_ = bf16[2048,128]{1,0:T(8,128)(2,1)S(1)} collective-permute-done((bf16[2048,128]{1,0:T(8,128)(2,1)S(1)}, bf16[2048,128]{1,0:T(8,128)(2,1)S(1)}, u32[]{:S(2)}, u32[]{:S(2)}) %collective-permute-start.4) | collective-permute-done | bytes 524320 | tf_op jit(solution)/shard_map/ppermute | solution.py:226
  17.8 0.0 copy-done
  17.8 2.5 %shard_map.46 = (s16[1040,128]{1,0:T(8,128)(2,1)S(1)}, s16[1040,128]{1,0:T(8,128)(2,1)S(1)}) custom-call(s32[12]{0:T(128)S(1)} %pad_add_fusion.facts, bf16[1024,2048]{1,0:T(8,128)(2,1)S(1)} %bitcast_multiply_fusion.a_ref, bf16[2048,128]{1,0:T(8,128)(2,1)S(1)} %copy-done, bf16[2048,128]{1,0:T(8,128)(2,1)S(1)} %collective-permute-done.refs_1_, ...), custom_call_target="tpu_custom_call" | custom-call | flops 3000000000 | bytes 9000000 | tf_op jit(solution)/shard_map/pallas_call | solution.py:130
  20.3 0.5 collective-permute-start.5
  20.8 2.2 %shard_map.47.refs_0_ = f32[1024,256]{1,0:T(8,128)S(1)} custom-call(s32[12]{0:T(128)S(1)} %pad_add_fusion.facts, bf16[1024,2048]{1,0:T(8,128)(2,1)S(1)} %bitcast_multiply_fusion.a_ref, bf16[2048,128]{1,0:T(8,128)(2,1)S(1)} %copy-done, bf16[2048,128]{1,0:T(8,128)(2,1)S(1)} %collective-permute-done.refs_1_, ...), custom_call_target="tpu_custom_call" | custom-call | flops 3000000000 | bytes 9000000 | tf_op jit(solution)/shard_map/pallas_call | solution.py:130
  23.0 1.2 %collective-permute-done.7.refs_4_ = bf16[1024,128]{1,0:T(8,128)(2,1)S(1)} collective-permute-done((bf16[1024,128]{1,0:T(8,128)(2,1)S(1)}, bf16[1024,128]{1,0:T(8,128)(2,1)S(1)}, u32[]{:S(2)}, u32[]{:S(2)}) %collective-permute-start.7) | collective-permute-done | bytes 262176 | tf_op jit(solution)/shard_map/ppermute | solution.py:226
  24.2 0.0 collective-permute-done.6.refs_3_
  24.2 0.0 collective-permute-start.8
  24.2 0.5 collective-permute-start.9
  24.7 0.5 collective-permute-start.10
  25.2 4.4 %collective-permute-done.5.refs_1_ = s16[1040,128]{1,0:T(8,128)(2,1)S(1)} collective-permute-done((s16[1040,128]{1,0:T(8,128)(2,1)S(1)}, s16[1040,128]{1,0:T(8,128)(2,1)S(1)}, u32[]{:S(2)}, u32[]{:S(2)}) %collective-permute-start.5) | collective-permute-done | bytes 266272 | tf_op jit(solution)/shard_map/ppermute | solution.py:229
  29.6 0.0 collective-permute-done.8.refs_8_
  29.6 0.0 collective-permute-done.9.refs_9_
  29.6 2.4 %shard_map.48 = s16[1040,256]{1,0:T(8,128)(2,1)S(1)} custom-call(s32[12]{0:T(128)S(1)} %pad_add_fusion.facts, bf16[1024,2048]{1,0:T(8,128)(2,1)S(1)} %bitcast_multiply_fusion.a_ref, bf16[2048,128]{1,0:T(8,128)(2,1)S(1)} %copy-done, bf16[2048,128]{1,0:T(8,128)(2,1)S(1)} %collective-permute-done.refs_1_, bf16[2048,128]{1,0:T(8,128)(2,1)S(1)} %collective-permute-done.1.refs_2_, ...), custom_call_target="tpu_custom_call" | custom-call | flops 3000000000 | bytes 9000000 | tf_op jit(solution)/shard_map/pallas_call | solution.py:130
  32.0 1.3 %collective-permute-start.11 = (s16[1040,256]{1,0:T(8,128)(2,1)S(1)}, s16[1040,256]{1,0:T(8,128)(2,1)S(1)}, u32[]{:S(2)}, u32[]{:S(2)}) collective-permute-start(s16[1040,256]{1,0:T(8,128)(2,1)S(1)} %shard_map.48), channel_id=1, source_target_pairs={{0,1},{3,2},{2,3},{4,5},{7,6},{6,7},{8,9},{11,10},{12,13},{15,14},... | collective-permute-start | bytes 1597448 | tf_op jit(solution)/shard_map/ppermute | solution.py:229
  33.3 1.2 %collective-permute-done.10.refs_2_ = s16[1040,128]{1,0:T(8,128)(2,1)S(1)} collective-permute-done((s16[1040,128]{1,0:T(8,128)(2,1)S(1)}, s16[1040,128]{1,0:T(8,128)(2,1)S(1)}, u32[]{:S(2)}, u32[]{:S(2)}) %collective-permute-start.10) | collective-permute-done | bytes 266272 | tf_op jit(solution)/shard_map/ppermute | solution.py:229
  34.5 0.9 %shard_map.49 = s16[1040,256]{1,0:T(8,128)(2,1)S(1)} custom-call(s32[12]{0:T(128)S(1)} %pad_add_fusion.facts, f32[1024,256]{1,0:T(8,128)S(1)} %shard_map.47.refs_0_, s16[1040,128]{1,0:T(8,128)(2,1)S(1)} %collective-permute-done.5.refs_1_, s16[1040,128]{1,0:T(8,128)(2,1)S(1)} %collective-permute-done.10.refs_2_), custom_call_target="tpu_custom_call" | custom-call | flops 3000000000 | bytes 9000000 | tf_op jit(solution)/shard_map/pallas_call | solution.py:179
  35.4 4.5 %collective-permute-start.12 = (s16[1040,256]{1,0:T(8,128)(2,1)S(1)}, s16[1040,256]{1,0:T(8,128)(2,1)S(1)}, u32[]{:S(2)}, u32[]{:S(2)}) collective-permute-start(s16[1040,256]{1,0:T(8,128)(2,1)S(1)} %shard_map.49), channel_id=1, source_target_pairs={{1,2},{2,0},{5,6},{6,4},{9,11},{10,8},{13,15},{14,12},{17,19},{18,... | collective-permute-start | bytes 1597448 | tf_op jit(solution)/shard_map/ppermute | solution.py:229
  39.9 3.7 %shard_map.50 = (s16[1040,256]{1,0:T(8,128)(2,1)S(1)}, f32[1024,256]{1,0:T(8,128)S(1)}) custom-call(s32[12]{0:T(128)S(1)} %pad_add_fusion.facts, bf16[1024,2048]{1,0:T(8,128)(2,1)S(1)} %bitcast_multiply_fusion.a_ref, bf16[2048,128]{1,0:T(8,128)(2,1)S(1)} %copy-done, bf16[2048,128]{1,0:T(8,128)(2,1)S(1)} %collective-permute-done.refs_1_, ...), custom_call_target="tpu_custom_call" | custom-call | flops 3000000000 | bytes 9000000 | tf_op jit(solution)/shard_map/pallas_call | solution.py:130
  43.7 1.3 %collective-permute-start.13 = (s16[1040,256]{1,0:T(8,128)(2,1)S(1)}, s16[1040,256]{1,0:T(8,128)(2,1)S(1)}, u32[]{:S(2)}, u32[]{:S(2)}) collective-permute-start(s16[1040,256]{1,0:T(8,128)(2,1)S(1)} %get-tuple-element.31), channel_id=1, source_target_pairs={{0,1},{3,2},{4,5},{7,6},{8,9},{11,10},{12,13},{15,14},{16,17},{19,... | collective-permute-start | bytes 1597448 | tf_op jit(solution)/shard_map/ppermute | solution.py:229
  45.0 1.4 %collective-permute-done.11.refs_1_.refs_3_ = s16[1040,256]{1,0:T(8,128)(2,1)S(1)} collective-permute-done((s16[1040,256]{1,0:T(8,128)(2,1)S(1)}, s16[1040,256]{1,0:T(8,128)(2,1)S(1)}, u32[]{:S(2)}, u32[]{:S(2)}) %collective-permute-start.11) | collective-permute-done | bytes 532512 | tf_op jit(solution)/shard_map/ppermute | solution.py:229
  46.4 0.9 %shard_map.51 = s16[1040,256]{1,0:T(8,128)(2,1)S(1)} custom-call(s32[12]{0:T(128)S(1)} %pad_add_fusion.facts, f32[1024,256]{1,0:T(8,128)S(1)} %get-tuple-element.33.refs_0_, s16[1040,256]{1,0:T(8,128)(2,1)S(1)} %collective-permute-done.11.refs_1_.refs_3_), custom_call_target="tpu_custom_call" | custom-call | flops 3000000000 | bytes 9000000 | tf_op jit(solution)/shard_map/pallas_call | solution.py:179
  47.3 4.9 %collective-permute-start.14 = (s16[1040,256]{1,0:T(8,128)(2,1)S(1)}, s16[1040,256]{1,0:T(8,128)(2,1)S(1)}, u32[]{:S(2)}, u32[]{:S(2)}) collective-permute-start(s16[1040,256]{1,0:T(8,128)(2,1)S(1)} %shard_map.51), channel_id=1, source_target_pairs={{1,3},{2,1},{5,7},{6,5},{9,10},{10,9},{13,14},{14,13},{17,18},{18,... | collective-permute-start | bytes 1597448 | tf_op jit(solution)/shard_map/ppermute | solution.py:229
  52.2 2.2 %shard_map.52.refs_0_ = f32[1024,256]{1,0:T(8,128)S(1)} custom-call(s32[12]{0:T(128)S(1)} %pad_add_fusion.facts, bf16[1024,2048]{1,0:T(8,128)(2,1)S(1)} %bitcast_multiply_fusion.a_ref, bf16[2048,128]{1,0:T(8,128)(2,1)S(1)} %copy-done, bf16[2048,128]{1,0:T(8,128)(2,1)S(1)} %collective-permute-done.refs_1_, ...), custom_call_target="tpu_custom_call" | custom-call | flops 3000000000 | bytes 9000000 | tf_op jit(solution)/shard_map/pallas_call | solution.py:130
  54.4 0.0 collective-permute-done.12.refs_4_
  54.4 4.2 %collective-permute-done.13.refs_5_ = s16[1040,256]{1,0:T(8,128)(2,1)S(1)} collective-permute-done((s16[1040,256]{1,0:T(8,128)(2,1)S(1)}, s16[1040,256]{1,0:T(8,128)(2,1)S(1)}, u32[]{:S(2)}, u32[]{:S(2)}) %collective-permute-start.13) | collective-permute-done | bytes 532512 | tf_op jit(solution)/shard_map/ppermute | solution.py:229
  58.6 1.2 %shard_map.53.refs_0_ = f32[1024,256]{1,0:T(8,128)S(1)} custom-call(s32[12]{0:T(128)S(1)} %pad_add_fusion.facts, f32[1024,256]{1,0:T(8,128)S(1)} %shard_map.52.refs_0_, s16[1040,128]{1,0:T(8,128)(2,1)S(1)} %collective-permute-done.5.refs_1_, s16[1040,128]{1,0:T(8,128)(2,1)S(1)} %collective-permute-done.10.refs_2_, ...), custom_call_target="tpu_custom_call" | custom-call | flops 3000000000 | bytes 9000000 | tf_op jit(solution)/shard_map/pallas_call | solution.py:179
  59.8 2.3 %collective-permute-done.14.refs_1_ = s16[1040,256]{1,0:T(8,128)(2,1)S(1)} collective-permute-done((s16[1040,256]{1,0:T(8,128)(2,1)S(1)}, s16[1040,256]{1,0:T(8,128)(2,1)S(1)}, u32[]{:S(2)}, u32[]{:S(2)}) %collective-permute-start.14) | collective-permute-done | bytes 532512 | tf_op jit(solution)/shard_map/ppermute | solution.py:229
  62.1 1.5 %shard_map.54 = bf16[1024,256]{1,0:T(8,128)(2,1)} custom-call(s32[12]{0:T(128)S(1)} %pad_add_fusion.facts, f32[1024,256]{1,0:T(8,128)S(1)} %shard_map.53.refs_0_, s16[1040,256]{1,0:T(8,128)(2,1)S(1)} %collective-permute-done.14.refs_1_), custom_call_target="tpu_custom_call" | custom-call | flops 3000000000 | bytes 9000000 | tf_op jit(solution)/shard_map/pallas_call | solution.py:179
  (2 shorter events, 0.0 us)
Async XLA Ops:
  0.0 13.9 %collective-permute-start.1 = (bf16[2048,128]{1,0:T(8,128)(2,1)}, bf16[2048,128]{1,0:T(8,128)(2,1)S(1)}, u32[]{:S(2)}, u32[]{:S(2)}) collective-permute-start(bf16[2048,128]{1,0:T(8,128)(2,1)} %refs_0_.9), channel_id=1, source_target_pairs={{0,16},{4,20},{8,24},{12,28},{16,0},{20,4},{24,8},{28,12},{1,17},{... | collective-permute-start | bytes 1572872 | tf_op jit(solution)/shard_map/ppermute | solution.py:226
  1.5 13.6 %collective-permute-start = (bf16[2048,128]{1,0:T(8,128)(2,1)}, bf16[2048,128]{1,0:T(8,128)(2,1)S(1)}, u32[]{:S(2)}, u32[]{:S(2)}) collective-permute-start(bf16[2048,128]{1,0:T(8,128)(2,1)} %refs_0_.9), channel_id=1, source_target_pairs={{0,8},{4,12},{8,0},{12,4},{16,24},{20,28},{24,16},{28,20},{1,9},{5... | collective-permute-start | bytes 1572872 | tf_op jit(solution)/shard_map/ppermute | solution.py:226
  2.1 2.5 %copy-start.1 = (bf16[1024,2048]{1,0:T(8,128)(2,1)S(1)}, bf16[1024,2048]{1,0:T(8,128)(2,1)}, u32[]{:S(2)}) copy-start(bf16[1024,2048]{1,0:T(8,128)(2,1)} %param.4) | copy-start | bytes 12582916
  3.0 13.8 %collective-permute-start.2 = (bf16[2048,128]{1,0:T(8,128)(2,1)}, bf16[2048,128]{1,0:T(8,128)(2,1)S(1)}, u32[]{:S(2)}, u32[]{:S(2)}) collective-permute-start(bf16[2048,128]{1,0:T(8,128)(2,1)} %refs_0_.9), channel_id=1, source_target_pairs={{0,4},{4,0},{8,12},{12,8},{16,20},{20,16},{24,28},{28,24},{1,5},{5... | collective-permute-start | bytes 1572872 | tf_op jit(solution)/shard_map/ppermute | solution.py:226
  4.5 13.2 %copy-start = (bf16[2048,128]{1,0:T(8,128)(2,1)S(1)}, bf16[2048,128]{1,0:T(8,128)(2,1)}, u32[]{:S(2)}) copy-start(bf16[2048,128]{1,0:T(8,128)(2,1)} %refs_0_.9) | copy-start | bytes 1572868
  15.1 1.9 %collective-permute-start.3 = (bf16[2048,128]{1,0:T(8,128)(2,1)S(1)}, bf16[2048,128]{1,0:T(8,128)(2,1)S(1)}, u32[]{:S(2)}, u32[]{:S(2)}) collective-permute-start(bf16[2048,128]{1,0:T(8,128)(2,1)S(1)} %collective-permute-done.refs_1_), channel_id=1, source_target_pairs={{0,4},{4,0},{8,12},{12,8},{16,20},{20,16},{24,28},{28,24},{1,5},{5... | collective-permute-start | bytes 1572872 | tf_op jit(solution)/shard_map/ppermute | solution.py:226
  15.1 2.7 %collective-permute-start.4 = (bf16[2048,128]{1,0:T(8,128)(2,1)S(1)}, bf16[2048,128]{1,0:T(8,128)(2,1)S(1)}, u32[]{:S(2)}, u32[]{:S(2)}) collective-permute-start(bf16[2048,128]{1,0:T(8,128)(2,1)S(1)} %collective-permute-done.1.refs_2_), channel_id=1, source_target_pairs={{0,4},{4,0},{8,12},{12,8},{16,20},{20,16},{24,28},{28,24},{1,5},{5... | collective-permute-start | bytes 1572872 | tf_op jit(solution)/shard_map/ppermute | solution.py:226
  15.7 8.5 %collective-permute-start.6 = (bf16[1024,128]{1,0:T(8,128)(2,1)S(1)}, bf16[1024,128]{1,0:T(8,128)(2,1)S(1)}, u32[]{:S(2)}, u32[]{:S(2)}) collective-permute-start(bf16[1024,128]{1,0:T(8,128)(2,1)S(1)} %slice.6), channel_id=1, source_target_pairs={{0,8},{4,12},{8,0},{12,4},{16,24},{20,28},{24,16},{28,20},{1,9},{5... | collective-permute-start | bytes 786440 | tf_op jit(solution)/shard_map/ppermute | solution.py:226
  16.3 7.9 %collective-permute-start.7 = (bf16[1024,128]{1,0:T(8,128)(2,1)S(1)}, bf16[1024,128]{1,0:T(8,128)(2,1)S(1)}, u32[]{:S(2)}, u32[]{:S(2)}) collective-permute-start(bf16[1024,128]{1,0:T(8,128)(2,1)S(1)} %slice.7), channel_id=1, source_target_pairs={{0,16},{4,20},{8,24},{12,28},{16,0},{20,4},{24,8},{28,12},{1,17},{... | collective-permute-start | bytes 786440 | tf_op jit(solution)/shard_map/ppermute | solution.py:226
  20.3 9.3 %collective-permute-start.5 = (s16[1040,128]{1,0:T(8,128)(2,1)S(1)}, s16[1040,128]{1,0:T(8,128)(2,1)S(1)}, u32[]{:S(2)}, u32[]{:S(2)}) collective-permute-start(s16[1040,128]{1,0:T(8,128)(2,1)S(1)} %get-tuple-element.25), channel_id=1, source_target_pairs={{0,1},{1,0},{2,3},{3,2},{4,5},{5,4},{6,7},{7,6},{8,9},{9,8},{10,11... | collective-permute-start | bytes 798728 | tf_op jit(solution)/shard_map/ppermute | solution.py:229
  24.2 5.4 %collective-permute-start.8 = (bf16[1024,128]{1,0:T(8,128)(2,1)S(1)}, bf16[1024,128]{1,0:T(8,128)(2,1)S(1)}, u32[]{:S(2)}, u32[]{:S(2)}) collective-permute-start(bf16[1024,128]{1,0:T(8,128)(2,1)S(1)} %collective-permute-done.6.refs_3_), channel_id=1, source_target_pairs={{0,4},{4,0},{8,12},{12,8},{16,20},{20,16},{24,28},{28,24},{1,5},{5... | collective-permute-start | bytes 786440 | tf_op jit(solution)/shard_map/ppermute | solution.py:226
  24.2 5.4 %collective-permute-start.9 = (bf16[1024,128]{1,0:T(8,128)(2,1)S(1)}, bf16[1024,128]{1,0:T(8,128)(2,1)S(1)}, u32[]{:S(2)}, u32[]{:S(2)}) collective-permute-start(bf16[1024,128]{1,0:T(8,128)(2,1)S(1)} %collective-permute-done.7.refs_4_), channel_id=1, source_target_pairs={{0,4},{4,0},{8,12},{12,8},{16,20},{20,16},{24,28},{28,24},{1,5},{5... | collective-permute-start | bytes 786440 | tf_op jit(solution)/shard_map/ppermute | solution.py:226
  24.7 9.7 %collective-permute-start.10 = (s16[1040,128]{1,0:T(8,128)(2,1)S(1)}, s16[1040,128]{1,0:T(8,128)(2,1)S(1)}, u32[]{:S(2)}, u32[]{:S(2)}) collective-permute-start(s16[1040,128]{1,0:T(8,128)(2,1)S(1)} %get-tuple-element.23), channel_id=1, source_target_pairs={{0,1},{1,0},{2,3},{3,2},{4,5},{5,4},{6,7},{7,6},{8,9},{9,8},{10,11... | collective-permute-start | bytes 798728 | tf_op jit(solution)/shard_map/ppermute | solution.py:229
  32.0 14.4 %collective-permute-start.11 = (s16[1040,256]{1,0:T(8,128)(2,1)S(1)}, s16[1040,256]{1,0:T(8,128)(2,1)S(1)}, u32[]{:S(2)}, u32[]{:S(2)}) collective-permute-start(s16[1040,256]{1,0:T(8,128)(2,1)S(1)} %shard_map.48), channel_id=1, source_target_pairs={{0,1},{3,2},{2,3},{4,5},{7,6},{6,7},{8,9},{11,10},{12,13},{15,14},... | collective-permute-start | bytes 1597448 | tf_op jit(solution)/shard_map/ppermute | solution.py:229
  35.4 19.0 %collective-permute-start.12 = (s16[1040,256]{1,0:T(8,128)(2,1)S(1)}, s16[1040,256]{1,0:T(8,128)(2,1)S(1)}, u32[]{:S(2)}, u32[]{:S(2)}) collective-permute-start(s16[1040,256]{1,0:T(8,128)(2,1)S(1)} %shard_map.49), channel_id=1, source_target_pairs={{1,2},{2,0},{5,6},{6,4},{9,11},{10,8},{13,15},{14,12},{17,19},{18,... | collective-permute-start | bytes 1597448 | tf_op jit(solution)/shard_map/ppermute | solution.py:229
  43.7 14.9 %collective-permute-start.13 = (s16[1040,256]{1,0:T(8,128)(2,1)S(1)}, s16[1040,256]{1,0:T(8,128)(2,1)S(1)}, u32[]{:S(2)}, u32[]{:S(2)}) collective-permute-start(s16[1040,256]{1,0:T(8,128)(2,1)S(1)} %get-tuple-element.31), channel_id=1, source_target_pairs={{0,1},{3,2},{4,5},{7,6},{8,9},{11,10},{12,13},{15,14},{16,17},{19,... | collective-permute-start | bytes 1597448 | tf_op jit(solution)/shard_map/ppermute | solution.py:229
  47.3 14.8 %collective-permute-start.14 = (s16[1040,256]{1,0:T(8,128)(2,1)S(1)}, s16[1040,256]{1,0:T(8,128)(2,1)S(1)}, u32[]{:S(2)}, u32[]{:S(2)}) collective-permute-start(s16[1040,256]{1,0:T(8,128)(2,1)S(1)} %shard_map.51), channel_id=1, source_target_pairs={{1,3},{2,1},{5,7},{6,5},{9,10},{10,9},{13,14},{14,13},{17,18},{18,... | collective-permute-start | bytes 1597448 | tf_op jit(solution)/shard_map/ppermute | solution.py:229

commit v8 on v5

--- a/solution.py
+++ b/solution.py
@@ -11,7 +11,7 @@
 CODE_ROWS = 16
 LEVELS = 32767.0
 STEPS_PER_OCTAVE = 64.0
-BLOCK_ROWS = 512
+BLOCK_ROWS = 256
 ADD_ROWS = 512
 
 

time: 64.8 us -> 65.5 us (1.011)
  waiting for transfers between devices: 25.3 us -> 22.9 us
  Pallas kernels: 17.7 us -> 20 us
  starting transfers between devices: 17.1 us -> 17.9 us
    pallas_call x5, Pallas kernels: 13.1 us -> 15.3 us  [multiply(): pl.pallas_call(functools.partial(multiply_kernel, slots, kinds, rows, wid...]
    ppermute x6, waiting for transfers between devices: 13.4 us -> 12 us  [along(): return lax.ppermute(block, ('row', 'col'), line_pairs(choose))]
    ppermute x9, waiting for transfers between devices: 11.8 us -> 10.9 us  [across(): return lax.ppermute(block, 'row', [(i, i ^ bit) for i in range(8)])]
    ppermute x6, starting transfers between devices: 12.9 us -> 13.7 us  [along(): return lax.ppermute(block, ('row', 'col'), line_pairs(choose))]
  transfers between devices with their start and end apart: 15 -> 15, of which waited for: 10 -> 10; matrix products, arithmetic and copies ran while one was open for 5% -> 5% of each run, Pallas kernels for 26% -> 29%
where the time goes in v8:
time: 65.5 us; the launch traced here: 64.4 us
  waiting for transfers between devices  22.9 us (35%)
  Pallas kernels  20 us (31%)
  starting transfers between devices  17.9 us (27%)
  other arithmetic  1.91 us (3%)
  local copies, waits for them, and re-layouts  1.5 us (2%)
    pallas_call x5, Pallas kernels, multiply(): pl.pallas_call(functools.partial(multiply_kernel, slots, kinds, rows, wid...  15.3 us
    ppermute x6, starting transfers between devices, along(): return lax.ppermute(block, ('row', 'col'), line_pairs(choose))  13.7 us
    ppermute x6, waiting for transfers between devices, along(): return lax.ppermute(block, ('row', 'col'), line_pairs(choose))  12 us
    ppermute x9, waiting for transfers between devices, across(): return lax.ppermute(block, 'row', [(i, i ^ bit) for i in range(8)])  10.9 us
    pallas_call x4, Pallas kernels, add(): pl.pallas_call(functools.partial(add_kernel, tuple(((weight, len(x)) for...  4.68 us
    ppermute x9, starting transfers between devices, across(): return lax.ppermute(block, 'row', [(i, i ^ bit) for i in range(8)])  4.19 us
  transfers between devices with their start and end apart: 15, of which 10 were waited for; matrix products, arithmetic and copies ran while one was open for 5% of the time, Pallas kernels for 29%

profile of v8, /device:TPU:10, one launch (start us, length us, event | category | flops | bytes accessed | tf_op | source)
XLA Modules:
  0.0 64.4 jit_solution(4759702951011647009)
XLA Ops:
  0.0 1.5 %collective-permute-start.1 = (bf16[2048,128]{1,0:T(8,128)(2,1)}, bf16[2048,128]{1,0:T(8,128)(2,1)S(1)}, u32[]{:S(2)}, u32[]{:S(2)}) collective-permute-start(bf16[2048,128]{1,0:T(8,128)(2,1)} %refs_0_.9), channel_id=1, source_target_pairs={{0,16},{4,20},{8,24},{12,28},{16,0},{20,4},{24,8},{28,12},{1,17},{... | collective-permute-start | bytes 1572872 | tf_op jit(solution)/shard_map/ppermute | solution.py:226
  1.5 0.5 collective-permute-start
  2.1 0.0 copy-start.1
  2.1 0.8 %dynamic-slice_bitcast_fusion = s32[10]{0:T(128)S(1)} fusion(s32[16,10]{1,0:T(8,128)} %constant.40.clone, s32[]{:T(128)S(6)} %select_n.15), kind=kLoop, calls=%fused_computation.2 | loop fusion | bytes 84 | tf_op jit(solution)/shard_map/squeeze | solution.py:247
  2.9 0.1 pad_add_fusion.facts
  3.0 0.0 collective-permute-start.2
  3.0 0.9 %convert_element_type.3 = bf16[8,16]{1,0:T(8,128)(2,1)S(1)} convert(s32[8,16]{1,0:T(8,128)} %param.6) | non-fusion elementwise | flops 128 | bytes 768 | tf_op jit(solution)/shard_map/convert_element_type | solution.py:23
  3.9 0.6 mul.15
  4.5 0.0 copy-done.1
  4.5 0.0 copy-start
  4.6 0.9 %bitcast_multiply_fusion.a_ref = bf16[1024,2048]{1,0:T(8,128)(2,1)S(1)} fusion(bf16[1024,2048]{1,0:T(8,128)(2,1)S(1)} %copy-done.1, bf16[128,8,16,128]{3,2,1,0:T(8,128)(2,1)S(1)} %bitcast.8), kind=kLoop, calls=%fused_computation | loop fusion | flops 2097152 | bytes 12582912 | tf_op jit(solution)/shard_map/mul | solution.py:24
  5.5 8.4 %collective-permute-done.1.refs_2_ = bf16[2048,128]{1,0:T(8,128)(2,1)S(1)} collective-permute-done((bf16[2048,128]{1,0:T(8,128)(2,1)}, bf16[2048,128]{1,0:T(8,128)(2,1)S(1)}, u32[]{:S(2)}, u32[]{:S(2)}) %collective-permute-start.1) | collective-permute-done | bytes 524320 | tf_op jit(solution)/shard_map/ppermute | solution.py:226
  13.9 1.2 %collective-permute-done.refs_1_ = bf16[2048,128]{1,0:T(8,128)(2,1)S(1)} collective-permute-done((bf16[2048,128]{1,0:T(8,128)(2,1)}, bf16[2048,128]{1,0:T(8,128)(2,1)S(1)}, u32[]{:S(2)}, u32[]{:S(2)}) %collective-permute-start) | collective-permute-done | bytes 524320 | tf_op jit(solution)/shard_map/ppermute | solution.py:226
  15.1 0.0 collective-permute-start.3
  15.1 0.5 collective-permute-start.4
  15.7 0.6 collective-permute-start.6
  16.3 0.5 collective-permute-start.7
  16.8 0.0 collective-permute-done.2.refs_3_.refs_5_
  16.8 0.2 collective-permute-done.3.refs_4_.refs_6_
  17.0 0.7 %collective-permute-done.4.refs_5_.refs_7_ = bf16[2048,128]{1,0:T(8,128)(2,1)S(1)} collective-permute-done((bf16[2048,128]{1,0:T(8,128)(2,1)S(1)}, bf16[2048,128]{1,0:T(8,128)(2,1)S(1)}, u32[]{:S(2)}, u32[]{:S(2)}) %collective-permute-start.4) | collective-permute-done | bytes 524320 | tf_op jit(solution)/shard_map/ppermute | solution.py:226
  17.8 0.0 copy-done
  17.8 3.0 %shard_map.46 = (s16[1040,128]{1,0:T(8,128)(2,1)S(1)}, s16[1040,128]{1,0:T(8,128)(2,1)S(1)}) custom-call(s32[12]{0:T(128)S(1)} %pad_add_fusion.facts, bf16[1024,2048]{1,0:T(8,128)(2,1)S(1)} %bitcast_multiply_fusion.a_ref, bf16[2048,128]{1,0:T(8,128)(2,1)S(1)} %copy-done, bf16[2048,128]{1,0:T(8,128)(2,1)S(1)} %collective-permute-done.refs_1_, ...), custom_call_target="tpu_custom_call" | custom-call | flops 3000000000 | bytes 9000000 | tf_op jit(solution)/shard_map/pallas_call | solution.py:130
  20.8 0.5 collective-permute-start.5
  21.3 2.6 %shard_map.47.refs_0_ = f32[1024,256]{1,0:T(8,128)S(1)} custom-call(s32[12]{0:T(128)S(1)} %pad_add_fusion.facts, bf16[1024,2048]{1,0:T(8,128)(2,1)S(1)} %bitcast_multiply_fusion.a_ref, bf16[2048,128]{1,0:T(8,128)(2,1)S(1)} %copy-done, bf16[2048,128]{1,0:T(8,128)(2,1)S(1)} %collective-permute-done.refs_1_, ...), custom_call_target="tpu_custom_call" | custom-call | flops 3000000000 | bytes 9000000 | tf_op jit(solution)/shard_map/pallas_call | solution.py:130
  23.9 0.3 collective-permute-done.7.refs_4_
  24.2 0.0 collective-permute-done.6.refs_3_
  24.2 0.0 collective-permute-start.8
  24.2 0.5 collective-permute-start.9
  24.7 1.4 %collective-permute-start.10 = (s16[1040,128]{1,0:T(8,128)(2,1)S(1)}, s16[1040,128]{1,0:T(8,128)(2,1)S(1)}, u32[]{:S(2)}, u32[]{:S(2)}) collective-permute-start(s16[1040,128]{1,0:T(8,128)(2,1)S(1)} %get-tuple-element.23), channel_id=1, source_target_pairs={{0,1},{1,0},{2,3},{3,2},{4,5},{5,4},{6,7},{7,6},{8,9},{9,8},{10,11... | collective-permute-start | bytes 798728 | tf_op jit(solution)/shard_map/ppermute | solution.py:229
  26.1 4.0 %collective-permute-done.5.refs_1_ = s16[1040,128]{1,0:T(8,128)(2,1)S(1)} collective-permute-done((s16[1040,128]{1,0:T(8,128)(2,1)S(1)}, s16[1040,128]{1,0:T(8,128)(2,1)S(1)}, u32[]{:S(2)}, u32[]{:S(2)}) %collective-permute-start.5) | collective-permute-done | bytes 266272 | tf_op jit(solution)/shard_map/ppermute | solution.py:229
  30.1 0.0 collective-permute-done.8.refs_8_
  30.1 0.0 collective-permute-done.9.refs_9_
  30.1 2.8 %shard_map.48 = s16[1040,256]{1,0:T(8,128)(2,1)S(1)} custom-call(s32[12]{0:T(128)S(1)} %pad_add_fusion.facts, bf16[1024,2048]{1,0:T(8,128)(2,1)S(1)} %bitcast_multiply_fusion.a_ref, bf16[2048,128]{1,0:T(8,128)(2,1)S(1)} %copy-done, bf16[2048,128]{1,0:T(8,128)(2,1)S(1)} %collective-permute-done.refs_1_, bf16[2048,128]{1,0:T(8,128)(2,1)S(1)} %collective-permute-done.1.refs_2_, ...), custom_call_target="tpu_custom_call" | custom-call | flops 3000000000 | bytes 9000000 | tf_op jit(solution)/shard_map/pallas_call | solution.py:130
  32.9 1.3 %collective-permute-start.11 = (s16[1040,256]{1,0:T(8,128)(2,1)S(1)}, s16[1040,256]{1,0:T(8,128)(2,1)S(1)}, u32[]{:S(2)}, u32[]{:S(2)}) collective-permute-start(s16[1040,256]{1,0:T(8,128)(2,1)S(1)} %shard_map.48), channel_id=1, source_target_pairs={{0,1},{3,2},{2,3},{4,5},{7,6},{6,7},{8,9},{11,10},{12,13},{15,14},... | collective-permute-start | bytes 1597448 | tf_op jit(solution)/shard_map/ppermute | solution.py:229
  34.2 0.7 %collective-permute-done.10.refs_2_ = s16[1040,128]{1,0:T(8,128)(2,1)S(1)} collective-permute-done((s16[1040,128]{1,0:T(8,128)(2,1)S(1)}, s16[1040,128]{1,0:T(8,128)(2,1)S(1)}, u32[]{:S(2)}, u32[]{:S(2)}) %collective-permute-start.10) | collective-permute-done | bytes 266272 | tf_op jit(solution)/shard_map/ppermute | solution.py:229
  35.0 1.0 %shard_map.49 = s16[1040,256]{1,0:T(8,128)(2,1)S(1)} custom-call(s32[12]{0:T(128)S(1)} %pad_add_fusion.facts, f32[1024,256]{1,0:T(8,128)S(1)} %shard_map.47.refs_0_, s16[1040,128]{1,0:T(8,128)(2,1)S(1)} %collective-permute-done.5.refs_1_, s16[1040,128]{1,0:T(8,128)(2,1)S(1)} %collective-permute-done.10.refs_2_), custom_call_target="tpu_custom_call" | custom-call | flops 3000000000 | bytes 9000000 | tf_op jit(solution)/shard_map/pallas_call | solution.py:179
  36.0 4.9 %collective-permute-start.12 = (s16[1040,256]{1,0:T(8,128)(2,1)S(1)}, s16[1040,256]{1,0:T(8,128)(2,1)S(1)}, u32[]{:S(2)}, u32[]{:S(2)}) collective-permute-start(s16[1040,256]{1,0:T(8,128)(2,1)S(1)} %shard_map.49), channel_id=1, source_target_pairs={{1,2},{2,0},{5,6},{6,4},{9,11},{10,8},{13,15},{14,12},{17,19},{18,... | collective-permute-start | bytes 1597448 | tf_op jit(solution)/shard_map/ppermute | solution.py:229
  40.9 4.2 %shard_map.50 = (s16[1040,256]{1,0:T(8,128)(2,1)S(1)}, f32[1024,256]{1,0:T(8,128)S(1)}) custom-call(s32[12]{0:T(128)S(1)} %pad_add_fusion.facts, bf16[1024,2048]{1,0:T(8,128)(2,1)S(1)} %bitcast_multiply_fusion.a_ref, bf16[2048,128]{1,0:T(8,128)(2,1)S(1)} %copy-done, bf16[2048,128]{1,0:T(8,128)(2,1)S(1)} %collective-permute-done.refs_1_, ...), custom_call_target="tpu_custom_call" | custom-call | flops 3000000000 | bytes 9000000 | tf_op jit(solution)/shard_map/pallas_call | solution.py:130
  45.1 1.3 %collective-permute-start.13 = (s16[1040,256]{1,0:T(8,128)(2,1)S(1)}, s16[1040,256]{1,0:T(8,128)(2,1)S(1)}, u32[]{:S(2)}, u32[]{:S(2)}) collective-permute-start(s16[1040,256]{1,0:T(8,128)(2,1)S(1)} %get-tuple-element.31), channel_id=1, source_target_pairs={{0,1},{3,2},{4,5},{7,6},{8,9},{11,10},{12,13},{15,14},{16,17},{19,... | collective-permute-start | bytes 1597448 | tf_op jit(solution)/shard_map/ppermute | solution.py:229
  46.4 0.9 %collective-permute-done.11.refs_1_.refs_3_ = s16[1040,256]{1,0:T(8,128)(2,1)S(1)} collective-permute-done((s16[1040,256]{1,0:T(8,128)(2,1)S(1)}, s16[1040,256]{1,0:T(8,128)(2,1)S(1)}, u32[]{:S(2)}, u32[]{:S(2)}) %collective-permute-start.11) | collective-permute-done | bytes 532512 | tf_op jit(solution)/shard_map/ppermute | solution.py:229
  47.3 1.0 %shard_map.51 = s16[1040,256]{1,0:T(8,128)(2,1)S(1)} custom-call(s32[12]{0:T(128)S(1)} %pad_add_fusion.facts, f32[1024,256]{1,0:T(8,128)S(1)} %get-tuple-element.33.refs_0_, s16[1040,256]{1,0:T(8,128)(2,1)S(1)} %collective-permute-done.11.refs_1_.refs_3_), custom_call_target="tpu_custom_call" | custom-call | flops 3000000000 | bytes 9000000 | tf_op jit(solution)/shard_map/pallas_call | solution.py:179
  48.3 4.4 %collective-permute-start.14 = (s16[1040,256]{1,0:T(8,128)(2,1)S(1)}, s16[1040,256]{1,0:T(8,128)(2,1)S(1)}, u32[]{:S(2)}, u32[]{:S(2)}) collective-permute-start(s16[1040,256]{1,0:T(8,128)(2,1)S(1)} %shard_map.51), channel_id=1, source_target_pairs={{1,3},{2,1},{5,7},{6,5},{9,10},{10,9},{13,14},{14,13},{17,18},{18,... | collective-permute-start | bytes 1597448 | tf_op jit(solution)/shard_map/ppermute | solution.py:229
  52.7 2.6 %shard_map.52.refs_0_ = f32[1024,256]{1,0:T(8,128)S(1)} custom-call(s32[12]{0:T(128)S(1)} %pad_add_fusion.facts, bf16[1024,2048]{1,0:T(8,128)(2,1)S(1)} %bitcast_multiply_fusion.a_ref, bf16[2048,128]{1,0:T(8,128)(2,1)S(1)} %copy-done, bf16[2048,128]{1,0:T(8,128)(2,1)S(1)} %collective-permute-done.refs_1_, ...), custom_call_target="tpu_custom_call" | custom-call | flops 3000000000 | bytes 9000000 | tf_op jit(solution)/shard_map/pallas_call | solution.py:130
  55.3 0.0 collective-permute-done.12.refs_4_
  55.3 4.3 %collective-permute-done.13.refs_5_ = s16[1040,256]{1,0:T(8,128)(2,1)S(1)} collective-permute-done((s16[1040,256]{1,0:T(8,128)(2,1)S(1)}, s16[1040,256]{1,0:T(8,128)(2,1)S(1)}, u32[]{:S(2)}, u32[]{:S(2)}) %collective-permute-start.13) | collective-permute-done | bytes 532512 | tf_op jit(solution)/shard_map/ppermute | solution.py:229
  59.7 1.2 %shard_map.53.refs_0_ = f32[1024,256]{1,0:T(8,128)S(1)} custom-call(s32[12]{0:T(128)S(1)} %pad_add_fusion.facts, f32[1024,256]{1,0:T(8,128)S(1)} %shard_map.52.refs_0_, s16[1040,128]{1,0:T(8,128)(2,1)S(1)} %collective-permute-done.5.refs_1_, s16[1040,128]{1,0:T(8,128)(2,1)S(1)} %collective-permute-done.10.refs_2_, ...), custom_call_target="tpu_custom_call" | custom-call | flops 3000000000 | bytes 9000000 | tf_op jit(solution)/shard_map/pallas_call | solution.py:179
  60.9 2.0 %collective-permute-done.14.refs_1_ = s16[1040,256]{1,0:T(8,128)(2,1)S(1)} collective-permute-done((s16[1040,256]{1,0:T(8,128)(2,1)S(1)}, s16[1040,256]{1,0:T(8,128)(2,1)S(1)}, u32[]{:S(2)}, u32[]{:S(2)}) %collective-permute-start.14) | collective-permute-done | bytes 532512 | tf_op jit(solution)/shard_map/ppermute | solution.py:229
  62.9 1.5 %shard_map.54 = bf16[1024,256]{1,0:T(8,128)(2,1)} custom-call(s32[12]{0:T(128)S(1)} %pad_add_fusion.facts, f32[1024,256]{1,0:T(8,128)S(1)} %shard_map.53.refs_0_, s16[1040,256]{1,0:T(8,128)(2,1)S(1)} %collective-permute-done.14.refs_1_), custom_call_target="tpu_custom_call" | custom-call | flops 3000000000 | bytes 9000000 | tf_op jit(solution)/shard_map/pallas_call | solution.py:179
  (2 shorter events, 0.0 us)
Async XLA Ops:
  0.0 13.9 %collective-permute-start.1 = (bf16[2048,128]{1,0:T(8,128)(2,1)}, bf16[2048,128]{1,0:T(8,128)(2,1)S(1)}, u32[]{:S(2)}, u32[]{:S(2)}) collective-permute-start(bf16[2048,128]{1,0:T(8,128)(2,1)} %refs_0_.9), channel_id=1, source_target_pairs={{0,16},{4,20},{8,24},{12,28},{16,0},{20,4},{24,8},{28,12},{1,17},{... | collective-permute-start | bytes 1572872 | tf_op jit(solution)/shard_map/ppermute | solution.py:226
  1.5 13.6 %collective-permute-start = (bf16[2048,128]{1,0:T(8,128)(2,1)}, bf16[2048,128]{1,0:T(8,128)(2,1)S(1)}, u32[]{:S(2)}, u32[]{:S(2)}) collective-permute-start(bf16[2048,128]{1,0:T(8,128)(2,1)} %refs_0_.9), channel_id=1, source_target_pairs={{0,8},{4,12},{8,0},{12,4},{16,24},{20,28},{24,16},{28,20},{1,9},{5... | collective-permute-start | bytes 1572872 | tf_op jit(solution)/shard_map/ppermute | solution.py:226
  2.1 2.5 %copy-start.1 = (bf16[1024,2048]{1,0:T(8,128)(2,1)S(1)}, bf16[1024,2048]{1,0:T(8,128)(2,1)}, u32[]{:S(2)}) copy-start(bf16[1024,2048]{1,0:T(8,128)(2,1)} %param.4) | copy-start | bytes 12582916
  3.0 13.8 %collective-permute-start.2 = (bf16[2048,128]{1,0:T(8,128)(2,1)}, bf16[2048,128]{1,0:T(8,128)(2,1)S(1)}, u32[]{:S(2)}, u32[]{:S(2)}) collective-permute-start(bf16[2048,128]{1,0:T(8,128)(2,1)} %refs_0_.9), channel_id=1, source_target_pairs={{0,4},{4,0},{8,12},{12,8},{16,20},{20,16},{24,28},{28,24},{1,5},{5... | collective-permute-start | bytes 1572872 | tf_op jit(solution)/shard_map/ppermute | solution.py:226
  4.5 13.2 %copy-start = (bf16[2048,128]{1,0:T(8,128)(2,1)S(1)}, bf16[2048,128]{1,0:T(8,128)(2,1)}, u32[]{:S(2)}) copy-start(bf16[2048,128]{1,0:T(8,128)(2,1)} %refs_0_.9) | copy-start | bytes 1572868
  15.1 1.9 %collective-permute-start.3 = (bf16[2048,128]{1,0:T(8,128)(2,1)S(1)}, bf16[2048,128]{1,0:T(8,128)(2,1)S(1)}, u32[]{:S(2)}, u32[]{:S(2)}) collective-permute-start(bf16[2048,128]{1,0:T(8,128)(2,1)S(1)} %collective-permute-done.refs_1_), channel_id=1, source_target_pairs={{0,4},{4,0},{8,12},{12,8},{16,20},{20,16},{24,28},{28,24},{1,5},{5... | collective-permute-start | bytes 1572872 | tf_op jit(solution)/shard_map/ppermute | solution.py:226
  15.1 2.7 %collective-permute-start.4 = (bf16[2048,128]{1,0:T(8,128)(2,1)S(1)}, bf16[2048,128]{1,0:T(8,128)(2,1)S(1)}, u32[]{:S(2)}, u32[]{:S(2)}) collective-permute-start(bf16[2048,128]{1,0:T(8,128)(2,1)S(1)} %collective-permute-done.1.refs_2_), channel_id=1, source_target_pairs={{0,4},{4,0},{8,12},{12,8},{16,20},{20,16},{24,28},{28,24},{1,5},{5... | collective-permute-start | bytes 1572872 | tf_op jit(solution)/shard_map/ppermute | solution.py:226
  15.7 8.5 %collective-permute-start.6 = (bf16[1024,128]{1,0:T(8,128)(2,1)S(1)}, bf16[1024,128]{1,0:T(8,128)(2,1)S(1)}, u32[]{:S(2)}, u32[]{:S(2)}) collective-permute-start(bf16[1024,128]{1,0:T(8,128)(2,1)S(1)} %slice.6), channel_id=1, source_target_pairs={{0,8},{4,12},{8,0},{12,4},{16,24},{20,28},{24,16},{28,20},{1,9},{5... | collective-permute-start | bytes 786440 | tf_op jit(solution)/shard_map/ppermute | solution.py:226
  16.3 7.9 %collective-permute-start.7 = (bf16[1024,128]{1,0:T(8,128)(2,1)S(1)}, bf16[1024,128]{1,0:T(8,128)(2,1)S(1)}, u32[]{:S(2)}, u32[]{:S(2)}) collective-permute-start(bf16[1024,128]{1,0:T(8,128)(2,1)S(1)} %slice.7), channel_id=1, source_target_pairs={{0,16},{4,20},{8,24},{12,28},{16,0},{20,4},{24,8},{28,12},{1,17},{... | collective-permute-start | bytes 786440 | tf_op jit(solution)/shard_map/ppermute | solution.py:226
  20.8 9.3 %collective-permute-start.5 = (s16[1040,128]{1,0:T(8,128)(2,1)S(1)}, s16[1040,128]{1,0:T(8,128)(2,1)S(1)}, u32[]{:S(2)}, u32[]{:S(2)}) collective-permute-start(s16[1040,128]{1,0:T(8,128)(2,1)S(1)} %get-tuple-element.25), channel_id=1, source_target_pairs={{0,1},{1,0},{2,3},{3,2},{4,5},{5,4},{6,7},{7,6},{8,9},{9,8},{10,11... | collective-permute-start | bytes 798728 | tf_op jit(solution)/shard_map/ppermute | solution.py:229
  24.2 5.9 %collective-permute-start.8 = (bf16[1024,128]{1,0:T(8,128)(2,1)S(1)}, bf16[1024,128]{1,0:T(8,128)(2,1)S(1)}, u32[]{:S(2)}, u32[]{:S(2)}) collective-permute-start(bf16[1024,128]{1,0:T(8,128)(2,1)S(1)} %collective-permute-done.6.refs_3_), channel_id=1, source_target_pairs={{0,4},{4,0},{8,12},{12,8},{16,20},{20,16},{24,28},{28,24},{1,5},{5... | collective-permute-start | bytes 786440 | tf_op jit(solution)/shard_map/ppermute | solution.py:226
  24.2 5.9 %collective-permute-start.9 = (bf16[1024,128]{1,0:T(8,128)(2,1)S(1)}, bf16[1024,128]{1,0:T(8,128)(2,1)S(1)}, u32[]{:S(2)}, u32[]{:S(2)}) collective-permute-start(bf16[1024,128]{1,0:T(8,128)(2,1)S(1)} %collective-permute-done.7.refs_4_), channel_id=1, source_target_pairs={{0,4},{4,0},{8,12},{12,8},{16,20},{20,16},{24,28},{28,24},{1,5},{5... | collective-permute-start | bytes 786440 | tf_op jit(solution)/shard_map/ppermute | solution.py:226
  24.7 10.3 %collective-permute-start.10 = (s16[1040,128]{1,0:T(8,128)(2,1)S(1)}, s16[1040,128]{1,0:T(8,128)(2,1)S(1)}, u32[]{:S(2)}, u32[]{:S(2)}) collective-permute-start(s16[1040,128]{1,0:T(8,128)(2,1)S(1)} %get-tuple-element.23), channel_id=1, source_target_pairs={{0,1},{1,0},{2,3},{3,2},{4,5},{5,4},{6,7},{7,6},{8,9},{9,8},{10,11... | collective-permute-start | bytes 798728 | tf_op jit(solution)/shard_map/ppermute | solution.py:229
  32.9 14.4 %collective-permute-start.11 = (s16[1040,256]{1,0:T(8,128)(2,1)S(1)}, s16[1040,256]{1,0:T(8,128)(2,1)S(1)}, u32[]{:S(2)}, u32[]{:S(2)}) collective-permute-start(s16[1040,256]{1,0:T(8,128)(2,1)S(1)} %shard_map.48), channel_id=1, source_target_pairs={{0,1},{3,2},{2,3},{4,5},{7,6},{6,7},{8,9},{11,10},{12,13},{15,14},... | collective-permute-start | bytes 1597448 | tf_op jit(solution)/shard_map/ppermute | solution.py:229
  36.0 19.4 %collective-permute-start.12 = (s16[1040,256]{1,0:T(8,128)(2,1)S(1)}, s16[1040,256]{1,0:T(8,128)(2,1)S(1)}, u32[]{:S(2)}, u32[]{:S(2)}) collective-permute-start(s16[1040,256]{1,0:T(8,128)(2,1)S(1)} %shard_map.49), channel_id=1, source_target_pairs={{1,2},{2,0},{5,6},{6,4},{9,11},{10,8},{13,15},{14,12},{17,19},{18,... | collective-permute-start | bytes 1597448 | tf_op jit(solution)/shard_map/ppermute | solution.py:229
  45.1 14.6 %collective-permute-start.13 = (s16[1040,256]{1,0:T(8,128)(2,1)S(1)}, s16[1040,256]{1,0:T(8,128)(2,1)S(1)}, u32[]{:S(2)}, u32[]{:S(2)}) collective-permute-start(s16[1040,256]{1,0:T(8,128)(2,1)S(1)} %get-tuple-element.31), channel_id=1, source_target_pairs={{0,1},{3,2},{4,5},{7,6},{8,9},{11,10},{12,13},{15,14},{16,17},{19,... | collective-permute-start | bytes 1597448 | tf_op jit(solution)/shard_map/ppermute | solution.py:229
  48.3 14.5 %collective-permute-start.14 = (s16[1040,256]{1,0:T(8,128)(2,1)S(1)}, s16[1040,256]{1,0:T(8,128)(2,1)S(1)}, u32[]{:S(2)}, u32[]{:S(2)}) collective-permute-start(s16[1040,256]{1,0:T(8,128)(2,1)S(1)} %shard_map.51), channel_id=1, source_target_pairs={{1,3},{2,1},{5,7},{6,5},{9,10},{10,9},{13,14},{14,13},{17,18},{18,... | collective-permute-start | bytes 1597448 | tf_op jit(solution)/shard_map/ppermute | solution.py:229
